TPU v7x, 32 devices: a whole 2x2x4 slice. The times are simulated.
32 devices in a mesh: grp: 2 (over y), gx: 4 (over z), gy: 2 (over x), gz: 2 (over core).
Axes of the slice: x: 2, y: 2, z: 4, core: 2. Of those that a mesh axis runs over, the one named last changes fastest.
Arguments:
- parent_old: float32 [8, 384, 512], P(None, ('grp', 'gx', 'gz'), 'gy'), parts along dimension 1, may hold values from -6 to 6
- parent_source: float32 [8, 384, 512], P(None, ('grp', 'gx', 'gz'), 'gy'), parts along dimension 1, may hold values from -4 to 4
- parent_coefs: float32 [2, 8], replicated, may hold values from 0.02 to 0.1
- nest_old: float32 [8, 1152, 768], P(None, ('grp', 'gx', 'gz'), 'gy'), parts along dimension 1, may hold values from -6 to 6
- nest_source: float32 [8, 1152, 768], P(None, ('grp', 'gx', 'gz'), 'gy'), parts along dimension 1, may hold values from -2 to 2
- nest_coefs: float32 [2, 8], replicated, may hold values from 0.02 to 0.1
- offset_x: int32 [2], P('grp'), parts along dimension 0, may hold values from 1 to 23
- offset_y: int32 [2], P('grp'), parts along dimension 0, may hold values from 1 to 255
Outputs:
- parent_new: float32 [8, 384, 512], P(None, ('grp', 'gx', 'gz'), 'gy'), parts along dimension 1
- nest_new: float32 [8, 1152, 768], P(None, ('grp', 'gx', 'gz'), 'gy'), parts along dimension 1
There are 2 independent parts, one for each index of `grp`. A program takes and returns all parts, laid end to end along the dimension named above; an argument that names none is the same for every part. Nothing has to cross between parts.
All inputs are finite; a program needn't handle non-finite values.
Results may differ from a plain program's by a relative error of at most 0.00002.
Values sent between devices are 32-bit elements; how exact they have to be, the bound alone decides.
No kernel may reach another device: no remote copies, remote signals or barrier semaphores. Data moves between devices by JAX's collectives and lax.ppermute only.
A program may use at most 128 MiB of HBM per device.

v0:
```python
import jax
import jax.numpy as jnp
from jax import lax
from jax.sharding import PartitionSpec as P

RATIO = 3
SUBSTEPS = 3
RIM = 6


def with_halo(shard, sides, width):
    for axis, dim in sides:
        devices, length = (lax.axis_size(axis), shard.shape[dim])
        up = [(i, (i + 1) % devices) for i in range(devices)]
        down = [(j, i) for i, j in up]
        last = lax.slice_in_dim(shard, length - width, length, axis=dim)
        leading = lax.slice_in_dim(shard, 0, width, axis=dim)
        before = lax.ppermute(last, axis, up)
        after = lax.ppermute(leading, axis, down)
        shard = jnp.concatenate([before, shard, after], axis=dim)
    return shard


def shifted(value, axis, steps):
    count = lax.axis_size(axis)
    pairs = [(source, (source + steps) % count) for source in range(count)]
    return lax.ppermute(value, axis, pairs)


def diffuse(padded, coefs_h, coefs_v, source):
    center = padded[1:-1, 1:-1, 1:-1]
    lateral = (
        padded[1:-1, 2:, 1:-1]
        + padded[1:-1, :-2, 1:-1]
        + padded[1:-1, 1:-1, 2:]
        + padded[1:-1, 1:-1, :-2]
        - 4.0 * center
    )
    vertical = padded[2:, 1:-1, 1:-1] + padded[:-2, 1:-1, 1:-1] - 2.0 * center
    return center + coefs_h[:, None, None] * lateral + coefs_v[:, None, None] * vertical + source


def inside_mask(first_pos, span_len, total_len):
    positions = first_pos + jnp.arange(span_len, dtype=jnp.int32)
    return ((positions >= 0) & (positions < total_len)).astype(jnp.float32)


def level_pad(grid_field):
    return jnp.pad(grid_field, ((1, 1), (0, 0), (0, 0)))


def shards(
    parent_old, parent_source, parent_coefs, nest_old, nest_source, nest_coefs, offset_x, offset_y
):
    parent_rows = parent_old.shape[1]
    parent_cols = parent_old.shape[2]
    nest_cols = nest_old.shape[2]
    foot_cols = nest_cols // RATIO
    band_width = foot_cols * lax.axis_size("gy")
    total_cols = nest_cols * lax.axis_size("gy")
    column_index = lax.axis_index("gy")
    shift_x = offset_x[0]
    shift_y = offset_y[0]

    def col_mask(grid_field, extent, col_first, col_total):
        ymask = inside_mask(col_first - extent, grid_field.shape[2], col_total)
        return grid_field * ymask[None, None, :]

    padded = with_halo(parent_old, ((("gx", "gz"), 1), ("gy", 2)), 1)
    padded = col_mask(padded, 1, column_index * parent_cols, parent_cols * lax.axis_size("gy"))
    parent_step = diffuse(level_pad(padded), parent_coefs[0], parent_coefs[1], parent_source)
    wanted = shift_y + jnp.stack(
        [jnp.int32(0), jnp.int32(1), jnp.int32(band_width - 2), jnp.int32(band_width - 1)]
    )
    local_cols = wanted - column_index * parent_cols
    is_valid = ((local_cols >= 0) & (local_cols < parent_cols)).astype(jnp.float32)
    both_times = jnp.stack([parent_old, parent_step])
    picked = jnp.take(both_times, jnp.clip(local_cols, 0, parent_cols - 1), axis=3) * is_valid
    edge_sum = lax.psum(picked, "gy")
    following = shifted(edge_sum, ("gx", "gz"), -1)
    joined = jnp.concatenate([edge_sum, following], axis=2)
    margin = 0
    edge_window = lax.dynamic_slice_in_dim(
        joined, shift_x - margin, parent_rows + 2 * margin, axis=2
    )
    old_edge = edge_window[0]
    new_edge = edge_window[1]
    nest_first = column_index * nest_cols
    nest_now = nest_old
    for substep in range(1, SUBSTEPS + 1):
        padded = with_halo(nest_now, ((("gx", "gz"), 1), ("gy", 2)), 1)
        padded = col_mask(padded, 1, nest_first, total_cols)
        nest_now = diffuse(level_pad(padded), nest_coefs[0], nest_coefs[1], nest_source)
        force_grid_field = nest_now
        weight = substep / SUBSTEPS
        edge_now = old_edge + weight * (new_edge - old_edge)
        fine_edges = jnp.repeat(edge_now, RATIO, axis=1)
        rim_width = RIM + 0
        force_col_first = column_index * nest_cols - 0
        south_pos = force_col_first + jnp.arange(rim_width, dtype=jnp.int32)
        south_on = (south_pos >= 0) & (south_pos < RIM)
        south_vals = jnp.take(fine_edges, jnp.clip(south_pos // RATIO, 0, 1), axis=2)
        force_grid_field = force_grid_field.at[:, :, :rim_width].set(
            jnp.where(south_on, south_vals, force_grid_field[:, :, :rim_width])
        )
        north_pos = (
            force_col_first
            + force_grid_field.shape[2]
            - rim_width
            + jnp.arange(rim_width, dtype=jnp.int32)
        )
        north_on = (north_pos >= total_cols - RIM) & (north_pos < total_cols)
        north_ids = jnp.clip(2 + (north_pos - (total_cols - RIM)) // RATIO, 2, 3)
        north_vals = jnp.take(fine_edges, north_ids, axis=2)
        tail_start = force_grid_field.shape[2] - rim_width
        force_grid_field = force_grid_field.at[:, :, tail_start:].set(
            jnp.where(north_on, north_vals, force_grid_field[:, :, tail_start:])
        )
        nest_now = force_grid_field
    level_count = nest_now.shape[0]
    coarse = nest_now.reshape(level_count, parent_rows, RATIO, foot_cols, RATIO).mean(axis=(2, 4))
    spread_raw = lax.all_gather(coarse, "gy", axis=2, tiled=True)
    previous = shifted(spread_raw, ("gx", "gz"), 1)
    spread = lax.dynamic_slice_in_dim(
        jnp.concatenate([previous, spread_raw], axis=1), parent_rows - shift_x, parent_rows, axis=1
    )
    offsets = column_index * parent_cols + jnp.arange(parent_cols, dtype=jnp.int32) - shift_y
    keep_cols = (offsets >= 2) & (offsets < band_width - 2)
    values = jnp.take(spread, jnp.clip(offsets, 0, band_width - 1), axis=2)
    parent_new = jnp.where(keep_cols, values, parent_step)
    return (parent_new, nest_now)


def solution(mesh):
    return jax.shard_map(
        shards,
        mesh=mesh,
        in_specs=(
            P(None, ("grp", "gx", "gz"), "gy"),
            P(None, ("grp", "gx", "gz"), "gy"),
            P(),
            P(None, ("grp", "gx", "gz"), "gy"),
            P(None, ("grp", "gx", "gz"), "gy"),
            P(),
            P("grp"),
            P("grp"),
        ),
        out_specs=(P(None, ("grp", "gx", "gz"), "gy"), P(None, ("grp", "gx", "gz"), "gy")),
        check_vma=False,
    )
```

profile of v0, /device:TPU:0, one launch (start us, length us, event | category | flops | bytes accessed | tf_op | source)
XLA Modules:
  0.0 170.9 jit_solution(1578808640325288007)
XLA Ops:
  2.1 4.1 %collective-permute-start.5 = (f32[8,1,256]{2,0,1:T(8,128)S(1)}, f32[8,1,256]{2,0,1:T(8,128)S(1)}, u32[]{:S(2)}, u32[]{:S(2)}) collective-permute-start(f32[8,1,256]{2,0,1:T(8,128)S(1)} %copy.152), channel_id=1, source_target_pairs={{1,0},{4,1},{5,4},{8,5},{9,8},{12,9},{13,12},{0,13},{3,2},{6,3},{7... | collective-permute-start | bytes 24584 | tf_op jit(solution)/shard_map/ppermute | solution.py:19
  8.7 1.3 slice_bitcast_fusion.3
  11.4 1.2 compare_and_fusion.3
  13.2 2.2 %copy.115 = f32[8,24,256]{1,0,2:T(8,128)} copy(f32[8,24,256]{2,1,0:T(8,128)} %param.22) | data formatting | bytes 393216 | tf_op args[0]
  15.6 1.8 %collective-permute-start.6 = (f32[8,26,1]{2,0,1:T(8,128)S(1)}, f32[8,26,1]{2,0,1:T(8,128)S(1)}, u32[]{:S(2)}, u32[]{:S(2)}) collective-permute-start(f32[8,26,1]{2,0,1:T(8,128)S(1)} %get-tuple-element.95), channel_id=1, source_target_pairs={{0,2},{2,0},{1,3},{3,1},{4,6},{6,4},{5,7},{7,5},{8,10},{10,8},{9,1... | collective-permute-start | bytes 2504 | tf_op jit(solution)/shard_map/ppermute | solution.py:18
  19.0 1.3 copy.120
  20.3 1.8 %copy.114 = f32[8,72,384]{1,0,2:T(8,128)S(1)} copy(f32[8,72,384]{2,1,0:T(8,128)} %param.26) | data formatting | bytes 1769472 | tf_op args[4]
  23.0 1.2 pad_maximum_fusion.1
  24.2 1.5 copy.119
  25.8 1.6 broadcast_multiply_fusion
  27.4 1.7 fusion.28
  29.2 1.0 copy-done
  30.1 1.5 pad_maximum_fusion
  31.7 2.1 %gather_fusion = f32[4,2,8,24]{3,2,1,0:T(8,128)S(1)} fusion(f32[2,8,24,256]{2,1,3,0:T(8,128)} %pad_maximum_fusion, s32[1024]{0:T(1024)S(1)} %pad_clamp_fusion.3), kind=kCustom, calls=%fused_computation.6 | custom fusion | bytes 12304 | tf_op jit(solution)/shard_map/jit(_take)/gather | solution.py:78
  33.9 1.7 copy.111
  35.6 1.7 copy.113
  38.1 1.7 %collective-permute-start.2 = (f32[8,74,1]{1,0,2:T(8,128)S(1)}, f32[8,74,1]{1,0,2:T(8,128)S(1)}, u32[]{:S(2)}, u32[]{:S(2)}) collective-permute-start(f32[8,74,1]{1,0,2:T(8,128)S(1)} %get-tuple-element.87), channel_id=1, source_target_pairs={{0,2},{2,0},{1,3},{3,1},{4,6},{6,4},{5,7},{7,5},{8,10},{10,8},{9,1... | collective-permute-start | bytes 7112 | tf_op jit(solution)/shard_map/ppermute | solution.py:18
  40.1 8.6 %psum.7 = f32[2,8,24,4]{2,1,0,3:T(8,128)S(1)} all-reduce(f32[2,8,24,4]{2,1,0,3:T(8,128)S(1)} %multiply_bitcast_fusion), channel_id=1, replica_groups=mesh['grp'=2,'gx'=4,'gy'=2,'gz'=2] {'gy'}, use_global_device_ids=true, to_apply=%region_0.1 | all-reduce | flops 1536 | bytes 12288 | tf_op jit(solution)/shard_map/psum | solution.py:79
  48.8 2.8 %maximum_multiply_fusion = f32[8,74,386]{1,0,2:T(8,128)S(1)} fusion(f32[8,74,1]{1,0,2:T(8,128)S(1)} %collective-permute-done.3, f32[8,1,384]{1,0,2:T(8,128)} %copy.113, f32[8,72,384]{1,0,2:T(8,128)S(1)} %copy.112, f32[8,1,384]{1,0,2:T(8,128)} %copy.111, f32[8,74,1]{1,0,2:T(8,128)S(1)} %collective-permute-done.2, f32[386]{0:T(512)S(1)} %fusion.46), kind=kLoop, calls=%fused_computation.17 | loop fusion | flops 1142560 | bytes 1829640 | tf_op jit(solution)/shard_map/mul | solution.py:67
  51.6 2.5 %fusion.4 = f32[8,72,384]{1,0,2:T(8,128)S(1)} fusion(f32[8,72,384]{1,0,2:T(8,128)S(1)} %copy.114, f32[8,74,386]{1,0,2:T(8,128)S(1)} %maximum_multiply_fusion, f32[8]{0:T(128)S(1)} %get-tuple-element.103, f32[8]{0:T(128)S(1)} %get-tuple-element.102), kind=kLoop, calls=%fused_computation.24 | loop fusion | flops 2875392 | bytes 11904000 | tf_op jit(solution)/shard_map/add | solution.py:40
  55.8 2.1 %fusion.51 = (f32[8,1,384]{1,0,2:T(8,128)}, f32[8,1,384]{1,0,2:T(8,128)}) fusion(f32[8,72,384]{1,0,2:T(8,128)S(1)} %fusion.37), kind=kLoop, calls=%fused_computation.143 | loop fusion | bytes 49152 | tf_op jit(solution)/shard_map/slice | solution.py:16
  57.9 1.9 %copy.125 = f32[8,1,384]{2,0,1:T(8,128)S(1)} copy(f32[8,1,384]{1,0,2:T(8,128)} %get-tuple-element.91) | data formatting | bytes 24576 | tf_op jit(solution)/shard_map/slice | solution.py:16
  60.3 1.9 %copy.126 = f32[8,1,384]{2,0,1:T(8,128)S(1)} copy(f32[8,1,384]{1,0,2:T(8,128)} %get-tuple-element.92) | data formatting | bytes 24576 | tf_op jit(solution)/shard_map/slice | solution.py:17
  62.2 3.3 %collective-permute-start.10 = (f32[8,1,384]{2,0,1:T(8,128)S(1)}, f32[8,1,384]{2,0,1:T(8,128)S(1)}, u32[]{:S(2)}, u32[]{:S(2)}) collective-permute-start(f32[8,1,384]{2,0,1:T(8,128)S(1)} %copy.126), channel_id=1, source_target_pairs={{1,0},{4,1},{5,4},{8,5},{9,8},{12,9},{13,12},{0,13},{3,2},{6,3},{7... | collective-permute-start | bytes 36872 | tf_op jit(solution)/shard_map/ppermute | solution.py:19
  65.5 1.7 copy.127
  67.2 1.7 copy.128
  70.1 1.6 collective-permute-start.12
  73.7 2.8 %maximum_multiply_fusion.1 = f32[8,74,386]{1,0,2:T(8,128)S(1)} fusion(f32[8,74,1]{1,0,2:T(8,128)S(1)} %collective-permute-done.12, f32[8,1,384]{1,0,2:T(8,128)} %copy.128, f32[8,72,384]{1,0,2:T(8,128)S(1)} %fusion.37, f32[8,1,384]{1,0,2:T(8,128)} %copy.127, f32[8,74,1]{1,0,2:T(8,128)S(1)} %collective-permute-done.11, f32[386]{0:T(512)S(1)} %fusion.46), kind=kLoop, calls=%fused_computation.18 | loop fusion | flops 1142560 | bytes 1829640 | tf_op jit(solution)/shard_map/mul | solution.py:67
  76.6 2.5 %fusion.9 = f32[8,72,384]{1,0,2:T(8,128)S(1)} fusion(f32[8,72,384]{1,0,2:T(8,128)S(1)} %copy.114, f32[8,74,386]{1,0,2:T(8,128)S(1)} %maximum_multiply_fusion.1, f32[8]{0:T(128)S(1)} %get-tuple-element.103, f32[8]{0:T(128)S(1)} %get-tuple-element.102), kind=kLoop, calls=%fused_computation.29 | loop fusion | flops 2875392 | bytes 11904000 | tf_op jit(solution)/shard_map/add | solution.py:40
  79.2 2.1 %fusion.50 = (f32[8,1,384]{1,0,2:T(8,128)}, f32[8,1,384]{1,0,2:T(8,128)}) fusion(f32[8,72,384]{1,0,2:T(8,128)S(1)} %fusion.35), kind=kLoop, calls=%fused_computation.142 | loop fusion | bytes 49152 | tf_op jit(solution)/shard_map/slice | solution.py:16
  81.4 1.9 %copy.133 = f32[8,1,384]{2,0,1:T(8,128)S(1)} copy(f32[8,1,384]{1,0,2:T(8,128)} %get-tuple-element.89) | data formatting | bytes 24576 | tf_op jit(solution)/shard_map/slice | solution.py:16
  83.3 1.9 %copy.134 = f32[8,1,384]{2,0,1:T(8,128)S(1)} copy(f32[8,1,384]{1,0,2:T(8,128)} %get-tuple-element.90) | data formatting | bytes 24576 | tf_op jit(solution)/shard_map/slice | solution.py:17
  85.2 3.6 %collective-permute-start.14 = (f32[8,1,384]{2,0,1:T(8,128)S(1)}, f32[8,1,384]{2,0,1:T(8,128)S(1)}, u32[]{:S(2)}, u32[]{:S(2)}) collective-permute-start(f32[8,1,384]{2,0,1:T(8,128)S(1)} %copy.134), channel_id=1, source_target_pairs={{1,0},{4,1},{5,4},{8,5},{9,8},{12,9},{13,12},{0,13},{3,2},{6,3},{7... | collective-permute-start | bytes 36872 | tf_op jit(solution)/shard_map/ppermute | solution.py:19
  88.7 1.7 copy.135
  90.4 1.7 copy.136
  92.9 1.6 collective-permute-start.15
  96.5 1.6 collective-permute-done.16
  98.1 2.8 %maximum_multiply_fusion.2 = f32[8,74,386]{1,0,2:T(8,128)S(1)} fusion(f32[8,74,1]{1,0,2:T(8,128)S(1)} %collective-permute-done.16, f32[8,1,384]{1,0,2:T(8,128)} %copy.136, f32[8,72,384]{1,0,2:T(8,128)S(1)} %fusion.35, f32[8,1,384]{1,0,2:T(8,128)} %copy.135, f32[8,74,1]{1,0,2:T(8,128)S(1)} %collective-permute-done.15, f32[386]{0:T(512)S(1)} %fusion.46), kind=kLoop, calls=%fused_computation.19 | loop fusion | flops 1142560 | bytes 1829640 | tf_op jit(solution)/shard_map/mul | solution.py:67
  100.9 2.5 %fusion.14 = f32[8,72,384]{1,0,2:T(8,128)S(1)} fusion(f32[8,72,384]{1,0,2:T(8,128)S(1)} %copy.114, f32[8,74,386]{1,0,2:T(8,128)S(1)} %maximum_multiply_fusion.2, f32[8]{0:T(128)S(1)} %get-tuple-element.103, f32[8]{0:T(128)S(1)} %get-tuple-element.102), kind=kLoop, calls=%fused_computation.34 | loop fusion | flops 2875392 | bytes 11904000 | tf_op jit(solution)/shard_map/add | solution.py:40
  103.6 11.7 %copy.141 = f32[8,72,384]{0,2,1:T(8,128)} copy(f32[8,72,384]{1,0,2:T(8,128)S(1)} %fusion.33) | data formatting | bytes 1769472 | tf_op jit(solution)/shard_map/scatter | solution.py:116
  115.3 21.8 %reshape.271 = f32[8,24,3,128,3]{0,4,3,2,1:T(4,128)} reshape(f32[8,72,384]{0,2,1:T(8,128)} %copy.141) | data formatting | bytes 1769472 | tf_op jit(solution)/shard_map/reshape | solution.py:121
  137.1 14.8 %reduce_sum.9 = f32[8,24,128]{0,2,1:T(8,128)S(1)} reduce(f32[8,24,3,128,3]{0,4,3,2,1:T(4,128)} %reshape.271, f32[]{:T(128)} %constant.250.clone.1), dimensions={2,4}, to_apply=%region_1.3 | reduce | flops 196608 | bytes 983044 | tf_op jit(solution)/shard_map/reduce_sum | solution.py:121
  152.4 5.3 %all_gather.3 = f32[8,24,256]{2,1,0:T(8,128)S(1)} all-gather(f32[8,24,128]{2,1,0:T(8,128)S(1)} %broadcast_multiply_fusion.1), channel_id=1, replica_groups=mesh['grp'=2,'gx'=4,'gy'=2,'gz'=2] {'gy'}, dimensions={2}, use_global_device_ids=true | all-gather | bytes 294912 | tf_op jit(solution)/shard_map/all_gather | solution.py:122
  157.7 1.4 copy.145
  159.2 5.4 %collective-permute-done.17 = f32[8,24,256]{2,1,0:T(8,128)S(1)} collective-permute-done((f32[8,24,256]{2,1,0:T(8,128)S(1)}, f32[8,24,256]{2,1,0:T(8,128)S(1)}, u32[]{:S(2)}, u32[]{:S(2)}) %collective-permute-start.17) | collective-permute-done | bytes 196640 | tf_op jit(solution)/shard_map/ppermute | solution.py:27
  165.1 2.0 %gather_fusion.1 = f32[256,8,24]{2,1,0:T(8,128)} fusion(f32[8,24,256]{1,0,2:T(8,128)S(1)} %copy.149, s32[1024]{0:T(1024)S(1)} %pad_clamp_fusion), kind=kCustom, calls=%fused_computation.7 | custom fusion | bytes 394240 | tf_op jit(solution)/shard_map/jit(_take)/gather | solution.py:129
  167.1 2.8 %bitcast_select_fusion = f32[8,24,256]{1,0,2:T(8,128)S(1)} fusion(f32[8,24,256]{1,0,2:T(8,128)S(1)} %copy-done.1, f32[256,8,24]{2,1,0:T(8,128)} %gather_fusion.1, pred[256]{0:T(512)(128)(4,1)S(1)} %get-tuple-element.112, pred[256]{0:T(512)(128)(4,1)S(1)} %get-tuple-element.113), kind=kLoop, calls=%fused_computation.64 | loop fusion | flops 98304 | bytes 590336 | tf_op jit(solution)/shard_map/jit(_where)/select_n | solution.py:130
  169.9 1.0 copy.144
  (109 shorter events, 17.8 us)
Async XLA Ops:
  0.6 14.8 %copy-start.6 = (f32[8,24,256]{2,1,0:T(8,128)S(1)}, f32[8,24,256]{2,1,0:T(8,128)}, u32[]{:S(2)}) copy-start(f32[8,24,256]{2,1,0:T(8,128)} %param.22) | copy-start | bytes 589828
  0.6 17.1 %copy-start.4 = (f32[8,72,384]{2,1,0:T(8,128)S(1)}, f32[8,72,384]{2,1,0:T(8,128)}, u32[]{:S(2)}) copy-start(f32[8,72,384]{2,1,0:T(8,128)} %param.25) | copy-start | bytes 2654212
  1.6 13.8 %collective-permute-start.4 = (f32[8,1,256]{2,0,1:T(8,128)S(1)}, f32[8,1,256]{2,0,1:T(8,128)S(1)}, u32[]{:S(2)}, u32[]{:S(2)}) collective-permute-start(f32[8,1,256]{2,0,1:T(8,128)S(1)} %copy.151), channel_id=1, source_target_pairs={{0,1},{1,4},{4,5},{5,8},{8,9},{9,12},{12,13},{13,0},{2,3},{3,6},{6... | collective-permute-start | bytes 24584 | tf_op jit(solution)/shard_map/ppermute | solution.py:18
  2.1 13.4 %collective-permute-start.5 = (f32[8,1,256]{2,0,1:T(8,128)S(1)}, f32[8,1,256]{2,0,1:T(8,128)S(1)}, u32[]{:S(2)}, u32[]{:S(2)}) collective-permute-start(f32[8,1,256]{2,0,1:T(8,128)S(1)} %copy.152), channel_id=1, source_target_pairs={{1,0},{4,1},{5,4},{8,5},{9,8},{12,9},{13,12},{0,13},{3,2},{6,3},{7... | collective-permute-start | bytes 24584 | tf_op jit(solution)/shard_map/ppermute | solution.py:19
  7.2 28.4 %collective-permute-start.1 = (f32[8,1,384]{2,0,1:T(8,128)S(1)}, f32[8,1,384]{2,0,1:T(8,128)S(1)}, u32[]{:S(2)}, u32[]{:S(2)}) collective-permute-start(f32[8,1,384]{2,0,1:T(8,128)S(1)} %copy.147), channel_id=1, source_target_pairs={{1,0},{4,1},{5,4},{8,5},{9,8},{12,9},{13,12},{0,13},{3,2},{6,3},{7... | collective-permute-start | bytes 36872 | tf_op jit(solution)/shard_map/ppermute | solution.py:19
  8.0 25.9 %collective-permute-start = (f32[8,1,384]{2,0,1:T(8,128)S(1)}, f32[8,1,384]{2,0,1:T(8,128)S(1)}, u32[]{:S(2)}, u32[]{:S(2)}) collective-permute-start(f32[8,1,384]{2,0,1:T(8,128)S(1)} %copy.146), channel_id=1, source_target_pairs={{0,1},{1,4},{4,5},{5,8},{8,9},{9,12},{12,13},{13,0},{2,3},{3,6},{6... | collective-permute-start | bytes 36872 | tf_op jit(solution)/shard_map/ppermute | solution.py:18
  15.4 3.6 %copy-start.7 = (f32[8,24,256]{2,1,0:T(8,128)S(1)}, f32[8,24,256]{2,1,0:T(8,128)}, u32[]{:S(2)}) copy-start(f32[8,24,256]{2,1,0:T(8,128)} %param.23) | copy-start | bytes 589828
  15.5 3.4 %copy-start.5 = (f32[8,26,256]{2,0,1:T(8,128)}, f32[8,26,256]{2,0,1:T(8,128)S(1)}, u32[]{:S(2)}) copy-start(f32[8,26,256]{2,0,1:T(8,128)S(1)} %constant_dynamic-update-slice_fusion) | copy-start | bytes 638980
  15.6 6.5 %collective-permute-start.6 = (f32[8,26,1]{2,0,1:T(8,128)S(1)}, f32[8,26,1]{2,0,1:T(8,128)S(1)}, u32[]{:S(2)}, u32[]{:S(2)}) collective-permute-start(f32[8,26,1]{2,0,1:T(8,128)S(1)} %get-tuple-element.95), channel_id=1, source_target_pairs={{0,2},{2,0},{1,3},{3,1},{4,6},{6,4},{5,7},{7,5},{8,10},{10,8},{9,1... | collective-permute-start | bytes 2504 | tf_op jit(solution)/shard_map/ppermute | solution.py:18
  17.5 5.5 %collective-permute-start.7 = (f32[8,26,1]{2,0,1:T(8,128)S(1)}, f32[8,26,1]{2,0,1:T(8,128)}, u32[]{:S(2)}, u32[]{:S(2)}) collective-permute-start(f32[8,26,1]{2,0,1:T(8,128)S(1)} %get-tuple-element.96), channel_id=1, source_target_pairs={{2,0},{0,2},{3,1},{1,3},{6,4},{4,6},{7,5},{5,7},{10,8},{8,10},{11,... | collective-permute-start | bytes 2504 | tf_op jit(solution)/shard_map/ppermute | solution.py:19
  22.1 0.6 copy-start.8
  25.7 1.7 copy-start.2
  25.7 1.7 copy-start.12
  25.8 1.7 copy-start.13
  27.4 2.7 %copy-start.3 = (f32[8,24,256]{1,0,2:T(8,128)S(1)}, f32[8,24,256]{1,0,2:T(8,128)}, u32[]{:S(2)}) copy-start(f32[8,24,256]{1,0,2:T(8,128)} %copy.115) | copy-start | bytes 589828
  29.1 1.0 copy-start
  30.1 3.7 %copy-start.10 = (pred[4]{0:T(512)(128)(4,1)S(1)}, pred[4]{0:T(512)(128)(4,1)}, u32[]{:S(2)}) copy-start(pred[4]{0:T(512)(128)(4,1)} %get-tuple-element.106) | copy-start | bytes 16
  30.1 3.7 %copy-start.11 = (f32[4]{0:T(128)S(1)}, f32[4]{0:T(128)}, u32[]{:S(2)}) copy-start(f32[4]{0:T(128)} %get-tuple-element.107) | copy-start | bytes 52
  38.1 10.7 %collective-permute-start.2 = (f32[8,74,1]{1,0,2:T(8,128)S(1)}, f32[8,74,1]{1,0,2:T(8,128)S(1)}, u32[]{:S(2)}, u32[]{:S(2)}) collective-permute-start(f32[8,74,1]{1,0,2:T(8,128)S(1)} %get-tuple-element.87), channel_id=1, source_target_pairs={{0,2},{2,0},{1,3},{3,1},{4,6},{6,4},{5,7},{7,5},{8,10},{10,8},{9,1... | collective-permute-start | bytes 7112 | tf_op jit(solution)/shard_map/ppermute | solution.py:18
  39.8 9.0 %collective-permute-start.3 = (f32[8,74,1]{1,0,2:T(8,128)S(1)}, f32[8,74,1]{1,0,2:T(8,128)S(1)}, u32[]{:S(2)}, u32[]{:S(2)}) collective-permute-start(f32[8,74,1]{1,0,2:T(8,128)S(1)} %get-tuple-element.88), channel_id=1, source_target_pairs={{2,0},{0,2},{3,1},{1,3},{6,4},{4,6},{7,5},{5,7},{10,8},{8,10},{11,... | collective-permute-start | bytes 7112 | tf_op jit(solution)/shard_map/ppermute | solution.py:19
  48.7 5.5 %collective-permute-start.8 = (f32[2,8,24,4]{2,1,0,3:T(8,128)S(1)}, f32[2,8,24,4]{2,1,0,3:T(8,128)S(1)}, u32[]{:S(2)}, u32[]{:S(2)}) collective-permute-start(f32[2,8,24,4]{2,1,0,3:T(8,128)S(1)} %psum.7), channel_id=1, source_target_pairs={{0,13},{1,0},{4,1},{5,4},{8,5},{9,8},{12,9},{13,12},{2,15},{3,2},{... | collective-permute-start | bytes 18440 | tf_op jit(solution)/shard_map/ppermute | solution.py:27
  54.1 1.5 copy-start.9
  59.8 5.7 %collective-permute-start.9 = (f32[8,1,384]{2,0,1:T(8,128)S(1)}, f32[8,1,384]{2,0,1:T(8,128)S(1)}, u32[]{:S(2)}, u32[]{:S(2)}) collective-permute-start(f32[8,1,384]{2,0,1:T(8,128)S(1)} %copy.125), channel_id=1, source_target_pairs={{0,1},{1,4},{4,5},{5,8},{8,9},{9,12},{12,13},{13,0},{2,3},{3,6},{6... | collective-permute-start | bytes 36872 | tf_op jit(solution)/shard_map/ppermute | solution.py:18
  62.2 5.0 %collective-permute-start.10 = (f32[8,1,384]{2,0,1:T(8,128)S(1)}, f32[8,1,384]{2,0,1:T(8,128)S(1)}, u32[]{:S(2)}, u32[]{:S(2)}) collective-permute-start(f32[8,1,384]{2,0,1:T(8,128)S(1)} %copy.126), channel_id=1, source_target_pairs={{1,0},{4,1},{5,4},{8,5},{9,8},{12,9},{13,12},{0,13},{3,2},{6,3},{7... | collective-permute-start | bytes 36872 | tf_op jit(solution)/shard_map/ppermute | solution.py:19
  69.7 3.6 %collective-permute-start.11 = (f32[8,74,1]{1,0,2:T(8,128)S(1)}, f32[8,74,1]{1,0,2:T(8,128)S(1)}, u32[]{:S(2)}, u32[]{:S(2)}) collective-permute-start(f32[8,74,1]{1,0,2:T(8,128)S(1)} %get-tuple-element.85), channel_id=1, source_target_pairs={{0,2},{2,0},{1,3},{3,1},{4,6},{6,4},{5,7},{7,5},{8,10},{10,8},{9,1... | collective-permute-start | bytes 7112 | tf_op jit(solution)/shard_map/ppermute | solution.py:18
  70.1 3.6 %collective-permute-start.12 = (f32[8,74,1]{1,0,2:T(8,128)S(1)}, f32[8,74,1]{1,0,2:T(8,128)S(1)}, u32[]{:S(2)}, u32[]{:S(2)}) collective-permute-start(f32[8,74,1]{1,0,2:T(8,128)S(1)} %get-tuple-element.86), channel_id=1, source_target_pairs={{2,0},{0,2},{3,1},{1,3},{6,4},{4,6},{7,5},{5,7},{10,8},{8,10},{11,... | collective-permute-start | bytes 7112 | tf_op jit(solution)/shard_map/ppermute | solution.py:19
  83.3 5.5 %collective-permute-start.13 = (f32[8,1,384]{2,0,1:T(8,128)S(1)}, f32[8,1,384]{2,0,1:T(8,128)S(1)}, u32[]{:S(2)}, u32[]{:S(2)}) collective-permute-start(f32[8,1,384]{2,0,1:T(8,128)S(1)} %copy.133), channel_id=1, source_target_pairs={{0,1},{1,4},{4,5},{5,8},{8,9},{9,12},{12,13},{13,0},{2,3},{3,6},{6... | collective-permute-start | bytes 36872 | tf_op jit(solution)/shard_map/ppermute | solution.py:18
  85.2 5.3 %collective-permute-start.14 = (f32[8,1,384]{2,0,1:T(8,128)S(1)}, f32[8,1,384]{2,0,1:T(8,128)S(1)}, u32[]{:S(2)}, u32[]{:S(2)}) collective-permute-start(f32[8,1,384]{2,0,1:T(8,128)S(1)} %copy.134), channel_id=1, source_target_pairs={{1,0},{4,1},{5,4},{8,5},{9,8},{12,9},{13,12},{0,13},{3,2},{6,3},{7... | collective-permute-start | bytes 36872 | tf_op jit(solution)/shard_map/ppermute | solution.py:19
  92.9 3.6 %collective-permute-start.15 = (f32[8,74,1]{1,0,2:T(8,128)S(1)}, f32[8,74,1]{1,0,2:T(8,128)S(1)}, u32[]{:S(2)}, u32[]{:S(2)}) collective-permute-start(f32[8,74,1]{1,0,2:T(8,128)S(1)} %get-tuple-element.83), channel_id=1, source_target_pairs={{0,2},{2,0},{1,3},{3,1},{4,6},{6,4},{5,7},{7,5},{8,10},{10,8},{9,1... | collective-permute-start | bytes 7112 | tf_op jit(solution)/shard_map/ppermute | solution.py:18
  94.5 3.6 %collective-permute-start.16 = (f32[8,74,1]{1,0,2:T(8,128)S(1)}, f32[8,74,1]{1,0,2:T(8,128)S(1)}, u32[]{:S(2)}, u32[]{:S(2)}) collective-permute-start(f32[8,74,1]{1,0,2:T(8,128)S(1)} %get-tuple-element.84), channel_id=1, source_target_pairs={{2,0},{0,2},{3,1},{1,3},{6,4},{4,6},{7,5},{5,7},{10,8},{8,10},{11,... | collective-permute-start | bytes 7112 | tf_op jit(solution)/shard_map/ppermute | solution.py:19
  157.7 6.9 %collective-permute-start.17 = (f32[8,24,256]{2,1,0:T(8,128)S(1)}, f32[8,24,256]{2,1,0:T(8,128)S(1)}, u32[]{:S(2)}, u32[]{:S(2)}) collective-permute-start(f32[8,24,256]{2,1,0:T(8,128)S(1)} %all_gather.3), channel_id=1, source_target_pairs={{0,1},{1,4},{4,5},{5,8},{8,9},{9,12},{12,13},{13,0},{2,3},{3,6},{6... | collective-permute-start | bytes 589832 | tf_op jit(solution)/shard_map/ppermute | solution.py:27
  159.2 7.9 %copy-start.1 = (f32[8,24,256]{1,0,2:T(8,128)S(1)}, f32[8,24,256]{1,0,2:T(8,128)}, u32[]{:S(2)}) copy-start(f32[8,24,256]{1,0,2:T(8,128)} %copy-done) | copy-start | bytes 589828
where the time goes:
time: 172 us; the launch traced here: 171 us
  local copies, waits for them, and re-layouts  80.1 us (47%)
  other arithmetic  45.3 us (26%)
  starting transfers between devices  21 us (12%)
  blocking collectives  13.9 us (8%)
  waiting for transfers between devices  8.16 us (5%)
  between operations  2.51 us (1%)
    reshape x1, local copies, waits for them, and re-layouts, shards(): nest_now.reshape(level_count, parent_rows, RATIO, foot_cols, RATIO)  21.8 us
    reduce_sum x1, other arithmetic, shards(): nest_now.reshape(level_count, parent_rows, RATIO, foot_cols, RATIO)  14.8 us
    ppermute x8, starting transfers between devices, with_halo(): after = lax.ppermute(leading, axis, down)  14.3 us
    scatter x1, local copies, waits for them, and re-layouts, shards(): force_grid_field.at[:, :, tail_start:]  11.7 us
    unnamed x41, local copies, waits for them, and re-layouts  10.6 us
    mul x4, other arithmetic, col_mask(): return grid_field * ymask[None, None, :]  10.2 us
    add x4, other arithmetic, diffuse(): center + coefs_h[:, None, None] * lateral  9.19 us
    slice x6, local copies, waits for them, and re-layouts, with_halo(): last = lax.slice_in_dim(shard, length - width, length, axis=dim)  9.06 us
  transfers between devices with their start and end apart: 18, of which 6 were waited for; matrix products, arithmetic and copies ran while one was open for 23% of the time, Pallas kernels for 0%

commit v1 on v0

v1 whole, which is shorter than its diff:
```python
import functools

import jax
import jax.numpy as jnp
from jax import lax
from jax.experimental import pallas as pl
from jax.experimental.pallas import tpu as pltpu
from jax.sharding import PartitionSpec as P

RATIO = 3
SUBSTEPS = 3
RIM = 6
LANES = 128
PARENT_LANE = 48
STRIP_LANE = 64
STRIP_SOURCE = 96
SOURCE_ROW = 24
TAIL_ROW = 40
VMEM = pltpu.VMEM
LIMIT = 24 * 1024 * 1024
HIGHEST = lax.Precision.HIGHEST


def iota(shape, dim):
    return lax.broadcasted_iota(jnp.int32, shape, dim)


def whole():
    return pl.BlockSpec(memory_space=VMEM)


def scalars():
    return pl.BlockSpec(memory_space=pltpu.SMEM)


def params():
    return pltpu.CompilerParams(vmem_limit_bytes=LIMIT)


def cost(flops, moved):
    return pl.CostEstimate(flops=flops, bytes_accessed=moved, transcendentals=0)


def tile(ref, level, index):
    return ref[level, :, index * LANES : (index + 1) * LANES]


def pack_columns(parts, band, oy_ref, nest, source, parent, parent_source, *rest):
    outs, (old_buf, src_buf, sems) = rest[:parts], rest[parts:]
    levels, rows, cols = nest.shape
    parent_cols = parent.shape[2]
    me = lax.axis_index("gy")
    oy = oy_ref[0]
    sides = [1] if parts == 2 else [1, parts - 1]
    copies = []
    for at, step in enumerate(sides):
        right = (me == 0) if parts == 2 else jnp.bool_(step == 1)
        start = pl.multiple_of(jnp.where(right, cols - LANES, 0), LANES)
        pair = [
            pltpu.make_async_copy(
                ref.at[:, :, pl.ds(start, LANES)], buf.at[at], sems.at[at, which]
            )
            for which, (ref, buf) in enumerate(((nest, old_buf), (source, src_buf)))
        ]
        for copy in pair:
            copy.start()
        copies.append((right, pair))
    lane = iota((parent.shape[1], LANES), 1)

    def strip(dest):
        base = jnp.where(dest == 0, oy - 1, oy + band - 3) - me * parent_cols
        total = jnp.zeros(lane.shape, jnp.float32)
        for ref, first in ((parent, STRIP_LANE), (parent_source, STRIP_SOURCE)):
            for level in range(levels):
                found = jnp.zeros(lane.shape, jnp.float32)
                for at in range(parent_cols // LANES):
                    place = lane + (at * LANES - base)
                    found = jnp.where(
                        (place >= 0) & (place < 4), tile(ref, level, at), found
                    )
                turn = (16384 + first + 4 * level - base) & (LANES - 1)
                total = total + pltpu.roll(found, turn, 1)
        return total

    outs[0][...] = strip(me)
    for step in range(1, parts):
        out = outs[step]
        part = strip(lax.rem(me + step, parts))
        if step not in sides:
            out[...] = part
            continue
        at = sides.index(step)
        right, pair = copies[at]
        first = jnp.where(right, LANES - 3, 0)
        for level in range(levels):
            edge = jnp.where(
                right, tile(parent, level, parent_cols // LANES - 1), tile(parent, level, 0)
            )
            edge = jnp.where(lane == jnp.where(right, LANES - 1, 0), edge, 0.0)
            turn = (LANES + PARENT_LANE + level - jnp.where(right, LANES - 1, 0)) & (LANES - 1)
            part = part + pltpu.roll(edge, turn, 1)
        for copy in pair:
            copy.wait()
        fine = iota((rows, LANES), 1) - first
        wanted = (fine >= 0) & (fine < 3)
        total = jnp.zeros((rows, LANES), jnp.float32)
        for level in range(levels):
            for buf, shift in ((old_buf, 0), (src_buf, 3)):
                value = jnp.where(wanted, buf[at, level], 0.0)
                turn = (LANES + 6 * level + shift - first) & (LANES - 1)
                total = total + pltpu.roll(value, turn, 1)
        out[...] = total
        out[: part.shape[0], :] += part


def with_columns(tiles, left, right, me, parts, place):
    lane = iota(left.shape, 1)
    from_right = pltpu.roll(right, (LANES - place) % LANES, 1)
    from_left = pltpu.roll(left, (2 * LANES - 3 - place) % LANES, 1)
    if parts == 2:
        tiles[0] = jnp.where((lane < 3) & (me == 0), from_right, tiles[0])
        tiles[-1] = jnp.where((lane >= LANES - 3) & (me == 1), from_left, tiles[-1])
        return tiles
    extra = jnp.where(lane < 3, from_right, jnp.where(lane >= LANES - 3, from_left, 0.0))
    return tiles + [extra]


def pack_rows(
    parts, old_top, old_end, src_top, src_end, par_top, par_end, own_strip, *rest
):
    columns = rest[: parts - 1]
    up, down, far, strip_out = rest[parts - 1 :]
    levels, _, cols = old_top.shape
    me = lax.axis_index("gy")
    left, right = columns[0], columns[-1]
    rows = left.shape[0]
    strip_rows = own_strip.shape[0]
    lane = iota((strip_rows, LANES), 1)
    strips = own_strip[...]
    for message in columns:
        strips = strips + message[:strip_rows, :]
    strips = jnp.where(lane >= STRIP_LANE, strips, 0.0)
    strip_out[...] = strips
    far[...] = strips[:8]
    pieces = cols // LANES
    for out, old, src, first, at, src_at in (
        (up, old_end, src_end, rows - 8, 5, 6),
        (down, old_top, src_top, 0, 0, 0),
    ):
        y_left = left[first : first + 8, :]
        y_right = right[first : first + 8, :]
        for level in range(levels):
            for ref, shift, row, count, base in (
                (old, 0, at, 3, 0),
                (src, 3, src_at, 2, SOURCE_ROW),
            ):
                tiles = [tile(ref, level, piece) for piece in range(pieces)]
                tiles = with_columns(tiles, y_left, y_right, me, parts, 6 * level + shift)
                for piece, value in enumerate(tiles):
                    out[
                        base + count * level : base + count * (level + 1),
                        piece * LANES : (piece + 1) * LANES,
                    ] = value[row : row + count]
    parent_cols = par_top.shape[2]
    for level in range(levels):
        up[TAIL_ROW + level : TAIL_ROW + level + 1, :parent_cols] = par_end[level, 7:8, :]
        down[TAIL_ROW + level : TAIL_ROW + level + 1, :parent_cols] = par_top[level, 0:1, :]
    up[TAIL_ROW : TAIL_ROW + 8, parent_cols : parent_cols + LANES] = strips[strip_rows - 8 :]
    down[TAIL_ROW : TAIL_ROW + 8, parent_cols : parent_cols + LANES] = strips[:8]
    down[TAIL_ROW + 8 : TAIL_ROW + 16, :LANES] = strips[8:16]
    down[TAIL_ROW + 8 : TAIL_ROW + 16, LANES : 2 * LANES] = strips[16:24]


def nest_steps(
    parts,
    parent_cols,
    ox_ref,
    parent_coefs,
    coefs,
    nest,
    source,
    strips,
    before,
    after,
    beyond,
    y_left,
    y_right,
    nest_out,
    coarse_out,
    ping,
    pong,
    src,
    rim_old,
    rim_diff,
    result,
    thin,
    sems,
):
    levels, rows, cols = nest.shape
    ring = ping.shape[1]
    width = ping.shape[2]
    pieces = cols // LANES
    strip_rows = strips.shape[0]
    me = lax.axis_index("gy")
    ox = ox_ref[0]
    loads = [
        pltpu.make_async_copy(nest, ping.at[1 : levels + 1, :rows, :cols], sems.at[0]),
        pltpu.make_async_copy(source, src.at[:, :rows, :cols], sems.at[1]),
    ]
    for copy in loads:
        copy.start()

    old = jnp.concatenate(
        [
            strips[...],
            after[TAIL_ROW : TAIL_ROW + 8, parent_cols : parent_cols + LANES],
            after[TAIL_ROW + 8 : TAIL_ROW + 16, :LANES],
            after[TAIL_ROW + 8 : TAIL_ROW + 16, LANES : 2 * LANES],
            jnp.where(
                iota((8, LANES), 0) == 0,
                beyond[...],
                jnp.where(
                    iota((8, LANES), 0) == 7,
                    before[TAIL_ROW : TAIL_ROW + 8, parent_cols : parent_cols + LANES],
                    0.0,
                ),
            ),
        ],
        axis=0,
    )
    count = old.shape[0]
    lane = iota(old.shape, 1)
    coef_h = jnp.zeros(old.shape, jnp.float32)
    coef_v = jnp.zeros(old.shape, jnp.float32)
    for level in range(levels):
        here = lane >= STRIP_LANE + 4 * level
        coef_h = jnp.where(here, parent_coefs[0, level], coef_h)
        coef_v = jnp.where(here, parent_coefs[1, level], coef_v)
    lateral = (
        pltpu.roll(old, 1, 0)
        + pltpu.roll(old, count - 1, 0)
        + pltpu.roll(old, 1, 1)
        + pltpu.roll(old, LANES - 1, 1)
        - 4.0 * old
    )
    higher = jnp.where(lane < STRIP_SOURCE - 4, pltpu.roll(old, LANES - 4, 1), 0.0)
    vertical = pltpu.roll(old, 4, 1) + higher - 2.0 * old
    forcing = pltpu.roll(old, LANES - (STRIP_SOURCE - STRIP_LANE), 1)
    diff = coef_h * lateral + coef_v * vertical + forcing
    index = iota((ring, count), 0)
    parent_row = jnp.where(index < rows + 3, (index * 171) >> 9, -1) + ox
    pick = (iota((ring, count), 1) == parent_row).astype(jnp.float32)
    picked = jnp.dot(
        pick,
        jnp.concatenate([old, diff], axis=1),
        precision=HIGHEST,
        preferred_element_type=jnp.float32,
    )
    lane = iota((ring, LANES), 1)
    first = jnp.where(me == 0, 0, LANES - RIM)
    column = jnp.where((lane >= first + 3) & (lane < first + RIM), 2, 1)
    for level in range(levels):
        at = column + (STRIP_LANE + 4 * level)
        rim_old[level] = jnp.take_along_axis(picked[:, :LANES], at, axis=1)
        rim_diff[level] = jnp.take_along_axis(picked[:, LANES:], at, axis=1)

    zero = jnp.zeros((ring, width), jnp.float32)
    for buf in (ping, pong):
        buf[0] = zero
        buf[levels + 1] = zero
    for level in range(levels):
        for buf, lead, base, n in ((ping, 1, 0, 3), (src, 0, SOURCE_ROW, 2)):
            rest = slice(base + n * level, base + n * (level + 1))
            buf[level + lead, rows : rows + n, :] = after[rest, :]
            buf[level + lead, ring - n : ring, :] = before[rest, :]
    for copy in loads:
        copy.wait()
    left = y_left[...]
    right = y_right[...]
    for level in range(levels):
        for buf, lead, shift in ((ping, 1, 0), (src, 0, 3)):
            edges = [
                buf[level + lead, :rows, :LANES],
                buf[level + lead, :rows, cols - LANES : cols],
            ]
            edges = with_columns(edges, left, right, me, parts, 6 * level + shift)
            if parts == 2:
                buf[level + lead, :rows, :LANES] = edges[0]
                buf[level + lead, :rows, cols - LANES : cols] = edges[1]
            else:
                buf[level + lead, :rows, cols:] = edges[2]

    lane = iota((8, LANES), 1)
    sub = iota((8, width), 0)
    is_south = me == 0
    is_north = me == parts - 1

    def substep(here, there, weight, last):
        low = 0 if last or parts > 2 else 3
        south = (lane >= low) & (lane < RIM) & is_south
        north = (lane >= LANES - RIM) & (lane < LANES - low) & is_north
        tiles = rows // 8 if last else ring // 8

        def one_level(level, carry):
            ch = coefs[0, level]
            cv = coefs[1, level]
            centre = 1.0 - 4.0 * ch - 2.0 * cv

            def row_tile(t):
                t = t % (ring // 8)
                return here[level + 1, 8 * t : 8 * t + 8, :]

            now = row_tile(-1)
            down_before = pltpu.roll(now, 1, 0)
            now = row_tile(0)
            up_now = pltpu.roll(now, 7, 0)
            for t in range(tiles):
                following = row_tile(t + 1)
                down_now = pltpu.roll(now, 1, 0)
                up_next = pltpu.roll(following, 7, 0)
                around = jnp.where(sub == 0, down_before, down_now) + jnp.where(
                    sub == 7, up_next, up_now
                )
                around = around + (pltpu.roll(now, 1, 1) + pltpu.roll(now, width - 1, 1))
                span = slice(8 * t, 8 * t + 8)
                stacked = here[level, span, :] + here[level + 2, span, :]
                value = centre * now + ch * around + (cv * stacked + src[level, span, :])
                rim = rim_old[level, span, :] + weight * rim_diff[level, span, :]
                if last:
                    store, at, stop = there, level, pieces
                else:
                    store, at, stop = there, level + 1, width // LANES
                for piece in range(stop):
                    part = value[:, piece * LANES : (piece + 1) * LANES]
                    if piece == 0:
                        part = jnp.where(south, rim, part)
                    if piece == pieces - 1:
                        part = jnp.where(north, rim, part)
                    store[at, span, piece * LANES : (piece + 1) * LANES] = part
                down_before, now, up_now = down_now, following, up_next
            return carry

        lax.fori_loop(0, levels, one_level, 0)

    substep(ping, pong, 1.0 / 3.0, False)
    substep(pong, ping, 2.0 / 3.0, False)
    substep(ping, result, 1.0, True)
    store = pltpu.make_async_copy(result, nest_out, sems.at[2])
    store.start()
    foot = cols // RATIO
    offset = iota((cols, foot), 0) - RATIO * iota((cols, foot), 1)
    gather = ((offset >= 0) & (offset < RATIO)).astype(jnp.float32)
    flat = result[...].reshape(levels * rows, cols)
    thin[...] = jnp.dot(
        flat, gather, precision=HIGHEST, preferred_element_type=jnp.float32
    )
    total = levels * rows // RATIO
    means = (
        thin[pl.ds(0, total, RATIO), :]
        + thin[pl.ds(1, total, RATIO), :]
        + thin[pl.ds(2, total, RATIO), :]
    ) * (1.0 / 9.0)
    coarse_out[...] = means.reshape(coarse_out.shape)
    store.wait()


def parent_step(parts, coefs, parent, source, before, after, y_left, y_right, out):
    levels, rows, cols = parent.shape
    me = lax.axis_index("gy")
    row = iota((rows, cols), 0)
    lane = iota((rows, cols), 1)
    has_left = me > 0
    has_right = me < parts - 1
    left = y_left[:rows, :]
    right = y_right[:rows, :]
    zero = jnp.zeros((rows, cols), jnp.float32)
    for level in range(levels):
        now = parent[level]
        from_left = left[:, PARENT_LANE + level : PARENT_LANE + level + 1]
        from_right = right[:, PARENT_LANE + level : PARENT_LANE + level + 1]
        top = before[TAIL_ROW + level : TAIL_ROW + level + 1, :cols]
        end = after[TAIL_ROW + level : TAIL_ROW + level + 1, :cols]
        around = (
            jnp.where(row == 0, top, pltpu.roll(now, 1, 0))
            + jnp.where(row == rows - 1, end, pltpu.roll(now, rows - 1, 0))
            + jnp.where(
                lane == 0, jnp.where(has_left, from_left, 0.0), pltpu.roll(now, 1, 1)
            )
            + jnp.where(
                lane == cols - 1,
                jnp.where(has_right, from_right, 0.0),
                pltpu.roll(now, cols - 1, 1),
            )
        )
        stacked = (parent[level - 1] if level > 0 else zero) + (
            parent[level + 1] if level < levels - 1 else zero
        )
        ch = coefs[0, level]
        cv = coefs[1, level]
        out[level] = (
            (1.0 - 4.0 * ch - 2.0 * cv) * now + ch * around + (cv * stacked + source[level])
        )


def merge(parts, band, ox_ref, oy_ref, step, *rest):
    own, previous, out, joined = (
        rest[:parts],
        rest[parts : 2 * parts],
        rest[2 * parts],
        rest[2 * parts + 1],
    )
    levels, rows, cols = step.shape
    foot = own[0].shape[2]
    me = lax.axis_index("gy")
    ox = ox_ref[0]
    oy = oy_ref[0]
    for k in range(parts):
        joined[k, :, :rows, :] = previous[k][...]
        joined[k, :, rows:, :] = own[k][...]
    lane = iota((rows, LANES), 1)
    for level in range(levels):
        values = [tile(step, level, piece) for piece in range(cols // LANES)]
        for k in range(parts):
            source = lax.rem(me + parts - k, parts)
            block = joined[k, level, pl.ds(rows - ox, rows), :]
            begin = oy + source * foot - me * cols
            block = pltpu.roll(block, (16384 + begin) & (LANES - 1), 1)
            low = jnp.maximum(source * foot, 2)
            high = jnp.minimum((source + 1) * foot, band - 2)
            for piece in range(cols // LANES):
                at = lane + (piece * LANES + me * cols - oy)
                values[piece] = jnp.where((at >= low) & (at < high), block, values[piece])
        for piece, value in enumerate(values):
            out[level, :, piece * LANES : (piece + 1) * LANES] = value


def shifted(value, axis, steps):
    count = lax.axis_size(axis)
    pairs = [(source, (source + steps) % count) for source in range(count)]
    return lax.ppermute(value, axis, pairs)


def shards(
    parent_old, parent_source, parent_coefs, nest_old, nest_source, nest_coefs, offset_x, offset_y
):
    parts = lax.axis_size("gy")
    along = ("gx", "gz")
    levels, parent_rows, parent_cols = parent_old.shape
    _, rows, cols = nest_old.shape
    foot = cols // RATIO
    band = foot * parts
    width = cols if parts == 2 else cols + LANES
    ring = rows + 8
    f32 = jnp.float32
    shape = jax.ShapeDtypeStruct
    sides = 1 if parts == 2 else 2
    messages = [shape((parent_rows, LANES), f32)] + [
        shape((rows if k in (1, parts - 1) else parent_rows, LANES), f32)
        for k in range(1, parts)
    ]
    anywhere = pl.BlockSpec(memory_space=pl.ANY)
    packed = pl.pallas_call(
        functools.partial(pack_columns, parts, band),
        out_shape=messages,
        in_specs=[scalars(), anywhere, anywhere, whole(), whole()],
        out_specs=[whole()] * parts,
        scratch_shapes=[
            VMEM((sides, levels, rows, LANES), f32),
            VMEM((sides, levels, rows, LANES), f32),
            pltpu.SemaphoreType.DMA((sides, 2)),
        ],
        compiler_params=params(),
        cost_estimate=cost(200000, 1000000),
        name="pack_columns",
    )(offset_y, nest_old, nest_source, parent_old, parent_source)
    columns = [shifted(packed[k], "gy", k) for k in range(1, parts)]

    def block(ref, last):
        count = ref.shape[1] // 8 - 1 if last else 0
        return pl.BlockSpec((levels, 8, ref.shape[2]), lambda i, c=count: (0, c, 0))

    def full(extent):
        return pl.BlockSpec(extent, lambda i: (0,) * len(extent))

    outs = [
        shape((TAIL_ROW + 8, width), f32),
        shape((TAIL_ROW + 16, width), f32),
        shape((8, LANES), f32),
        shape((parent_rows, LANES), f32),
    ]
    up, down, far, strips = pl.pallas_call(
        functools.partial(pack_rows, parts),
        out_shape=outs,
        grid=(1,),
        in_specs=[
            block(nest_old, False),
            block(nest_old, True),
            block(nest_old, False),
            block(nest_old, True),
            block(parent_old, False),
            block(parent_old, True),
            full(packed[0].shape),
        ]
        + [full(message.shape) for message in columns],
        out_specs=[full(out.shape) for out in outs],
        compiler_params=params(),
        cost_estimate=cost(100000, 700000),
        name="pack_rows",
    )(nest_old, nest_old, nest_source, nest_source, parent_old, parent_old, packed[0], *columns)
    before = shifted(up, along, 1)
    after = shifted(down, along, -1)
    beyond = shifted(far, along, -2)
    nest_new, coarse = pl.pallas_call(
        functools.partial(nest_steps, parts, parent_cols),
        out_shape=[
            shape(nest_old.shape, f32),
            shape((levels, parent_rows, foot), f32),
        ],
        in_specs=[scalars()] * 3 + [anywhere] * 2 + [whole()] * 6,
        out_specs=[anywhere, whole()],
        scratch_shapes=[
            VMEM((levels + 2, ring, width), f32),
            VMEM((levels + 2, ring, width), f32),
            VMEM((levels, ring, width), f32),
            VMEM((levels, ring, LANES), f32),
            VMEM((levels, ring, LANES), f32),
            VMEM((levels, rows, cols), f32),
            VMEM((levels * rows, foot), f32),
            pltpu.SemaphoreType.DMA((3,)),
        ],
        compiler_params=params(),
        cost_estimate=cost(10000000, 3000000),
        name="nest_steps",
    )(
        offset_x,
        parent_coefs,
        nest_coefs,
        nest_old,
        nest_source,
        strips,
        before,
        after,
        beyond,
        columns[0],
        columns[-1],
    )
    own = [coarse] + [shifted(coarse, "gy", k) for k in range(1, parts)]
    previous = [shifted(coarse, along, 1)] + [
        shifted_both(coarse, k) for k in range(1, parts)
    ]
    step = pl.pallas_call(
        functools.partial(parent_step, parts),
        out_shape=shape(parent_old.shape, f32),
        in_specs=[scalars()] + [whole()] * 6,
        out_specs=whole(),
        compiler_params=params(),
        cost_estimate=cost(800000, 800000),
        name="parent_step",
    )(parent_coefs, parent_old, parent_source, before, after, columns[0], columns[-1])
    parent_new = pl.pallas_call(
        functools.partial(merge, parts, band),
        out_shape=shape(parent_old.shape, f32),
        in_specs=[scalars()] * 2 + [whole()] * (1 + 2 * parts),
        out_specs=whole(),
        scratch_shapes=[VMEM((parts, levels, 2 * parent_rows, foot), f32)],
        compiler_params=params(),
        cost_estimate=cost(200000, 800000),
        name="merge",
    )(offset_x, offset_y, step, *own, *previous)
    return (parent_new, nest_new)


def shifted_both(value, steps):
    sizes = [lax.axis_size(axis) for axis in ("gx", "gy", "gz")]
    gx, gy, gz = sizes
    pairs = []
    for x in range(gx):
        for y in range(gy):
            for z in range(gz):
                place = (x * gz + z + 1) % (gx * gz)
                target = (place // gz * gy + (y + steps) % gy) * gz + place % gz
                pairs.append(((x * gy + y) * gz + z, target))
    return lax.ppermute(value, ("gx", "gy", "gz"), pairs)


def solution(mesh):
    return jax.shard_map(
        shards,
        mesh=mesh,
        in_specs=(
            P(None, ("grp", "gx", "gz"), "gy"),
            P(None, ("grp", "gx", "gz"), "gy"),
            P(),
            P(None, ("grp", "gx", "gz"), "gy"),
            P(None, ("grp", "gx", "gz"), "gy"),
            P(),
            P("grp"),
            P("grp"),
        ),
        out_specs=(P(None, ("grp", "gx", "gz"), "gy"), P(None, ("grp", "gx", "gz"), "gy")),
        check_vma=False,
    )
```

time: 172 us -> 34.2 us (0.20)
  local copies, waits for them, and re-layouts: 80.1 us -> 4.2 us
  other arithmetic: 45.3 us -> 0 us
  blocking collectives: 13.9 us -> 0 us
  starting transfers between devices: 21 us -> 9.38 us
  Pallas kernels: 0 us -> 8.3 us
  waiting for transfers between devices: 8.16 us -> 9.99 us
    reshape x4 -> x0, local copies, waits for them, and re-layouts: 22.1 us -> none  [the longest x1 21.8 us: shards(): nest_now.reshape(level_count, parent_rows, RATIO, foot_cols, RATIO)]
    ppermute x16 -> x1, starting transfers between devices: 20.9 us -> 0.54 us  [shifted_both(): return lax.ppermute(value, ('gx', 'gy', 'gz'), pairs)]
    reduce_sum x1 -> x0, other arithmetic: 14.8 us -> none  [shards(): nest_now.reshape(level_count, parent_rows, RATIO, foot_cols, RATIO)]
    slice x9 -> x0, local copies, waits for them, and re-layouts: 13.8 us -> none  [the longest x6 9.06 us: with_halo(): last = lax.slice_in_dim(shard, length - width, length, axis=dim)]
    scatter x1 -> x0, local copies, waits for them, and re-layouts: 11.7 us -> none  [shards(): force_grid_field.at[:, :, tail_start:]]
    mul x5 -> x0, other arithmetic: 10.2 us -> none  [the longest x4 10.2 us: col_mask(): return grid_field * ymask[None, None, :]]
    ppermute x6 -> x0, local copies, waits for them, and re-layouts: 10.1 us -> none  [the longest x3 5.08 us: with_halo(): after = lax.ppermute(leading, axis, down)]
    add x5 -> x0, other arithmetic: 9.2 us -> none  [the longest x4 9.19 us: diffuse(): center + coefs_h[:, None, None] * lateral]
  transfers between devices with their start and end apart: 18 -> 7, of which waited for: 6 -> 5; matrix products, arithmetic and copies ran while one was open for 23% -> 0% of each run, Pallas kernels for 0% -> 2%
where the time goes in v1:
time: 34.2 us; the launch traced here: 33.9 us
  waiting for transfers between devices  9.99 us (29%)
  starting transfers between devices  9.38 us (27%)
  Pallas kernels  8.3 us (24%)
  local copies, waits for them, and re-layouts  4.2 us (12%)
  between operations  2.02 us (6%)
    ppermute x6, starting transfers between devices, shifted(): return lax.ppermute(value, axis, pairs)  8.84 us
    pallas_call x1, Pallas kernels, shards(): pl.pallas_call(functools.partial(nest_steps, parts, parent_cols), out_sha...  6.09 us
    ppermute x6, waiting for transfers between devices, shifted(): return lax.ppermute(value, axis, pairs)  5.7 us
    ppermute x1, waiting for transfers between devices, shifted_both(): return lax.ppermute(value, ('gx', 'gy', 'gz'), pairs)  4.29 us
    unnamed x16, local copies, waits for them, and re-layouts  4.2 us
    pallas_call x1, Pallas kernels, shards(): pl.pallas_call(functools.partial(merge, parts, band), out_shape=shape(par...  0.82 us
    pallas_call x1, Pallas kernels, shards(): pl.pallas_call(functools.partial(parent_step, parts), out_shape=shape(par...  0.8 us
  transfers between devices with their start and end apart: 7, of which 5 were waited for; matrix products, arithmetic and copies ran while one was open for 0% of the time, Pallas kernels for 2%

profile of v1, /device:TPU:0, one launch (start us, length us, event | category | flops | bytes accessed | tf_op | source)
XLA Modules:
  0.0 33.9 jit_solution(3104367479772595135)
XLA Ops:
  1.3 0.0 copy-start
  1.3 1.2 %copy-done = f32[8,72,384]{2,1,0:T(8,128)S(1)} copy-done((f32[8,72,384]{2,1,0:T(8,128)S(1)}, f32[8,72,384]{2,1,0:T(8,128)}, u32[]{:S(2)}) %copy-start) | copy-done | bytes 884760
  2.4 0.0 copy-start.1
  2.4 1.2 %copy-done.1 = f32[8,72,384]{2,1,0:T(8,128)S(1)} copy-done((f32[8,72,384]{2,1,0:T(8,128)S(1)}, f32[8,72,384]{2,1,0:T(8,128)}, u32[]{:S(2)}) %copy-start.1) | copy-done | bytes 884760
  3.6 0.0 copy-start.2
  3.6 0.9 %copy-done.2 = f32[8,24,256]{2,1,0:T(8,128)S(1)} copy-done((f32[8,24,256]{2,1,0:T(8,128)S(1)}, f32[8,24,256]{2,1,0:T(8,128)}, u32[]{:S(2)}) %copy-start.2) | copy-done | bytes 196632
  4.5 0.0 copy-start.4
  4.5 0.9 %copy-done.4 = f32[8,24,256]{2,1,0:T(8,128)S(1)} copy-done((f32[8,24,256]{2,1,0:T(8,128)S(1)}, f32[8,24,256]{2,1,0:T(8,128)}, u32[]{:S(2)}) %copy-start.4) | copy-done | bytes 196632
  5.5 0.5 %pack_columns.1 = (f32[24,128]{1,0:T(8,128)S(1)}, f32[72,128]{1,0:T(8,128)S(1)}) custom-call(s32[1]{0:T(128)S(6)} %copy.11.oy_ref, f32[8,72,384]{2,1,0:T(8,128)S(1)} %copy-done, f32[8,72,384]{2,1,0:T(8,128)S(1)} %copy-done.1, f32[8,24,256]{2,1,0:T(8,128)S(1)} %copy-done.2, f32[8,24,256]{2,1,0:T(8,128)S(1)} %copy-done.4), custom_call_target="tpu_custom_call" | custom-call | flops 200000 | bytes 1000000 | tf_op jit(solution)/shard_map/pack_columns/pallas_call | solution.py:462
  6.0 3.0 %collective-permute-start = (f32[72,128]{1,0:T(8,128)S(1)}, f32[72,128]{1,0:T(8,128)S(1)}, u32[]{:S(2)}, u32[]{:S(2)}) collective-permute-start(f32[72,128]{1,0:T(8,128)S(1)} %get-tuple-element.11), channel_id=1, source_target_pairs={{0,2},{2,0},{1,3},{3,1},{4,6},{6,4},{5,7},{7,5},{8,10},{10,8},{9,1... | collective-permute-start | bytes 110600 | tf_op jit(solution)/shard_map/ppermute | solution.py:440
  9.0 1.9 %collective-permute-done.rest_0_.y_left.y_right = f32[72,128]{1,0:T(8,128)S(1)} collective-permute-done((f32[72,128]{1,0:T(8,128)S(1)}, f32[72,128]{1,0:T(8,128)S(1)}, u32[]{:S(2)}, u32[]{:S(2)}) %collective-permute-start) | collective-permute-done | bytes 36896 | tf_op jit(solution)/shard_map/ppermute | solution.py:440
  10.9 0.1 pack_rows.1
  11.0 2.5 %collective-permute-start.2 = (f32[56,384]{1,0:T(8,128)S(1)}, f32[56,384]{1,0:T(8,128)S(1)}, u32[]{:S(2)}, u32[]{:S(2)}) collective-permute-start(f32[56,384]{1,0:T(8,128)S(1)} %get-tuple-element.13), channel_id=1, source_target_pairs={{0,13},{1,0},{4,1},{5,4},{8,5},{9,8},{12,9},{13,12},{2,15},{3,2},{... | collective-permute-start | bytes 258056 | tf_op jit(solution)/shard_map/ppermute | solution.py:440
  13.5 0.0 collective-permute-start.1
  13.5 2.2 %collective-permute-start.3 = (f32[8,128]{1,0:T(8,128)S(1)}, f32[8,128]{1,0:T(8,128)S(1)}, u32[]{:S(2)}, u32[]{:S(2)}) collective-permute-start(f32[8,128]{1,0:T(8,128)S(1)} %get-tuple-element.15), channel_id=1, source_target_pairs={{0,12},{1,13},{4,0},{5,1},{8,4},{9,5},{12,8},{13,9},{2,14},{3,15},... | collective-permute-start | bytes 12296 | tf_op jit(solution)/shard_map/ppermute | solution.py:440
  15.7 0.0 copy-start.7
  16.4 0.0 copy-start.6
  16.4 0.7 %collective-permute-done.3.beyond = f32[8,128]{1,0:T(8,128)S(1)} collective-permute-done((f32[8,128]{1,0:T(8,128)S(1)}, f32[8,128]{1,0:T(8,128)S(1)}, u32[]{:S(2)}, u32[]{:S(2)}) %collective-permute-start.3) | collective-permute-done | bytes 4128 | tf_op jit(solution)/shard_map/ppermute | solution.py:440
  17.1 2.0 %collective-permute-done.1.before = f32[48,384]{1,0:T(8,128)S(1)} collective-permute-done((f32[48,384]{1,0:T(8,128)S(1)}, f32[48,384]{1,0:T(8,128)S(1)}, u32[]{:S(2)}, u32[]{:S(2)}) %collective-permute-start.1) | collective-permute-done | bytes 73760 | tf_op jit(solution)/shard_map/ppermute | solution.py:440
  19.1 0.0 collective-permute-done.2.after
  19.1 0.0 copy-done.7
  19.1 0.0 copy-done.6
  19.1 0.0 copy-start.3
  19.1 0.0 copy-start.5
  19.1 6.1 %nest_steps.1 = (f32[8,72,384]{2,1,0:T(8,128)}, f32[8,24,128]{2,1,0:T(8,128)S(1)}) custom-call(s32[1]{0:T(128)S(6)} %copy.10.ox_ref, f32[2,8]{1,0:T(2,128)S(1)} %copy-done.6, f32[2,8]{1,0:T(2,128)S(1)} %copy-done.7, f32[8,72,384]{2,1,0:T(8,128)S(1)} %copy-done, f32[8,72,384]{2,1,0:T(8,128)S(1)} %copy-done.1, f32[24,128]{1,0:T(8,128)S(1)} %get-tuple-element.14.strips, ...), custom_call_target="tpu_custom_call" | custom-call | flops 10000000 | bytes 3000000 | tf_op jit(solution)/shard_map/nest_steps/pallas_call | solution.py:513
  25.2 0.5 %collective-permute-start.6 = (f32[8,24,128]{2,1,0:T(8,128)S(1)}, f32[8,24,128]{2,1,0:T(8,128)S(1)}, u32[]{:S(2)}, u32[]{:S(2)}) collective-permute-start(f32[8,24,128]{2,1,0:T(8,128)S(1)} %get-tuple-element.16.rest_0_), channel_id=1, source_target_pairs={{0,3},{1,6},{2,1},{3,4},{4,7},{5,10},{6,5},{7,8},{8,11},{9,14},{10... | collective-permute-start | bytes 294920 | tf_op jit(solution)/shard_map/ppermute | solution.py:583
  25.7 0.0 collective-permute-start.5
  25.7 1.1 %collective-permute-start.4 = (f32[8,24,128]{2,1,0:T(8,128)S(1)}, f32[8,24,128]{2,1,0:T(8,128)S(1)}, u32[]{:S(2)}, u32[]{:S(2)}) collective-permute-start(f32[8,24,128]{2,1,0:T(8,128)S(1)} %get-tuple-element.16.rest_0_), channel_id=1, source_target_pairs={{0,2},{2,0},{1,3},{3,1},{4,6},{6,4},{5,7},{7,5},{8,10},{10,8},{9,1... | collective-permute-start | bytes 294920 | tf_op jit(solution)/shard_map/ppermute | solution.py:440
  26.9 0.0 copy-done.3
  26.9 0.0 copy-done.5
  26.9 0.8 %parent_step.1.step = f32[8,24,256]{2,1,0:T(8,128)S(1)} custom-call(f32[2,8]{1,0:T(2,128)S(1)} %copy-done.6, f32[8,24,256]{2,1,0:T(8,128)S(1)} %copy-done.3, f32[8,24,256]{2,1,0:T(8,128)S(1)} %copy-done.5, f32[48,384]{1,0:T(8,128)S(1)} %collective-permute-done.1.before, f32[56,384]{1,0:T(8,128)S(1)} %collective-permute-done.2.after, ...), custom_call_target="tpu_custom_call" | custom-call | flops 800000 | bytes 800000 | tf_op jit(solution)/shard_map/parent_step/pallas_call | solution.py:551
  27.7 4.3 %collective-permute-done.6.rest_3_ = f32[8,24,128]{2,1,0:T(8,128)S(1)} collective-permute-done((f32[8,24,128]{2,1,0:T(8,128)S(1)}, f32[8,24,128]{2,1,0:T(8,128)S(1)}, u32[]{:S(2)}, u32[]{:S(2)}) %collective-permute-start.6) | collective-permute-done | bytes 98336 | tf_op jit(solution)/shard_map/ppermute | solution.py:583
  32.0 1.1 %collective-permute-done.5.rest_2_ = f32[8,24,128]{2,1,0:T(8,128)S(1)} collective-permute-done((f32[8,24,128]{2,1,0:T(8,128)S(1)}, f32[8,24,128]{2,1,0:T(8,128)S(1)}, u32[]{:S(2)}, u32[]{:S(2)}) %collective-permute-start.5) | collective-permute-done | bytes 98336 | tf_op jit(solution)/shard_map/ppermute | solution.py:440
  33.1 0.0 collective-permute-done.4.rest_1_
  33.1 0.8 %merge.1 = f32[8,24,256]{2,1,0:T(8,128)} custom-call(s32[1]{0:T(128)S(6)} %copy.10.ox_ref, s32[1]{0:T(128)S(6)} %copy.11.oy_ref, f32[8,24,256]{2,1,0:T(8,128)S(1)} %parent_step.1.step, f32[8,24,128]{2,1,0:T(8,128)S(1)} %get-tuple-element.16.rest_0_, f32[8,24,128]{2,1,0:T(8,128)S(1)} %collective-permute-done.4.rest_1_, ...), custom_call_target="tpu_custom_call" | custom-call | flops 200000 | bytes 800000 | tf_op jit(solution)/shard_map/merge/pallas_call | solution.py:560
Async XLA Ops:
  1.3 1.2 %copy-start = (f32[8,72,384]{2,1,0:T(8,128)S(1)}, f32[8,72,384]{2,1,0:T(8,128)}, u32[]{:S(2)}) copy-start(f32[8,72,384]{2,1,0:T(8,128)} %nest.3) | copy-start | bytes 2654212
  2.4 1.2 %copy-start.1 = (f32[8,72,384]{2,1,0:T(8,128)S(1)}, f32[8,72,384]{2,1,0:T(8,128)}, u32[]{:S(2)}) copy-start(f32[8,72,384]{2,1,0:T(8,128)} %source.5) | copy-start | bytes 2654212
  3.6 0.9 %copy-start.2 = (f32[8,24,256]{2,1,0:T(8,128)S(1)}, f32[8,24,256]{2,1,0:T(8,128)}, u32[]{:S(2)}) copy-start(f32[8,24,256]{2,1,0:T(8,128)} %parent.3) | copy-start | bytes 589828
  4.5 0.9 %copy-start.4 = (f32[8,24,256]{2,1,0:T(8,128)S(1)}, f32[8,24,256]{2,1,0:T(8,128)}, u32[]{:S(2)}) copy-start(f32[8,24,256]{2,1,0:T(8,128)} %source.4) | copy-start | bytes 589828
  6.0 4.9 %collective-permute-start = (f32[72,128]{1,0:T(8,128)S(1)}, f32[72,128]{1,0:T(8,128)S(1)}, u32[]{:S(2)}, u32[]{:S(2)}) collective-permute-start(f32[72,128]{1,0:T(8,128)S(1)} %get-tuple-element.11), channel_id=1, source_target_pairs={{0,2},{2,0},{1,3},{3,1},{4,6},{6,4},{5,7},{7,5},{8,10},{10,8},{9,1... | collective-permute-start | bytes 110600 | tf_op jit(solution)/shard_map/ppermute | solution.py:440
  11.0 8.1 %collective-permute-start.2 = (f32[56,384]{1,0:T(8,128)S(1)}, f32[56,384]{1,0:T(8,128)S(1)}, u32[]{:S(2)}, u32[]{:S(2)}) collective-permute-start(f32[56,384]{1,0:T(8,128)S(1)} %get-tuple-element.13), channel_id=1, source_target_pairs={{0,13},{1,0},{4,1},{5,4},{8,5},{9,8},{12,9},{13,12},{2,15},{3,2},{... | collective-permute-start | bytes 258056 | tf_op jit(solution)/shard_map/ppermute | solution.py:440
  13.5 5.6 %collective-permute-start.1 = (f32[48,384]{1,0:T(8,128)S(1)}, f32[48,384]{1,0:T(8,128)S(1)}, u32[]{:S(2)}, u32[]{:S(2)}) collective-permute-start(f32[48,384]{1,0:T(8,128)S(1)} %get-tuple-element.12), channel_id=1, source_target_pairs={{0,1},{1,4},{4,5},{5,8},{8,9},{9,12},{12,13},{13,0},{2,3},{3,6},{6... | collective-permute-start | bytes 221192 | tf_op jit(solution)/shard_map/ppermute | solution.py:440
  13.5 3.6 %collective-permute-start.3 = (f32[8,128]{1,0:T(8,128)S(1)}, f32[8,128]{1,0:T(8,128)S(1)}, u32[]{:S(2)}, u32[]{:S(2)}) collective-permute-start(f32[8,128]{1,0:T(8,128)S(1)} %get-tuple-element.15), channel_id=1, source_target_pairs={{0,12},{1,13},{4,0},{5,1},{8,4},{9,5},{12,8},{13,9},{2,14},{3,15},... | collective-permute-start | bytes 12296 | tf_op jit(solution)/shard_map/ppermute | solution.py:440
  15.7 3.4 %copy-start.7 = (f32[2,8]{1,0:T(2,128)S(1)}, f32[2,8]{1,0:T(2,128)}, u32[]{:S(2)}) copy-start(f32[2,8]{1,0:T(2,128)} %coefs.3) | copy-start | bytes 196
  16.4 2.7 %copy-start.6 = (f32[2,8]{1,0:T(2,128)S(1)}, f32[2,8]{1,0:T(2,128)}, u32[]{:S(2)}) copy-start(f32[2,8]{1,0:T(2,128)} %parent_coefs.1) | copy-start | bytes 196
  19.1 7.8 %copy-start.3 = (f32[8,24,256]{2,1,0:T(8,128)S(1)}, f32[8,24,256]{2,1,0:T(8,128)}, u32[]{:S(2)}) copy-start(f32[8,24,256]{2,1,0:T(8,128)} %parent.3) | copy-start | bytes 589828
  19.1 7.8 %copy-start.5 = (f32[8,24,256]{2,1,0:T(8,128)S(1)}, f32[8,24,256]{2,1,0:T(8,128)}, u32[]{:S(2)}) copy-start(f32[8,24,256]{2,1,0:T(8,128)} %source.4) | copy-start | bytes 589828
  25.2 6.8 %collective-permute-start.6 = (f32[8,24,128]{2,1,0:T(8,128)S(1)}, f32[8,24,128]{2,1,0:T(8,128)S(1)}, u32[]{:S(2)}, u32[]{:S(2)}) collective-permute-start(f32[8,24,128]{2,1,0:T(8,128)S(1)} %get-tuple-element.16.rest_0_), channel_id=1, source_target_pairs={{0,3},{1,6},{2,1},{3,4},{4,7},{5,10},{6,5},{7,8},{8,11},{9,14},{10... | collective-permute-start | bytes 294920 | tf_op jit(solution)/shard_map/ppermute | solution.py:583
  25.7 7.3 %collective-permute-start.5 = (f32[8,24,128]{2,1,0:T(8,128)S(1)}, f32[8,24,128]{2,1,0:T(8,128)S(1)}, u32[]{:S(2)}, u32[]{:S(2)}) collective-permute-start(f32[8,24,128]{2,1,0:T(8,128)S(1)} %get-tuple-element.16.rest_0_), channel_id=1, source_target_pairs={{0,1},{1,4},{4,5},{5,8},{8,9},{9,12},{12,13},{13,0},{2,3},{3,6},{6... | collective-permute-start | bytes 294920 | tf_op jit(solution)/shard_map/ppermute | solution.py:440
  25.7 7.3 %collective-permute-start.4 = (f32[8,24,128]{2,1,0:T(8,128)S(1)}, f32[8,24,128]{2,1,0:T(8,128)S(1)}, u32[]{:S(2)}, u32[]{:S(2)}) collective-permute-start(f32[8,24,128]{2,1,0:T(8,128)S(1)} %get-tuple-element.16.rest_0_), channel_id=1, source_target_pairs={{0,2},{2,0},{1,3},{3,1},{4,6},{6,4},{5,7},{7,5},{8,10},{10,8},{9,1... | collective-permute-start | bytes 294920 | tf_op jit(solution)/shard_map/ppermute | solution.py:440

commit v2 on v1

--- a/solution.py
+++ b/solution.py
@@ -45,13 +45,21 @@
     return ref[level, :, index * LANES : (index + 1) * LANES]
 
 
-def pack_columns(parts, band, oy_ref, nest, source, parent, parent_source, *rest):
-    outs, (old_buf, src_buf, sems) = rest[:parts], rest[parts:]
+def pack_columns(parts, band, oy_hbm, nest, source, parent_hbm, parent_source_hbm, *rest):
+    outs = rest[:parts]
+    old_buf, src_buf, parent, parent_source, oy_ref, sems, field_sems = rest[parts:]
     levels, rows, cols = nest.shape
     parent_cols = parent.shape[2]
     me = lax.axis_index("gy")
-    oy = oy_ref[0]
     sides = [1] if parts == 2 else [1, parts - 1]
+    fields = [
+        pltpu.make_async_copy(ref, buf, field_sems.at[at])
+        for at, (ref, buf) in enumerate(
+            ((oy_hbm, oy_ref), (parent_hbm, parent), (parent_source_hbm, parent_source))
+        )
+    ]
+    for copy in fields:
+        copy.start()
     copies = []
     for at, step in enumerate(sides):
         right = (me == 0) if parts == 2 else jnp.bool_(step == 1)
@@ -66,6 +74,9 @@
             copy.start()
         copies.append((right, pair))
     lane = iota((parent.shape[1], LANES), 1)
+    for copy in fields:
+        copy.wait()
+    oy = oy_ref[0]
 
     def strip(dest):
         base = jnp.where(dest == 0, oy - 1, oy + band - 3) - me * parent_cols
@@ -129,7 +140,9 @@
     parts, old_top, old_end, src_top, src_end, par_top, par_end, own_strip, *rest
 ):
     columns = rest[: parts - 1]
-    up, down, far, strip_out = rest[parts - 1 :]
+    within, across, far, strip_out, both = rest[parts - 1 :]
+    core = lax.axis_index("gz")
+    up, down = both.at[core], both.at[1 - core]
     levels, _, cols = old_top.shape
     me = lax.axis_index("gy")
     left, right = columns[0], columns[-1]
@@ -169,6 +182,8 @@
     down[TAIL_ROW : TAIL_ROW + 8, parent_cols : parent_cols + LANES] = strips[:8]
     down[TAIL_ROW + 8 : TAIL_ROW + 16, :LANES] = strips[8:16]
     down[TAIL_ROW + 8 : TAIL_ROW + 16, LANES : 2 * LANES] = strips[16:24]
+    within[...] = both[0]
+    across[...] = both[1]
 
 
 def nest_steps(
@@ -180,8 +195,8 @@
     nest,
     source,
     strips,
-    before,
-    after,
+    within,
+    across,
     beyond,
     y_left,
     y_right,
@@ -194,8 +209,13 @@
     rim_diff,
     result,
     thin,
+    both,
     sems,
 ):
+    core = lax.axis_index("gz")
+    both[0] = within[...]
+    both[1] = across[...]
+    before, after = both.at[1 - core], both.at[core]
     levels, rows, cols = nest.shape
     ring = ping.shape[1]
     width = ping.shape[2]
@@ -364,8 +384,11 @@
     store.wait()
 
 
-def parent_step(parts, coefs, parent, source, before, after, y_left, y_right, out):
+def parent_step(parts, coefs, parent, source, within, across, y_left, y_right, out, tail):
+    core = lax.axis_index("gz")
     levels, rows, cols = parent.shape
+    tail[0] = within[TAIL_ROW : TAIL_ROW + levels, :cols]
+    tail[1] = across[TAIL_ROW : TAIL_ROW + levels, :cols]
     me = lax.axis_index("gy")
     row = iota((rows, cols), 0)
     lane = iota((rows, cols), 1)
@@ -378,8 +401,8 @@
         now = parent[level]
         from_left = left[:, PARENT_LANE + level : PARENT_LANE + level + 1]
         from_right = right[:, PARENT_LANE + level : PARENT_LANE + level + 1]
-        top = before[TAIL_ROW + level : TAIL_ROW + level + 1, :cols]
-        end = after[TAIL_ROW + level : TAIL_ROW + level + 1, :cols]
+        top = tail[1 - core, level : level + 1, :]
+        end = tail[core, level : level + 1, :]
         around = (
             jnp.where(row == 0, top, pltpu.roll(now, 1, 0))
             + jnp.where(row == rows - 1, end, pltpu.roll(now, rows - 1, 0))
@@ -459,15 +482,20 @@
         for k in range(1, parts)
     ]
     anywhere = pl.BlockSpec(memory_space=pl.ANY)
+    in_hbm = pl.BlockSpec(memory_space=pltpu.HBM)
     packed = pl.pallas_call(
         functools.partial(pack_columns, parts, band),
         out_shape=messages,
-        in_specs=[scalars(), anywhere, anywhere, whole(), whole()],
+        in_specs=[in_hbm] * 5,
         out_specs=[whole()] * parts,
         scratch_shapes=[
             VMEM((sides, levels, rows, LANES), f32),
             VMEM((sides, levels, rows, LANES), f32),
+            VMEM(parent_old.shape, f32),
+            VMEM(parent_old.shape, f32),
+            pltpu.SMEM(offset_y.shape, jnp.int32),
             pltpu.SemaphoreType.DMA((sides, 2)),
+            pltpu.SemaphoreType.DMA((3,)),
         ],
         compiler_params=params(),
         cost_estimate=cost(200000, 1000000),
@@ -482,13 +510,14 @@
     def full(extent):
         return pl.BlockSpec(extent, lambda i: (0,) * len(extent))
 
+    height = TAIL_ROW + 16
     outs = [
-        shape((TAIL_ROW + 8, width), f32),
-        shape((TAIL_ROW + 16, width), f32),
+        shape((height, width), f32),
+        shape((height, width), f32),
         shape((8, LANES), f32),
         shape((parent_rows, LANES), f32),
     ]
-    up, down, far, strips = pl.pallas_call(
+    within, across, far, strips = pl.pallas_call(
         functools.partial(pack_rows, parts),
         out_shape=outs,
         grid=(1,),
@@ -503,12 +532,13 @@
         ]
         + [full(message.shape) for message in columns],
         out_specs=[full(out.shape) for out in outs],
+        scratch_shapes=[VMEM((2, height, width), f32)],
         compiler_params=params(),
         cost_estimate=cost(100000, 700000),
         name="pack_rows",
     )(nest_old, nest_old, nest_source, nest_source, parent_old, parent_old, packed[0], *columns)
-    before = shifted(up, along, 1)
-    after = shifted(down, along, -1)
+    across = swapped(across, 1)
+    within = swapped(within, 0)
     beyond = shifted(far, along, -2)
     nest_new, coarse = pl.pallas_call(
         functools.partial(nest_steps, parts, parent_cols),
@@ -526,6 +556,7 @@
             VMEM((levels, ring, LANES), f32),
             VMEM((levels, rows, cols), f32),
             VMEM((levels * rows, foot), f32),
+            VMEM((2, height, width), f32),
             pltpu.SemaphoreType.DMA((3,)),
         ],
         compiler_params=params(),
@@ -538,8 +569,8 @@
         nest_old,
         nest_source,
         strips,
-        before,
-        after,
+        within,
+        across,
         beyond,
         columns[0],
         columns[-1],
@@ -553,10 +584,11 @@
         out_shape=shape(parent_old.shape, f32),
         in_specs=[scalars()] + [whole()] * 6,
         out_specs=whole(),
+        scratch_shapes=[VMEM((2, levels, parent_cols), f32)],
         compiler_params=params(),
         cost_estimate=cost(800000, 800000),
         name="parent_step",
-    )(parent_coefs, parent_old, parent_source, before, after, columns[0], columns[-1])
+    )(parent_coefs, parent_old, parent_source, within, across, columns[0], columns[-1])
     parent_new = pl.pallas_call(
         functools.partial(merge, parts, band),
         out_shape=shape(parent_old.shape, f32),
@@ -568,6 +600,15 @@
         name="merge",
     )(offset_x, offset_y, step, *own, *previous)
     return (parent_new, nest_new)
+
+
+def swapped(value, first):
+    along = ("gx", "gz")
+    count = lax.axis_size(along)
+    pairs = []
+    for at in range(first, count, 2):
+        pairs += [(at, (at + 1) % count), ((at + 1) % count, at)]
+    return lax.ppermute(value, along, pairs)
 
 
 def shifted_both(value, steps):

time: 34.2 us -> 34.6 us (1.012)
  Pallas kernels: 8.3 us -> 8.87 us
    ppermute x0 -> x2, starting transfers between devices: none -> 4.3 us  [swapped(): return lax.ppermute(value, along, pairs)]
    ppermute x6 -> x4, starting transfers between devices: 8.84 us -> 5.07 us  [shifted(): return lax.ppermute(value, axis, pairs)]
    pallas_call x1, Pallas kernels: 0.48 us -> 1.01 us  [shards(): pl.pallas_call(functools.partial(pack_columns, parts, band), out_shape=me...]
    ppermute x1, starting transfers between devices: 0.54 us -> 0.06 us  [shifted_both(): return lax.ppermute(value, ('gx', 'gy', 'gz'), pairs)]
    ppermute x6 -> x4, waiting for transfers between devices: 5.7 us -> 5.39 us  [shifted(): return lax.ppermute(value, axis, pairs)]
  transfers between devices with their start and end apart: 7 -> 7, of which waited for: 5 -> 4; matrix products, arithmetic and copies ran while one was open for 0% -> 0% of each run, Pallas kernels for 2% -> 2%
where the time goes in v2:
time: 34.6 us; the launch traced here: 34.3 us
  waiting for transfers between devices  9.79 us (28%)
  starting transfers between devices  9.43 us (27%)
  Pallas kernels  8.87 us (26%)
  local copies, waits for them, and re-layouts  4.2 us (12%)
  between operations  2.04 us (6%)
    pallas_call x1, Pallas kernels, shards(): pl.pallas_call(functools.partial(nest_steps, parts, parent_cols), out_sha...  6.11 us
    ppermute x4, waiting for transfers between devices, shifted(): return lax.ppermute(value, axis, pairs)  5.39 us
    ppermute x4, starting transfers between devices, shifted(): return lax.ppermute(value, axis, pairs)  5.07 us
    ppermute x1, waiting for transfers between devices, shifted_both(): return lax.ppermute(value, ('gx', 'gy', 'gz'), pairs)  4.4 us
    ppermute x2, starting transfers between devices, swapped(): return lax.ppermute(value, along, pairs)  4.3 us
    unnamed x16, local copies, waits for them, and re-layouts  4.2 us
    pallas_call x1, Pallas kernels, shards(): pl.pallas_call(functools.partial(pack_columns, parts, band), out_shape=me...  1.01 us
    pallas_call x1, Pallas kernels, shards(): pl.pallas_call(functools.partial(merge, parts, band), out_shape=shape(par...  0.82 us
  transfers between devices with their start and end apart: 7, of which 4 were waited for; matrix products, arithmetic and copies ran while one was open for 0% of the time, Pallas kernels for 2%

profile of v2, /device:TPU:0, one launch (start us, length us, event | category | flops | bytes accessed | tf_op | source)
XLA Modules:
  0.0 34.3 jit_solution(14829205127320239410)
XLA Ops:
  1.3 0.0 copy-start
  1.3 1.2 %copy-done = f32[8,72,384]{2,1,0:T(8,128)S(1)} copy-done((f32[8,72,384]{2,1,0:T(8,128)S(1)}, f32[8,72,384]{2,1,0:T(8,128)}, u32[]{:S(2)}) %copy-start) | copy-done | bytes 884760
  2.4 0.0 copy-start.1
  2.4 1.2 %copy-done.1 = f32[8,72,384]{2,1,0:T(8,128)S(1)} copy-done((f32[8,72,384]{2,1,0:T(8,128)S(1)}, f32[8,72,384]{2,1,0:T(8,128)}, u32[]{:S(2)}) %copy-start.1) | copy-done | bytes 884760
  3.6 0.0 copy-start.2
  3.6 0.9 %copy-done.2 = f32[8,24,256]{2,1,0:T(8,128)S(1)} copy-done((f32[8,24,256]{2,1,0:T(8,128)S(1)}, f32[8,24,256]{2,1,0:T(8,128)}, u32[]{:S(2)}) %copy-start.2) | copy-done | bytes 196632
  4.5 0.0 copy-start.4
  4.5 0.9 %copy-done.4 = f32[8,24,256]{2,1,0:T(8,128)S(1)} copy-done((f32[8,24,256]{2,1,0:T(8,128)S(1)}, f32[8,24,256]{2,1,0:T(8,128)}, u32[]{:S(2)}) %copy-start.4) | copy-done | bytes 196632
  5.5 1.0 %pack_columns.1 = (f32[24,128]{1,0:T(8,128)S(1)}, f32[72,128]{1,0:T(8,128)S(1)}) custom-call(s32[1]{0:T(128)S(6)} %copy.11.oy_hbm.oy_ref, f32[8,72,384]{2,1,0:T(8,128)S(1)} %copy-done, f32[8,72,384]{2,1,0:T(8,128)S(1)} %copy-done.1, f32[8,24,256]{2,1,0:T(8,128)S(1)} %copy-done.2, f32[8,24,256]{2,1,0:T(8,128)S(1)} %copy-done.4), custom_call_target="tpu_custom_call" | custom-call | flops 200000 | bytes 1000000 | tf_op jit(solution)/shard_map/pack_columns/pallas_call | solution.py:486
  6.5 3.0 %collective-permute-start = (f32[72,128]{1,0:T(8,128)S(1)}, f32[72,128]{1,0:T(8,128)S(1)}, u32[]{:S(2)}, u32[]{:S(2)}) collective-permute-start(f32[72,128]{1,0:T(8,128)S(1)} %get-tuple-element.11), channel_id=1, source_target_pairs={{0,2},{2,0},{1,3},{3,1},{4,6},{6,4},{5,7},{7,5},{8,10},{10,8},{9,1... | collective-permute-start | bytes 110600 | tf_op jit(solution)/shard_map/ppermute | solution.py:463
  9.5 1.9 %collective-permute-done.rest_0_.y_left.y_right = f32[72,128]{1,0:T(8,128)S(1)} collective-permute-done((f32[72,128]{1,0:T(8,128)S(1)}, f32[72,128]{1,0:T(8,128)S(1)}, u32[]{:S(2)}, u32[]{:S(2)}) %collective-permute-start) | collective-permute-done | bytes 36896 | tf_op jit(solution)/shard_map/ppermute | solution.py:463
  11.4 0.1 pack_rows.1
  11.6 0.1 collective-permute-start.1
  11.6 4.2 %collective-permute-start.2 = (f32[56,384]{1,0:T(8,128)S(1)}, f32[56,384]{1,0:T(8,128)S(1)}, u32[]{:S(2)}, u32[]{:S(2)}) collective-permute-start(f32[56,384]{1,0:T(8,128)S(1)} %get-tuple-element.13), channel_id=1, source_target_pairs={{1,4},{4,1},{5,8},{8,5},{9,12},{12,9},{13,0},{0,13},{3,6},{6,3},{7... | collective-permute-start | bytes 258056 | tf_op jit(solution)/shard_map/ppermute | solution.py:611
  15.9 0.4 %collective-permute-start.3 = (f32[8,128]{1,0:T(8,128)S(1)}, f32[8,128]{1,0:T(8,128)S(1)}, u32[]{:S(2)}, u32[]{:S(2)}) collective-permute-start(f32[8,128]{1,0:T(8,128)S(1)} %get-tuple-element.15), channel_id=1, source_target_pairs={{0,12},{1,13},{4,0},{5,1},{8,4},{9,5},{12,8},{13,9},{2,14},{3,15},... | collective-permute-start | bytes 12296 | tf_op jit(solution)/shard_map/ppermute | solution.py:463
  16.3 0.0 copy-start.7
  17.0 0.0 copy-start.6
  17.0 2.5 %collective-permute-done.3.beyond = f32[8,128]{1,0:T(8,128)S(1)} collective-permute-done((f32[8,128]{1,0:T(8,128)S(1)}, f32[8,128]{1,0:T(8,128)S(1)}, u32[]{:S(2)}, u32[]{:S(2)}) %collective-permute-start.3) | collective-permute-done | bytes 4128 | tf_op jit(solution)/shard_map/ppermute | solution.py:463
  19.5 0.0 collective-permute-done.1.within
  19.5 0.0 collective-permute-done.2.across
  19.5 0.0 copy-done.7
  19.5 0.0 copy-done.6
  19.5 0.0 copy-start.3
  19.5 0.0 copy-start.5
  19.5 6.1 %nest_steps.1 = (f32[8,72,384]{2,1,0:T(8,128)}, f32[8,24,128]{2,1,0:T(8,128)S(1)}) custom-call(s32[1]{0:T(128)S(6)} %copy.10.ox_ref, f32[2,8]{1,0:T(2,128)S(1)} %copy-done.6, f32[2,8]{1,0:T(2,128)S(1)} %copy-done.7, f32[8,72,384]{2,1,0:T(8,128)S(1)} %copy-done, f32[8,72,384]{2,1,0:T(8,128)S(1)} %copy-done.1, f32[24,128]{1,0:T(8,128)S(1)} %get-tuple-element.14.strips, ...), custom_call_target="tpu_custom_call" | custom-call | flops 10000000 | bytes 3000000 | tf_op jit(solution)/shard_map/nest_steps/pallas_call | solution.py:543
  25.6 0.1 collective-permute-start.6
  25.7 0.9 %collective-permute-start.5 = (f32[8,24,128]{2,1,0:T(8,128)S(1)}, f32[8,24,128]{2,1,0:T(8,128)S(1)}, u32[]{:S(2)}, u32[]{:S(2)}) collective-permute-start(f32[8,24,128]{2,1,0:T(8,128)S(1)} %get-tuple-element.16.rest_0_), channel_id=1, source_target_pairs={{0,1},{1,4},{4,5},{5,8},{8,9},{9,12},{12,13},{13,0},{2,3},{3,6},{6... | collective-permute-start | bytes 294920 | tf_op jit(solution)/shard_map/ppermute | solution.py:463
  26.6 0.7 %collective-permute-start.4 = (f32[8,24,128]{2,1,0:T(8,128)S(1)}, f32[8,24,128]{2,1,0:T(8,128)S(1)}, u32[]{:S(2)}, u32[]{:S(2)}) collective-permute-start(f32[8,24,128]{2,1,0:T(8,128)S(1)} %get-tuple-element.16.rest_0_), channel_id=1, source_target_pairs={{0,2},{2,0},{1,3},{3,1},{4,6},{6,4},{5,7},{7,5},{8,10},{10,8},{9,1... | collective-permute-start | bytes 294920 | tf_op jit(solution)/shard_map/ppermute | solution.py:463
  27.3 0.0 copy-done.3
  27.3 0.0 copy-done.5
  27.3 0.8 %parent_step.1.step = f32[8,24,256]{2,1,0:T(8,128)S(1)} custom-call(f32[2,8]{1,0:T(2,128)S(1)} %copy-done.6, f32[8,24,256]{2,1,0:T(8,128)S(1)} %copy-done.3, f32[8,24,256]{2,1,0:T(8,128)S(1)} %copy-done.5, f32[56,384]{1,0:T(8,128)S(1)} %collective-permute-done.1.within, f32[56,384]{1,0:T(8,128)S(1)} %collective-permute-done.2.across, ...), custom_call_target="tpu_custom_call" | custom-call | flops 800000 | bytes 800000 | tf_op jit(solution)/shard_map/parent_step/pallas_call | solution.py:582
  28.1 4.4 %collective-permute-done.6.rest_3_ = f32[8,24,128]{2,1,0:T(8,128)S(1)} collective-permute-done((f32[8,24,128]{2,1,0:T(8,128)S(1)}, f32[8,24,128]{2,1,0:T(8,128)S(1)}, u32[]{:S(2)}, u32[]{:S(2)}) %collective-permute-start.6) | collective-permute-done | bytes 98336 | tf_op jit(solution)/shard_map/ppermute | solution.py:624
  32.5 1.0 %collective-permute-done.5.rest_2_ = f32[8,24,128]{2,1,0:T(8,128)S(1)} collective-permute-done((f32[8,24,128]{2,1,0:T(8,128)S(1)}, f32[8,24,128]{2,1,0:T(8,128)S(1)}, u32[]{:S(2)}, u32[]{:S(2)}) %collective-permute-start.5) | collective-permute-done | bytes 98336 | tf_op jit(solution)/shard_map/ppermute | solution.py:463
  33.5 0.0 collective-permute-done.4.rest_1_
  33.5 0.8 %merge.1 = f32[8,24,256]{2,1,0:T(8,128)} custom-call(s32[1]{0:T(128)S(6)} %copy.10.ox_ref, s32[1]{0:T(128)S(6)} %copy.11.oy_hbm.oy_ref, f32[8,24,256]{2,1,0:T(8,128)S(1)} %parent_step.1.step, f32[8,24,128]{2,1,0:T(8,128)S(1)} %get-tuple-element.16.rest_0_, f32[8,24,128]{2,1,0:T(8,128)S(1)} %collective-permute-done.4.rest_1_, ...), custom_call_target="tpu_custom_call" | custom-call | flops 200000 | bytes 800000 | tf_op jit(solution)/shard_map/merge/pallas_call | solution.py:592
Async XLA Ops:
  1.3 1.2 %copy-start = (f32[8,72,384]{2,1,0:T(8,128)S(1)}, f32[8,72,384]{2,1,0:T(8,128)}, u32[]{:S(2)}) copy-start(f32[8,72,384]{2,1,0:T(8,128)} %nest.3) | copy-start | bytes 2654212
  2.4 1.2 %copy-start.1 = (f32[8,72,384]{2,1,0:T(8,128)S(1)}, f32[8,72,384]{2,1,0:T(8,128)}, u32[]{:S(2)}) copy-start(f32[8,72,384]{2,1,0:T(8,128)} %source.5) | copy-start | bytes 2654212
  3.6 0.9 %copy-start.2 = (f32[8,24,256]{2,1,0:T(8,128)S(1)}, f32[8,24,256]{2,1,0:T(8,128)}, u32[]{:S(2)}) copy-start(f32[8,24,256]{2,1,0:T(8,128)} %parent.1) | copy-start | bytes 589828
  4.5 0.9 %copy-start.4 = (f32[8,24,256]{2,1,0:T(8,128)S(1)}, f32[8,24,256]{2,1,0:T(8,128)}, u32[]{:S(2)}) copy-start(f32[8,24,256]{2,1,0:T(8,128)} %source.4) | copy-start | bytes 589828
  6.5 4.9 %collective-permute-start = (f32[72,128]{1,0:T(8,128)S(1)}, f32[72,128]{1,0:T(8,128)S(1)}, u32[]{:S(2)}, u32[]{:S(2)}) collective-permute-start(f32[72,128]{1,0:T(8,128)S(1)} %get-tuple-element.11), channel_id=1, source_target_pairs={{0,2},{2,0},{1,3},{3,1},{4,6},{6,4},{5,7},{7,5},{8,10},{10,8},{9,1... | collective-permute-start | bytes 110600 | tf_op jit(solution)/shard_map/ppermute | solution.py:463
  11.6 7.9 %collective-permute-start.1 = (f32[56,384]{1,0:T(8,128)S(1)}, f32[56,384]{1,0:T(8,128)S(1)}, u32[]{:S(2)}, u32[]{:S(2)}) collective-permute-start(f32[56,384]{1,0:T(8,128)S(1)} %get-tuple-element.12), channel_id=1, source_target_pairs={{0,1},{1,0},{4,5},{5,4},{8,9},{9,8},{12,13},{13,12},{2,3},{3,2},{6... | collective-permute-start | bytes 258056 | tf_op jit(solution)/shard_map/ppermute | solution.py:611
  11.6 7.8 %collective-permute-start.2 = (f32[56,384]{1,0:T(8,128)S(1)}, f32[56,384]{1,0:T(8,128)S(1)}, u32[]{:S(2)}, u32[]{:S(2)}) collective-permute-start(f32[56,384]{1,0:T(8,128)S(1)} %get-tuple-element.13), channel_id=1, source_target_pairs={{1,4},{4,1},{5,8},{8,5},{9,12},{12,9},{13,0},{0,13},{3,6},{6,3},{7... | collective-permute-start | bytes 258056 | tf_op jit(solution)/shard_map/ppermute | solution.py:611
  15.9 3.6 %collective-permute-start.3 = (f32[8,128]{1,0:T(8,128)S(1)}, f32[8,128]{1,0:T(8,128)S(1)}, u32[]{:S(2)}, u32[]{:S(2)}) collective-permute-start(f32[8,128]{1,0:T(8,128)S(1)} %get-tuple-element.15), channel_id=1, source_target_pairs={{0,12},{1,13},{4,0},{5,1},{8,4},{9,5},{12,8},{13,9},{2,14},{3,15},... | collective-permute-start | bytes 12296 | tf_op jit(solution)/shard_map/ppermute | solution.py:463
  16.3 3.2 %copy-start.7 = (f32[2,8]{1,0:T(2,128)S(1)}, f32[2,8]{1,0:T(2,128)}, u32[]{:S(2)}) copy-start(f32[2,8]{1,0:T(2,128)} %coefs.3) | copy-start | bytes 196
  17.0 2.5 %copy-start.6 = (f32[2,8]{1,0:T(2,128)S(1)}, f32[2,8]{1,0:T(2,128)}, u32[]{:S(2)}) copy-start(f32[2,8]{1,0:T(2,128)} %parent_coefs.1) | copy-start | bytes 196
  19.5 7.8 %copy-start.3 = (f32[8,24,256]{2,1,0:T(8,128)S(1)}, f32[8,24,256]{2,1,0:T(8,128)}, u32[]{:S(2)}) copy-start(f32[8,24,256]{2,1,0:T(8,128)} %parent.1) | copy-start | bytes 589828
  19.5 7.8 %copy-start.5 = (f32[8,24,256]{2,1,0:T(8,128)S(1)}, f32[8,24,256]{2,1,0:T(8,128)}, u32[]{:S(2)}) copy-start(f32[8,24,256]{2,1,0:T(8,128)} %source.4) | copy-start | bytes 589828
  25.6 6.9 %collective-permute-start.6 = (f32[8,24,128]{2,1,0:T(8,128)S(1)}, f32[8,24,128]{2,1,0:T(8,128)S(1)}, u32[]{:S(2)}, u32[]{:S(2)}) collective-permute-start(f32[8,24,128]{2,1,0:T(8,128)S(1)} %get-tuple-element.16.rest_0_), channel_id=1, source_target_pairs={{0,3},{1,6},{2,1},{3,4},{4,7},{5,10},{6,5},{7,8},{8,11},{9,14},{10... | collective-permute-start | bytes 294920 | tf_op jit(solution)/shard_map/ppermute | solution.py:624
  25.7 7.8 %collective-permute-start.5 = (f32[8,24,128]{2,1,0:T(8,128)S(1)}, f32[8,24,128]{2,1,0:T(8,128)S(1)}, u32[]{:S(2)}, u32[]{:S(2)}) collective-permute-start(f32[8,24,128]{2,1,0:T(8,128)S(1)} %get-tuple-element.16.rest_0_), channel_id=1, source_target_pairs={{0,1},{1,4},{4,5},{5,8},{8,9},{9,12},{12,13},{13,0},{2,3},{3,6},{6... | collective-permute-start | bytes 294920 | tf_op jit(solution)/shard_map/ppermute | solution.py:463
  26.6 6.9 %collective-permute-start.4 = (f32[8,24,128]{2,1,0:T(8,128)S(1)}, f32[8,24,128]{2,1,0:T(8,128)S(1)}, u32[]{:S(2)}, u32[]{:S(2)}) collective-permute-start(f32[8,24,128]{2,1,0:T(8,128)S(1)} %get-tuple-element.16.rest_0_), channel_id=1, source_target_pairs={{0,2},{2,0},{1,3},{3,1},{4,6},{6,4},{5,7},{7,5},{8,10},{10,8},{9,1... | collective-permute-start | bytes 294920 | tf_op jit(solution)/shard_map/ppermute | solution.py:463

commit v3 on v2

v3 whole, which is shorter than its diff:
```python
import functools

import jax
import jax.numpy as jnp
from jax import lax
from jax.experimental import pallas as pl
from jax.experimental.pallas import tpu as pltpu
from jax.sharding import PartitionSpec as P

RATIO = 3
SUBSTEPS = 3
RIM = 6
LANES = 128
STRIDE = 16
SOURCE_AT = 3
PARENT_AT = 6
STRIP_AT = 8
STRIP_SOURCE_AT = 12
SOURCE_ROW = 24
TAIL_ROW = 40
FIXED = 8
LEFT_AT = 3
RIGHT_OWN = STRIDE - 3
VMEM = pltpu.VMEM
LIMIT = 24 * 1024 * 1024
MOST = 54 * 1024 * 1024
HIGHEST = lax.Precision.HIGHEST


def iota(shape, dim):
    return lax.broadcasted_iota(jnp.int32, shape, dim)


def whole():
    return pl.BlockSpec(memory_space=VMEM)


def scalars():
    return pl.BlockSpec(memory_space=pltpu.SMEM)


def params(limit=LIMIT):
    return pltpu.CompilerParams(vmem_limit_bytes=limit)


def cost(flops, moved):
    return pl.CostEstimate(flops=flops, bytes_accessed=moved, transcendentals=0)


def tile(ref, level, index):
    return ref[level, :, index * LANES : (index + 1) * LANES]


def turned(value, lanes):
    lanes = lanes % LANES
    return pltpu.roll(value, lanes, 1) if lanes else value


def edge_strip(dest, band, oy, parent, parent_source):
    levels, rows, cols = parent.shape
    lane = iota((rows, LANES), 1)
    base = jnp.where(dest == 0, oy - 1, oy + band - 3) - lax.axis_index("gy") * cols
    total = jnp.zeros(lane.shape, jnp.float32)
    for ref, first in ((parent, STRIP_AT), (parent_source, STRIP_SOURCE_AT)):
        for level in range(levels):
            found = jnp.zeros(lane.shape, jnp.float32)
            for at in range(cols // LANES):
                place = lane + (at * LANES - base)
                found = jnp.where((place >= 0) & (place < 4), tile(ref, level, at), found)
            turn = (16384 + first + STRIDE * level - base) & (LANES - 1)
            total = total + pltpu.roll(found, turn, 1)
    return total


def pack_columns(parts, band, oy_hbm, nest, source, parent_hbm, parent_source_hbm, *rest):
    outs = rest[: parts - 1]
    old_buf, src_buf, parent, parent_source, oy_ref, sems, field_sems = rest[parts - 1 :]
    levels, rows, cols = nest.shape
    parent_cols = parent.shape[2]
    me = lax.axis_index("gy")
    sides = [1] if parts == 2 else [1, parts - 1]
    fields = [
        pltpu.make_async_copy(ref, buf, field_sems.at[at])
        for at, (ref, buf) in enumerate(
            ((oy_hbm, oy_ref), (parent_hbm, parent), (parent_source_hbm, parent_source))
        )
    ]
    for copy in fields:
        copy.start()
    copies = []
    for at, step in enumerate(sides):
        right = (me == 0) if parts == 2 else jnp.bool_(step == 1)
        start = pl.multiple_of(jnp.where(right, cols - LANES, 0), LANES)
        pair = [
            pltpu.make_async_copy(
                ref.at[:, :, pl.ds(start, LANES)], buf.at[at], sems.at[at, which]
            )
            for which, (ref, buf) in enumerate(((nest, old_buf), (source, src_buf)))
        ]
        for copy in pair:
            copy.start()
        copies.append((right, pair))
    for copy in fields:
        copy.wait()
    oy = oy_ref[0]
    lane = iota((parent.shape[1], LANES), 1)
    for step in range(1, parts):
        out = outs[step - 1]
        part = edge_strip(lax.rem(me + step, parts), band, oy, parent, parent_source)
        if step not in sides:
            out[...] = part
            continue
        at = sides.index(step)
        right, pair = copies[at]
        first = jnp.where(right, LANES - 3, 0)
        outer = jnp.where(right, LANES - 1, 0)
        for level in range(levels):
            edge = jnp.where(
                right, tile(parent, level, parent_cols // LANES - 1), tile(parent, level, 0)
            )
            edge = jnp.where(lane == outer, edge, 0.0)
            turn = (LANES + PARENT_AT + STRIDE * level - outer) & (LANES - 1)
            part = part + pltpu.roll(edge, turn, 1)
        for copy in pair:
            copy.wait()
        fine = iota((rows, LANES), 1) - first
        wanted = (fine >= 0) & (fine < 3)
        total = jnp.zeros((rows, LANES), jnp.float32)
        for level in range(levels):
            for buf, shift in ((old_buf, 0), (src_buf, SOURCE_AT)):
                value = jnp.where(wanted, buf[at, level], 0.0)
                turn = (LANES + STRIDE * level + shift - first) & (LANES - 1)
                total = total + pltpu.roll(value, turn, 1)
        out[...] = total
        out[: part.shape[0], :] += part


def inner_substep(coefs, here, source, there):
    levels, rows, cols = here.shape
    sub = iota((8, cols), 0)
    tiles = rows // 8

    def one_level(level):
        ch = coefs[0, level]
        cv = coefs[1, level]
        centre = 1.0 - 4.0 * ch - 2.0 * cv
        below = jnp.maximum(level - 1, 0)
        above = jnp.minimum(level + 1, levels - 1)
        cv_below = jnp.where(level > 0, cv, 0.0)
        cv_above = jnp.where(level < levels - 1, cv, 0.0)

        def row_tile(t):
            t = t % tiles
            return here[level, 8 * t : 8 * t + 8, :]

        down_before = pltpu.roll(row_tile(-1), 1, 0)
        now = row_tile(0)
        up_now = pltpu.roll(now, 7, 0)
        for t in range(tiles):
            following = row_tile(t + 1)
            down_now = pltpu.roll(now, 1, 0)
            up_next = pltpu.roll(following, 7, 0)
            around = jnp.where(sub == 0, down_before, down_now) + jnp.where(
                sub == 7, up_next, up_now
            )
            around = around + (pltpu.roll(now, 1, 1) + pltpu.roll(now, cols - 1, 1))
            span = slice(8 * t, 8 * t + 8)
            stacked = cv_below * here[below, span, :] + cv_above * here[above, span, :]
            there[level, span, :] = centre * now + ch * around + (stacked + source[level, span, :])
            down_before, now, up_now = down_now, following, up_next

    def two_levels(pair, carry):
        one_level(2 * pair)
        one_level(2 * pair + 1)
        return carry

    lax.fori_loop(0, levels // 2, two_levels, 0)


def inner_first(
    band, oy_ref, coefs, nest, source, parent, parent_source, strip, first, packs
):
    levels, rows, cols = nest.shape
    strip[...] = edge_strip(lax.axis_index("gy"), band, oy_ref[0], parent, parent_source)
    lane = iota((rows, LANES), 1)
    for at, ref in enumerate((nest, source)):
        left = jnp.zeros(lane.shape, jnp.float32)
        right = jnp.zeros(lane.shape, jnp.float32)
        for level in range(levels):
            value = jnp.where(lane < RIGHT_OWN, tile(ref, level, 0), 0.0)
            left = left + turned(value, STRIDE * level + LEFT_AT)
            value = jnp.where(lane >= LANES - RIGHT_OWN, tile(ref, level, cols // LANES - 1), 0.0)
            right = right + turned(value, STRIDE * level + RIGHT_OWN)
        packs[2 * at] = left
        packs[2 * at + 1] = right
    inner_substep(coefs, nest, source, first)


def inner_rest(coefs, first, source, after_pack, third, second):
    inner_substep(coefs, first, source, second)
    inner_substep(coefs, second, source, third)


def with_columns(tiles, left, right, me, parts, place):
    lane = iota(left.shape, 1)
    from_right = turned(right, -place)
    from_left = turned(left, -3 - place)
    if parts == 2:
        tiles[0] = jnp.where((lane < 3) & (me == 0), from_right, tiles[0])
        tiles[-1] = jnp.where((lane >= LANES - 3) & (me == 1), from_left, tiles[-1])
        return tiles
    extra = jnp.where(lane < 3, from_right, jnp.where(lane >= LANES - 3, from_left, 0.0))
    return tiles + [extra]


def pack_rows(
    parts, old_top, old_end, src_top, src_end, par_top, par_end, own_strip, *rest
):
    columns = rest[: parts - 1]
    within, across, far, strip_out, both = rest[parts - 1 :]
    core = lax.axis_index("gz")
    up, down = both.at[core], both.at[1 - core]
    levels, _, cols = old_top.shape
    me = lax.axis_index("gy")
    left, right = columns[0], columns[-1]
    rows = left.shape[0]
    strip_rows = own_strip.shape[0]
    lane = iota((strip_rows, LANES), 1)
    strips = own_strip[...]
    for message in columns:
        strips = strips + message[:strip_rows, :]
    strips = jnp.where((lane & (STRIDE - 1)) >= STRIP_AT, strips, 0.0)
    strip_out[...] = strips
    far[...] = strips[:8]
    pieces = cols // LANES
    for out, old, src, first, at, src_at in (
        (up, old_end, src_end, rows - 8, 5, 6),
        (down, old_top, src_top, 0, 0, 0),
    ):
        y_left = left[first : first + 8, :]
        y_right = right[first : first + 8, :]
        for level in range(levels):
            for ref, shift, row, count, base in (
                (old, 0, at, 3, 0),
                (src, SOURCE_AT, src_at, 2, SOURCE_ROW),
            ):
                tiles = [tile(ref, level, piece) for piece in range(pieces)]
                tiles = with_columns(
                    tiles, y_left, y_right, me, parts, STRIDE * level + shift
                )
                for piece, value in enumerate(tiles):
                    out[
                        base + count * level : base + count * (level + 1),
                        piece * LANES : (piece + 1) * LANES,
                    ] = value[row : row + count]
    parent_cols = par_top.shape[2]
    for level in range(levels):
        up[TAIL_ROW + level : TAIL_ROW + level + 1, :parent_cols] = par_end[level, 7:8, :]
        down[TAIL_ROW + level : TAIL_ROW + level + 1, :parent_cols] = par_top[level, 0:1, :]
    up[TAIL_ROW : TAIL_ROW + 8, parent_cols : parent_cols + LANES] = strips[strip_rows - 8 :]
    down[TAIL_ROW : TAIL_ROW + 8, parent_cols : parent_cols + LANES] = strips[:8]
    down[TAIL_ROW + 8 : TAIL_ROW + 16, :LANES] = strips[8:16]
    down[TAIL_ROW + 8 : TAIL_ROW + 16, LANES : 2 * LANES] = strips[16:24]
    within[...] = both[0]
    across[...] = both[1]


def edges(
    parts,
    parent_cols,
    ox_ref,
    parent_coefs,
    coefs,
    nest,
    source,
    third,
    packs,
    strips,
    within,
    across,
    beyond,
    y_left,
    y_right,
    result,
    coarse_out,
    both,
    ping,
    pong,
    src,
    split,
):
    levels, rows, cols = nest.shape
    width = ping.shape[3]
    pieces = cols // LANES
    me = lax.axis_index("gy")
    core = lax.axis_index("gz")
    both[0] = within[...]
    both[1] = across[...]
    before, after = both.at[1 - core], both.at[core]
    ox = ox_ref[0]
    is_south = me == 0
    is_north = me == parts - 1

    sub = iota((8, LANES), 0)
    old = jnp.concatenate(
        [
            strips[...],
            after[TAIL_ROW : TAIL_ROW + 8, parent_cols : parent_cols + LANES],
            after[TAIL_ROW + 8 : TAIL_ROW + 16, :LANES],
            after[TAIL_ROW + 8 : TAIL_ROW + 16, LANES : 2 * LANES],
            jnp.where(
                sub == 0,
                beyond[...],
                jnp.where(
                    sub == 7,
                    before[TAIL_ROW : TAIL_ROW + 8, parent_cols : parent_cols + LANES],
                    0.0,
                ),
            ),
        ],
        axis=0,
    )
    count = old.shape[0]

    def per_level(ref, which, shape):
        lane = iota(shape, 1)
        total = jnp.full(shape, ref[which, 0], jnp.float32)
        for level in range(1, levels):
            total = jnp.where(lane >= STRIDE * level, ref[which, level], total)
        return total

    def stacked(value):
        lane = iota(value.shape, 1)
        below = jnp.where(lane >= STRIDE, turned(value, STRIDE), 0.0)
        return below + jnp.where(lane < STRIDE * (levels - 1), turned(value, -STRIDE), 0.0)

    def around(value):
        return (
            pltpu.roll(value, 1, 0)
            + pltpu.roll(value, value.shape[0] - 1, 0)
            + turned(value, 1)
            + turned(value, -1)
        )

    diff = (
        per_level(parent_coefs, 0, old.shape) * (around(old) - 4.0 * old)
        + per_level(parent_coefs, 1, old.shape) * (stacked(old) - 2.0 * old)
        + turned(old, STRIP_AT - STRIP_SOURCE_AT)
    )
    index = iota((rows + 16, count), 0)
    nest_row = jnp.where(index < rows, index, jnp.where(index < rows + 8, index - rows - 3, index - 13))
    parent_row = ((nest_row + 3) * 171 >> 9) - 1 + ox
    pick = (iota((rows + 16, count), 1) == parent_row).astype(jnp.float32)
    picked = jnp.dot(
        pick,
        jnp.concatenate([old, diff], axis=1),
        precision=HIGHEST,
        preferred_element_type=jnp.float32,
    )
    picked_old, picked_diff = picked[:, :LANES], picked[:, LANES:]

    lane = iota((rows, LANES), 1)
    c = lane & (STRIDE - 1)
    rim_first = jnp.where(is_south, LEFT_AT, RIGHT_OWN - RIM)
    in_rim = (c >= rim_first) & (c < rim_first + RIM)
    at = lane - c + STRIP_AT + jnp.where(c >= rim_first + 3, 2, 1)
    rim_old = jnp.take_along_axis(picked_old[:rows], at, axis=1)
    rim_diff = jnp.take_along_axis(picked_diff[:rows], at, axis=1)
    ch = per_level(coefs, 0, lane.shape)
    cv = per_level(coefs, 1, lane.shape)
    centre = 1.0 - 4.0 * ch - 2.0 * cv
    left = jnp.where(c < 3, y_left[...], packs[0])
    left_src = jnp.where(c < 3, turned(y_left[...], -SOURCE_AT), packs[2])
    right = jnp.where(c >= RIGHT_OWN, turned(y_right[...], RIGHT_OWN), packs[1])
    right_src = jnp.where(c >= RIGHT_OWN, turned(y_right[...], RIGHT_OWN - SOURCE_AT), packs[3])
    sides = []
    for value, forcing, rim in (
        (left, left_src, in_rim & is_south),
        (right, right_src, in_rim & is_north),
    ):
        for substep in range(1, SUBSTEPS + 1):
            value = centre * value + ch * around(value) + (cv * stacked(value) + forcing)
            value = jnp.where(rim, rim_old + (substep / SUBSTEPS) * rim_diff, value)
        sides.append(value)

    sub = iota((8, width), 0)
    lane = iota((8, LANES), 1)
    for level in range(levels):
        for buf, field, shift, n, base in (
            (ping, nest, 0, 3, 0),
            (src, source, SOURCE_AT, 2, SOURCE_ROW),
        ):
            for window, first, turn, at, message in (
                (0, 0, 3, 3 - n, before),
                (1, rows - 8, 5, 5, after),
            ):
                tiles = [
                    field[level, first : first + 8, piece * LANES : (piece + 1) * LANES]
                    for piece in range(pieces)
                ]
                tiles = with_columns(
                    tiles,
                    y_left[first : first + 8, :],
                    y_right[first : first + 8, :],
                    me,
                    parts,
                    STRIDE * level + shift,
                )
                for piece, value in enumerate(tiles):
                    value = pltpu.roll(value, turn, 0)
                    span = slice(piece * LANES, (piece + 1) * LANES)
                    buf[level, window, :, span] = value
                    if n == 3:
                        pong[level, window, :, span] = value
                buf[level, window, at : at + n, :] = message[
                    base + n * level : base + n * (level + 1), :
                ]
    rim_first = jnp.where(is_south, 0, LANES - RIM)
    column = STRIP_AT + jnp.where((lane >= rim_first + 3) & (lane < rim_first + RIM), 2, 1)
    rims = {}
    for level in range(levels):
        for window in range(2):
            span = slice(rows + 8 * window, rows + 8 * window + 8)
            at = column + STRIDE * level
            rims[level, window] = (
                jnp.take_along_axis(picked_old[span], at, axis=1),
                jnp.take_along_axis(picked_diff[span], at, axis=1),
            )
    for substep in range(1, SUBSTEPS + 1):
        here, there = (ping, pong) if substep % 2 else (pong, ping)
        low = 0 if substep == SUBSTEPS or parts > 2 else 3
        south = (lane >= low) & (lane < RIM) & is_south
        north = (lane >= LANES - RIM) & (lane < LANES - low) & is_north
        weight = substep / SUBSTEPS
        for level in range(levels):
            c_h = coefs[0, level]
            c_v = coefs[1, level]
            c_0 = 1.0 - 4.0 * c_h - 2.0 * c_v
            for window in range(2):
                now = here[level, window]
                up = pltpu.roll(now, 1, 0)
                down = pltpu.roll(now, 7, 0)
                if substep == 1:
                    beyond_row = pong[level, window]
                    if window == 0:
                        down = jnp.where(sub == 7, pltpu.roll(beyond_row, 7, 0), down)
                    else:
                        up = jnp.where(sub == 0, pltpu.roll(beyond_row, 1, 0), up)
                beside = pltpu.roll(now, 1, 1) + pltpu.roll(now, width - 1, 1)
                value = c_0 * now + c_h * ((up + down) + beside) + src[level, window]
                if level > 0:
                    value = value + c_v * here[level - 1, window]
                if level < levels - 1:
                    value = value + c_v * here[level + 1, window]
                rim_o, rim_d = rims[level, window]
                rim = rim_o + weight * rim_d
                for piece in range(width // LANES):
                    span = slice(piece * LANES, (piece + 1) * LANES)
                    part = value[:, span]
                    if piece == 0:
                        part = jnp.where(south, rim, part)
                    if piece == pieces - 1:
                        part = jnp.where(north, rim, part)
                    there[level, window, :, span] = part

    lane = iota((rows, LANES), 1)
    sub = iota((8, cols), 0)
    for level in range(levels):
        fixed = turned(sides[0], -STRIDE * level - LEFT_AT)
        result[level, :, :LANES] = jnp.where(lane < FIXED, fixed, tile(third, level, 0))
        for piece in range(1, pieces - 1):
            result[level, :, piece * LANES : (piece + 1) * LANES] = tile(third, level, piece)
        fixed = turned(sides[1], -STRIDE * level - RIGHT_OWN)
        result[level, :, cols - LANES :] = jnp.where(
            lane >= LANES - FIXED, fixed, tile(third, level, pieces - 1)
        )
        top = pltpu.roll(there[level, 0, :, :cols], 5, 0)
        result[level, :8, :] = jnp.where(sub < 3, top, result[level, :8, :])
        end = pltpu.roll(there[level, 1, :, :cols], 3, 0)
        result[level, rows - 8 :, :] = jnp.where(sub >= 5, end, result[level, rows - 8 :, :])

    foot = cols // RATIO
    offset = iota((cols, foot), 0) - RATIO * iota((cols, foot), 1)
    gather = ((offset >= 0) & (offset < RATIO)).astype(jnp.float32)
    parent_rows = rows // RATIO
    for level in range(levels):
        for piece in range(pieces):
            split[piece, level * rows : (level + 1) * rows, :] = tile(result, level, piece)
    total = levels * parent_rows
    sums = [
        split[piece, pl.ds(0, total, RATIO), :]
        + split[piece, pl.ds(1, total, RATIO), :]
        + split[piece, pl.ds(2, total, RATIO), :]
        for piece in range(pieces)
    ]
    means = jnp.dot(
        jnp.concatenate(sums, axis=1),
        gather,
        precision=HIGHEST,
        preferred_element_type=jnp.float32,
    ) * (1.0 / 9.0)
    coarse_out[...] = means.reshape(coarse_out.shape)


def parent_step(
    parts, coefs, nest, parent, source, within, across, y_left, y_right, out, nest_out, tail, sem
):
    store = pltpu.make_async_copy(nest, nest_out, sem)
    store.start()
    core = lax.axis_index("gz")
    levels, rows, cols = parent.shape
    tail[0] = within[TAIL_ROW : TAIL_ROW + levels, :cols]
    tail[1] = across[TAIL_ROW : TAIL_ROW + levels, :cols]
    me = lax.axis_index("gy")
    row = iota((rows, cols), 0)
    lane = iota((rows, cols), 1)
    has_left = me > 0
    has_right = me < parts - 1
    left = y_left[:rows, :]
    right = y_right[:rows, :]
    zero = jnp.zeros((rows, cols), jnp.float32)
    for level in range(levels):
        now = parent[level]
        at = STRIDE * level + PARENT_AT
        from_left = left[:, at : at + 1]
        from_right = right[:, at : at + 1]
        top = tail[1 - core, level : level + 1, :]
        end = tail[core, level : level + 1, :]
        around = (
            jnp.where(row == 0, top, pltpu.roll(now, 1, 0))
            + jnp.where(row == rows - 1, end, pltpu.roll(now, rows - 1, 0))
            + jnp.where(
                lane == 0, jnp.where(has_left, from_left, 0.0), pltpu.roll(now, 1, 1)
            )
            + jnp.where(
                lane == cols - 1,
                jnp.where(has_right, from_right, 0.0),
                pltpu.roll(now, cols - 1, 1),
            )
        )
        stacked = (parent[level - 1] if level > 0 else zero) + (
            parent[level + 1] if level < levels - 1 else zero
        )
        ch = coefs[0, level]
        cv = coefs[1, level]
        out[level] = (
            (1.0 - 4.0 * ch - 2.0 * cv) * now + ch * around + (cv * stacked + source[level])
        )
    store.wait()


def merge(parts, band, ox_ref, oy_ref, step, *rest):
    own, previous, out, joined = (
        rest[:parts],
        rest[parts : 2 * parts],
        rest[2 * parts],
        rest[2 * parts + 1],
    )
    levels, rows, cols = step.shape
    foot = own[0].shape[2]
    me = lax.axis_index("gy")
    ox = ox_ref[0]
    oy = oy_ref[0]
    for k in range(parts):
        joined[k, :, :rows, :] = previous[k][...]
        joined[k, :, rows:, :] = own[k][...]
    lane = iota((rows, LANES), 1)
    for level in range(levels):
        values = [tile(step, level, piece) for piece in range(cols // LANES)]
        for k in range(parts):
            source = lax.rem(me + parts - k, parts)
            block = joined[k, level, pl.ds(rows - ox, rows), :]
            begin = oy + source * foot - me * cols
            block = pltpu.roll(block, (16384 + begin) & (LANES - 1), 1)
            low = jnp.maximum(source * foot, 2)
            high = jnp.minimum((source + 1) * foot, band - 2)
            for piece in range(cols // LANES):
                at = lane + (piece * LANES + me * cols - oy)
                values[piece] = jnp.where((at >= low) & (at < high), block, values[piece])
        for piece, value in enumerate(values):
            out[level, :, piece * LANES : (piece + 1) * LANES] = value


def shifted(value, axis, steps):
    count = lax.axis_size(axis)
    pairs = [(source, (source + steps) % count) for source in range(count)]
    return lax.ppermute(value, axis, pairs)


def shards(
    parent_old, parent_source, parent_coefs, nest_old, nest_source, nest_coefs, offset_x, offset_y
):
    parts = lax.axis_size("gy")
    along = ("gx", "gz")
    levels, parent_rows, parent_cols = parent_old.shape
    _, rows, cols = nest_old.shape
    foot = cols // RATIO
    band = foot * parts
    width = cols if parts == 2 else cols + LANES
    height = TAIL_ROW + 16
    f32 = jnp.float32
    shape = jax.ShapeDtypeStruct
    anywhere = pl.BlockSpec(memory_space=pl.ANY)
    in_hbm = pl.BlockSpec(memory_space=pltpu.HBM)
    sides = 1 if parts == 2 else 2
    packed = pl.pallas_call(
        functools.partial(pack_columns, parts, band),
        out_shape=[
            shape((rows if k in (1, parts - 1) else parent_rows, LANES), f32)
            for k in range(1, parts)
        ],
        in_specs=[in_hbm] * 5,
        out_specs=[whole()] * (parts - 1),
        scratch_shapes=[
            VMEM((sides, levels, rows, LANES), f32),
            VMEM((sides, levels, rows, LANES), f32),
            VMEM(parent_old.shape, f32),
            VMEM(parent_old.shape, f32),
            pltpu.SMEM(offset_y.shape, jnp.int32),
            pltpu.SemaphoreType.DMA((sides, 2)),
            pltpu.SemaphoreType.DMA((3,)),
        ],
        compiler_params=params(MOST),
        cost_estimate=cost(200000, 1000000),
        name="pack_columns",
    )(offset_y, nest_old, nest_source, parent_old, parent_source)
    columns = [shifted(packed[k - 1], "gy", k) for k in range(1, parts)]
    own_strip, first, packs = pl.pallas_call(
        functools.partial(inner_first, band),
        out_shape=[
            shape((parent_rows, LANES), f32),
            shape(nest_old.shape, f32),
            shape((4, rows, LANES), f32),
        ],
        in_specs=[scalars()] * 2 + [whole()] * 4,
        out_specs=[whole()] * 3,
        compiler_params=params(),
        cost_estimate=cost(4000000, 3000000),
        name="inner_first",
    )(offset_y, nest_coefs, nest_old, nest_source, parent_old, parent_source)

    def block(ref, last):
        count = ref.shape[1] // 8 - 1 if last else 0
        return pl.BlockSpec((levels, 8, ref.shape[2]), lambda i, c=count: (0, c, 0))

    def full(extent):
        return pl.BlockSpec(extent, lambda i: (0,) * len(extent))

    outs = [
        shape((height, width), f32),
        shape((height, width), f32),
        shape((8, LANES), f32),
        shape((parent_rows, LANES), f32),
    ]
    within, across, far, strips = pl.pallas_call(
        functools.partial(pack_rows, parts),
        out_shape=outs,
        grid=(1,),
        in_specs=[
            block(nest_old, False),
            block(nest_old, True),
            block(nest_old, False),
            block(nest_old, True),
            block(parent_old, False),
            block(parent_old, True),
            full(own_strip.shape),
        ]
        + [full(message.shape) for message in columns],
        out_specs=[full(out.shape) for out in outs],
        scratch_shapes=[VMEM((2, height, width), f32)],
        compiler_params=params(),
        cost_estimate=cost(100000, 700000),
        name="pack_rows",
    )(nest_old, nest_old, nest_source, nest_source, parent_old, parent_old, own_strip, *columns)
    across = swapped(across, 1)
    within = swapped(within, 0)
    beyond = shifted(far, along, -2)
    third = pl.pallas_call(
        inner_rest,
        out_shape=shape(nest_old.shape, f32),
        in_specs=[scalars()] + [whole()] * 2 + [anywhere],
        out_specs=whole(),
        scratch_shapes=[VMEM(nest_old.shape, f32)],
        compiler_params=params(),
        cost_estimate=cost(8000000, 6000000),
        name="inner_rest",
    )(nest_coefs, first, nest_source, strips)
    nest_done, coarse = pl.pallas_call(
        functools.partial(edges, parts, parent_cols),
        out_shape=[
            shape(nest_old.shape, f32),
            shape((levels, parent_rows, foot), f32),
        ],
        in_specs=[scalars()] * 3 + [whole()] * 10,
        out_specs=[whole(), whole()],
        scratch_shapes=[
            VMEM((2, height, width), f32),
            VMEM((levels, 2, 8, width), f32),
            VMEM((levels, 2, 8, width), f32),
            VMEM((levels, 2, 8, width), f32),
            VMEM((cols // LANES, levels * rows, LANES), f32),
        ],
        compiler_params=params(),
        cost_estimate=cost(4000000, 3000000),
        name="edges",
    )(
        offset_x,
        parent_coefs,
        nest_coefs,
        nest_old,
        nest_source,
        third,
        packs,
        strips,
        within,
        across,
        beyond,
        columns[0],
        columns[-1],
    )
    own = [coarse] + [shifted(coarse, "gy", k) for k in range(1, parts)]
    previous = [shifted(coarse, along, 1)] + [
        shifted_both(coarse, k) for k in range(1, parts)
    ]
    step, nest_new = pl.pallas_call(
        functools.partial(parent_step, parts),
        out_shape=[shape(parent_old.shape, f32), shape(nest_old.shape, f32)],
        in_specs=[scalars(), anywhere] + [whole()] * 6,
        out_specs=[whole(), in_hbm],
        scratch_shapes=[VMEM((2, levels, parent_cols), f32), pltpu.SemaphoreType.DMA],
        compiler_params=params(),
        cost_estimate=cost(800000, 2500000),
        name="parent_step",
    )(
        parent_coefs,
        nest_done,
        parent_old,
        parent_source,
        within,
        across,
        columns[0],
        columns[-1],
    )
    parent_new = pl.pallas_call(
        functools.partial(merge, parts, band),
        out_shape=shape(parent_old.shape, f32),
        in_specs=[scalars()] * 2 + [whole()] * (1 + 2 * parts),
        out_specs=whole(),
        scratch_shapes=[VMEM((parts, levels, 2 * parent_rows, foot), f32)],
        compiler_params=params(),
        cost_estimate=cost(200000, 800000),
        name="merge",
    )(offset_x, offset_y, step, *own, *previous)
    return (parent_new, nest_new)


def swapped(value, first):
    along = ("gx", "gz")
    count = lax.axis_size(along)
    pairs = []
    for at in range(first, count, 2):
        pairs += [(at, (at + 1) % count), ((at + 1) % count, at)]
    return lax.ppermute(value, along, pairs)


def shifted_both(value, steps):
    sizes = [lax.axis_size(axis) for axis in ("gx", "gy", "gz")]
    gx, gy, gz = sizes
    pairs = []
    for x in range(gx):
        for y in range(gy):
            for z in range(gz):
                place = (x * gz + z + 1) % (gx * gz)
                target = (place // gz * gy + (y + steps) % gy) * gz + place % gz
                pairs.append(((x * gy + y) * gz + z, target))
    return lax.ppermute(value, ("gx", "gy", "gz"), pairs)


def solution(mesh):
    return jax.shard_map(
        shards,
        mesh=mesh,
        in_specs=(
            P(None, ("grp", "gx", "gz"), "gy"),
            P(None, ("grp", "gx", "gz"), "gy"),
            P(),
            P(None, ("grp", "gx", "gz"), "gy"),
            P(None, ("grp", "gx", "gz"), "gy"),
            P(),
            P("grp"),
            P("grp"),
        ),
        out_specs=(P(None, ("grp", "gx", "gz"), "gy"), P(None, ("grp", "gx", "gz"), "gy")),
        check_vma=False,
    )
```

time: 34.6 us -> 28.7 us (0.83)
  waiting for transfers between devices: 9.79 us -> 4.26 us
  local copies, waits for them, and re-layouts: 4.2 us -> 0.37 us
  Pallas kernels: 8.87 us -> 10.9 us
  starting transfers between devices: 9.43 us -> 11 us
    unnamed x16 -> x12, local copies, waits for them, and re-layouts: 4.2 us -> 0.37 us
    ppermute x4, waiting for transfers between devices: 5.39 us -> 2.15 us  [shifted(): return lax.ppermute(value, axis, pairs)]
    ppermute x1, waiting for transfers between devices: 4.4 us -> 2.1 us  [shifted_both(): return lax.ppermute(value, ('gx', 'gy', 'gz'), pairs)]
    pallas_call x3 -> x5, Pallas kernels: 7.92 us -> 9.91 us  [the longest x1 2.27 us: shards(): pl.pallas_call(functools.partial(pack_columns, parts, band), out_shape=[s...]
    ppermute x1, starting transfers between devices: 0.06 us -> 0.85 us  [shifted_both(): return lax.ppermute(value, ('gx', 'gy', 'gz'), pairs)]
    ppermute x4, starting transfers between devices: 5.07 us -> 5.81 us  [shifted(): return lax.ppermute(value, axis, pairs)]
  transfers between devices with their start and end apart: 7 -> 7, of which waited for: 4 -> 5; matrix products, arithmetic and copies ran while one was open for 0% -> 0% of each run, Pallas kernels for 2% -> 20%
where the time goes in v3:
time: 28.7 us; the launch traced here: 28.5 us
  starting transfers between devices  11 us (38%)
  Pallas kernels  10.9 us (38%)
  waiting for transfers between devices  4.26 us (15%)
  between operations  2.05 us (7%)
  local copies, waits for them, and re-layouts  0.37 us (1%)
    ppermute x4, starting transfers between devices, shifted(): return lax.ppermute(value, axis, pairs)  5.81 us
    ppermute x2, starting transfers between devices, swapped(): return lax.ppermute(value, along, pairs)  4.3 us
    pallas_call x1, Pallas kernels, shards(): pl.pallas_call(functools.partial(pack_columns, parts, band), out_shape=[s...  2.27 us
    pallas_call x1, Pallas kernels, shards(): pl.pallas_call(inner_rest, out_shape=shape(nest_old.shape, f32), in_specs...  2.17 us
    ppermute x4, waiting for transfers between devices, shifted(): return lax.ppermute(value, axis, pairs)  2.15 us
    ppermute x1, waiting for transfers between devices, shifted_both(): return lax.ppermute(value, ('gx', 'gy', 'gz'), pairs)  2.1 us
    pallas_call x1, Pallas kernels, shards(): pl.pallas_call(functools.partial(edges, parts, parent_cols), out_shape=[s...  2.08 us
    pallas_call x1, Pallas kernels, shards(): pl.pallas_call(functools.partial(inner_first, band), out_shape=[shape((pa...  1.81 us
  transfers between devices with their start and end apart: 7, of which 5 were waited for; matrix products, arithmetic and copies ran while one was open for 0% of the time, Pallas kernels for 20%

profile of v3, /device:TPU:0, one launch (start us, length us, event | category | flops | bytes accessed | tf_op | source)
XLA Modules:
  0.0 28.5 jit_solution(14459807461629475843)
XLA Ops:
  1.3 0.0 copy-start
  1.3 0.0 copy-start.1
  1.3 0.0 copy-start.2
  1.3 0.0 copy-start.3
  1.3 0.0 copy-start.4
  1.3 2.3 %pack_columns.1 = f32[72,128]{1,0:T(8,128)} custom-call(s32[1]{0:T(128)S(6)} %copy.11.oy_ref.oy_hbm, f32[8,72,384]{2,1,0:T(8,128)} %nest.5, f32[8,72,384]{2,1,0:T(8,128)} %source.8, f32[8,24,256]{2,1,0:T(8,128)} %parent.3, f32[8,24,256]{2,1,0:T(8,128)} %source.9), custom_call_target="tpu_custom_call" | custom-call | flops 200000 | bytes 1000000 | tf_op jit(solution)/shard_map/pack_columns/pallas_call | solution.py:606
  3.6 3.0 %collective-permute-start = (f32[72,128]{1,0:T(8,128)}, f32[72,128]{1,0:T(8,128)S(1)}, u32[]{:S(2)}, u32[]{:S(2)}) collective-permute-start(f32[72,128]{1,0:T(8,128)} %pack_columns.1), channel_id=1, source_target_pairs={{0,2},{2,0},{1,3},{3,1},{4,6},{6,4},{5,7},{7,5},{8,10},{10,8},{9,1... | collective-permute-start | bytes 110600 | tf_op jit(solution)/shard_map/ppermute | solution.py:587
  6.6 0.0 copy-done
  6.6 0.0 copy-done.1
  6.6 0.0 copy-done.2
  6.6 0.0 copy-done.3
  6.6 0.0 copy-done.4
  6.6 1.8 %inner_first.1 = (f32[24,128]{1,0:T(8,128)S(1)}, f32[8,72,384]{2,1,0:T(8,128)S(1)}, f32[4,72,128]{2,1,0:T(8,128)S(1)}) custom-call(s32[1]{0:T(128)S(6)} %copy.11.oy_ref.oy_hbm, f32[2,8]{1,0:T(2,128)S(1)} %copy-done.4, f32[8,72,384]{2,1,0:T(8,128)S(1)} %copy-done.1, f32[8,72,384]{2,1,0:T(8,128)S(1)} %copy-done, f32[8,24,256]{2,1,0:T(8,128)S(1)} %copy-done.2, ...), custom_call_target="tpu_custom_call" | custom-call | flops 4000000 | bytes 3000000 | tf_op jit(solution)/shard_map/inner_first/pallas_call | solution.py:628
  8.5 0.3 %collective-permute-done.rest_0_.y_left.y_right = f32[72,128]{1,0:T(8,128)S(1)} collective-permute-done((f32[72,128]{1,0:T(8,128)}, f32[72,128]{1,0:T(8,128)S(1)}, u32[]{:S(2)}, u32[]{:S(2)}) %collective-permute-start) | collective-permute-done | bytes 36896 | tf_op jit(solution)/shard_map/ppermute | solution.py:587
  8.8 0.1 pack_rows.1
  8.9 0.1 collective-permute-start.1
  9.0 4.2 %collective-permute-start.2 = (f32[56,384]{1,0:T(8,128)S(1)}, f32[56,384]{1,0:T(8,128)S(1)}, u32[]{:S(2)}, u32[]{:S(2)}) collective-permute-start(f32[56,384]{1,0:T(8,128)S(1)} %get-tuple-element.18), channel_id=1, source_target_pairs={{1,4},{4,1},{5,8},{8,5},{9,12},{12,9},{13,0},{0,13},{3,6},{6,3},{7... | collective-permute-start | bytes 258056 | tf_op jit(solution)/shard_map/ppermute | solution.py:763
  13.2 0.4 %collective-permute-start.3 = (f32[8,128]{1,0:T(8,128)S(1)}, f32[8,128]{1,0:T(8,128)S(1)}, u32[]{:S(2)}, u32[]{:S(2)}) collective-permute-start(f32[8,128]{1,0:T(8,128)S(1)} %get-tuple-element.19), channel_id=1, source_target_pairs={{0,12},{1,13},{4,0},{5,1},{8,4},{9,5},{12,8},{13,9},{2,14},{3,15},... | collective-permute-start | bytes 12296 | tf_op jit(solution)/shard_map/ppermute | solution.py:587
  14.3 2.2 %inner_rest.1.third = f32[8,72,384]{2,1,0:T(8,128)S(1)} custom-call(f32[2,8]{1,0:T(2,128)S(1)} %copy-done.4, f32[8,72,384]{2,1,0:T(8,128)S(1)} %get-tuple-element.13.first, f32[8,72,384]{2,1,0:T(8,128)S(1)} %copy-done, f32[24,128]{1,0:T(8,128)S(1)} %get-tuple-element.15.after_pack.strips), custom_call_target="tpu_custom_call" | custom-call | flops 8000000 | bytes 6000000 | tf_op jit(solution)/shard_map/inner_rest/pallas_call | solution.py:678
  16.5 0.0 copy-start.5
  16.5 0.3 %collective-permute-done.3.beyond = f32[8,128]{1,0:T(8,128)S(1)} collective-permute-done((f32[8,128]{1,0:T(8,128)S(1)}, f32[8,128]{1,0:T(8,128)S(1)}, u32[]{:S(2)}, u32[]{:S(2)}) %collective-permute-start.3) | collective-permute-done | bytes 4128 | tf_op jit(solution)/shard_map/ppermute | solution.py:587
  16.8 0.0 collective-permute-done.1.within
  16.8 0.0 collective-permute-done.2.across
  16.8 0.3 %copy-done.5 = f32[2,8]{1,0:T(2,128)S(1)} copy-done((f32[2,8]{1,0:T(2,128)S(1)}, f32[2,8]{1,0:T(2,128)}, u32[]{:S(2)}) %copy-start.5) | copy-done | bytes 88
  17.2 2.1 %edges.1 = (f32[8,72,384]{2,1,0:T(8,128)S(1)}, f32[8,24,128]{2,1,0:T(8,128)S(1)}) custom-call(s32[1]{0:T(128)S(6)} %copy.10.ox_ref, f32[2,8]{1,0:T(2,128)S(1)} %copy-done.5, f32[2,8]{1,0:T(2,128)S(1)} %copy-done.4, f32[8,72,384]{2,1,0:T(8,128)S(1)} %copy-done.1, f32[8,72,384]{2,1,0:T(8,128)S(1)} %copy-done, f32[8,72,384]{2,1,0:T(8,128)S(1)} %inner_rest.1.third, ...), custom_call_target="tpu_custom_call" | custom-call | flops 4000000 | bytes 3000000 | tf_op jit(solution)/shard_map/edges/pallas_call | solution.py:688
  19.3 0.8 %collective-permute-start.6 = (f32[8,24,128]{2,1,0:T(8,128)S(1)}, f32[8,24,128]{2,1,0:T(8,128)S(1)}, u32[]{:S(2)}, u32[]{:S(2)}) collective-permute-start(f32[8,24,128]{2,1,0:T(8,128)S(1)} %get-tuple-element.22.rest_0_), channel_id=1, source_target_pairs={{0,3},{1,6},{2,1},{3,4},{4,7},{5,10},{6,5},{7,8},{8,11},{9,14},{10... | collective-permute-start | bytes 294920 | tf_op jit(solution)/shard_map/ppermute | solution.py:776
  20.1 1.8 %collective-permute-start.5 = (f32[8,24,128]{2,1,0:T(8,128)S(1)}, f32[8,24,128]{2,1,0:T(8,128)S(1)}, u32[]{:S(2)}, u32[]{:S(2)}) collective-permute-start(f32[8,24,128]{2,1,0:T(8,128)S(1)} %get-tuple-element.22.rest_0_), channel_id=1, source_target_pairs={{0,1},{1,4},{4,5},{5,8},{8,9},{9,12},{12,13},{13,0},{2,3},{3,6},{6... | collective-permute-start | bytes 294920 | tf_op jit(solution)/shard_map/ppermute | solution.py:587
  21.9 0.5 %collective-permute-start.4 = (f32[8,24,128]{2,1,0:T(8,128)S(1)}, f32[8,24,128]{2,1,0:T(8,128)S(1)}, u32[]{:S(2)}, u32[]{:S(2)}) collective-permute-start(f32[8,24,128]{2,1,0:T(8,128)S(1)} %get-tuple-element.22.rest_0_), channel_id=1, source_target_pairs={{0,2},{2,0},{1,3},{3,1},{4,6},{6,4},{5,7},{7,5},{8,10},{10,8},{9,1... | collective-permute-start | bytes 294920 | tf_op jit(solution)/shard_map/ppermute | solution.py:587
  22.5 1.6 %parent_step.1 = (f32[8,24,256]{2,1,0:T(8,128)S(1)}, f32[8,72,384]{2,1,0:T(8,128)}) custom-call(f32[2,8]{1,0:T(2,128)S(1)} %copy-done.5, f32[8,72,384]{2,1,0:T(8,128)S(1)} %get-tuple-element.20.nest, f32[8,24,256]{2,1,0:T(8,128)S(1)} %copy-done.2, f32[8,24,256]{2,1,0:T(8,128)S(1)} %copy-done.3, f32[56,384]{1,0:T(8,128)S(1)} %collective-permute-done.1.within, ...), custom_call_target="tpu_custom_call" | custom-call | flops 800000 | bytes 2500000 | tf_op jit(solution)/shard_map/parent_step/pallas_call | solution.py:725
  24.0 2.1 %collective-permute-done.6.rest_3_ = f32[8,24,128]{2,1,0:T(8,128)S(1)} collective-permute-done((f32[8,24,128]{2,1,0:T(8,128)S(1)}, f32[8,24,128]{2,1,0:T(8,128)S(1)}, u32[]{:S(2)}, u32[]{:S(2)}) %collective-permute-start.6) | collective-permute-done | bytes 98336 | tf_op jit(solution)/shard_map/ppermute | solution.py:776
  26.1 1.0 %collective-permute-done.5.rest_2_ = f32[8,24,128]{2,1,0:T(8,128)S(1)} collective-permute-done((f32[8,24,128]{2,1,0:T(8,128)S(1)}, f32[8,24,128]{2,1,0:T(8,128)S(1)}, u32[]{:S(2)}, u32[]{:S(2)}) %collective-permute-start.5) | collective-permute-done | bytes 98336 | tf_op jit(solution)/shard_map/ppermute | solution.py:587
  27.2 0.5 %collective-permute-done.4.rest_1_ = f32[8,24,128]{2,1,0:T(8,128)S(1)} collective-permute-done((f32[8,24,128]{2,1,0:T(8,128)S(1)}, f32[8,24,128]{2,1,0:T(8,128)S(1)}, u32[]{:S(2)}, u32[]{:S(2)}) %collective-permute-start.4) | collective-permute-done | bytes 98336 | tf_op jit(solution)/shard_map/ppermute | solution.py:587
  27.7 0.8 %merge.1 = f32[8,24,256]{2,1,0:T(8,128)} custom-call(s32[1]{0:T(128)S(6)} %copy.10.ox_ref, s32[1]{0:T(128)S(6)} %copy.11.oy_ref.oy_hbm, f32[8,24,256]{2,1,0:T(8,128)S(1)} %get-tuple-element.21.step, f32[8,24,128]{2,1,0:T(8,128)S(1)} %get-tuple-element.22.rest_0_, f32[8,24,128]{2,1,0:T(8,128)S(1)} %collective-permute-done.4.rest_1_, ...), custom_call_target="tpu_custom_call" | custom-call | flops 200000 | bytes 800000 | tf_op jit(solution)/shard_map/merge/pallas_call | solution.py:744
Async XLA Ops:
  1.3 5.3 %copy-start = (f32[8,72,384]{2,1,0:T(8,128)S(1)}, f32[8,72,384]{2,1,0:T(8,128)}, u32[]{:S(2)}) copy-start(f32[8,72,384]{2,1,0:T(8,128)} %source.8) | copy-start | bytes 2654212
  1.3 5.3 %copy-start.1 = (f32[8,72,384]{2,1,0:T(8,128)S(1)}, f32[8,72,384]{2,1,0:T(8,128)}, u32[]{:S(2)}) copy-start(f32[8,72,384]{2,1,0:T(8,128)} %nest.5) | copy-start | bytes 2654212
  1.3 5.3 %copy-start.2 = (f32[8,24,256]{2,1,0:T(8,128)S(1)}, f32[8,24,256]{2,1,0:T(8,128)}, u32[]{:S(2)}) copy-start(f32[8,24,256]{2,1,0:T(8,128)} %parent.3) | copy-start | bytes 589828
  1.3 5.3 %copy-start.3 = (f32[8,24,256]{2,1,0:T(8,128)S(1)}, f32[8,24,256]{2,1,0:T(8,128)}, u32[]{:S(2)}) copy-start(f32[8,24,256]{2,1,0:T(8,128)} %source.9) | copy-start | bytes 589828
  1.3 5.3 %copy-start.4 = (f32[2,8]{1,0:T(2,128)S(1)}, f32[2,8]{1,0:T(2,128)}, u32[]{:S(2)}) copy-start(f32[2,8]{1,0:T(2,128)} %coefs.6) | copy-start | bytes 196
  3.6 5.2 %collective-permute-start = (f32[72,128]{1,0:T(8,128)}, f32[72,128]{1,0:T(8,128)S(1)}, u32[]{:S(2)}, u32[]{:S(2)}) collective-permute-start(f32[72,128]{1,0:T(8,128)} %pack_columns.1), channel_id=1, source_target_pairs={{0,2},{2,0},{1,3},{3,1},{4,6},{6,4},{5,7},{7,5},{8,10},{10,8},{9,1... | collective-permute-start | bytes 110600 | tf_op jit(solution)/shard_map/ppermute | solution.py:587
  8.9 7.9 %collective-permute-start.1 = (f32[56,384]{1,0:T(8,128)S(1)}, f32[56,384]{1,0:T(8,128)S(1)}, u32[]{:S(2)}, u32[]{:S(2)}) collective-permute-start(f32[56,384]{1,0:T(8,128)S(1)} %get-tuple-element.17), channel_id=1, source_target_pairs={{0,1},{1,0},{4,5},{5,4},{8,9},{9,8},{12,13},{13,12},{2,3},{3,2},{6... | collective-permute-start | bytes 258056 | tf_op jit(solution)/shard_map/ppermute | solution.py:763
  9.0 7.8 %collective-permute-start.2 = (f32[56,384]{1,0:T(8,128)S(1)}, f32[56,384]{1,0:T(8,128)S(1)}, u32[]{:S(2)}, u32[]{:S(2)}) collective-permute-start(f32[56,384]{1,0:T(8,128)S(1)} %get-tuple-element.18), channel_id=1, source_target_pairs={{1,4},{4,1},{5,8},{8,5},{9,12},{12,9},{13,0},{0,13},{3,6},{6,3},{7... | collective-permute-start | bytes 258056 | tf_op jit(solution)/shard_map/ppermute | solution.py:763
  13.2 3.6 %collective-permute-start.3 = (f32[8,128]{1,0:T(8,128)S(1)}, f32[8,128]{1,0:T(8,128)S(1)}, u32[]{:S(2)}, u32[]{:S(2)}) collective-permute-start(f32[8,128]{1,0:T(8,128)S(1)} %get-tuple-element.19), channel_id=1, source_target_pairs={{0,12},{1,13},{4,0},{5,1},{8,4},{9,5},{12,8},{13,9},{2,14},{3,15},... | collective-permute-start | bytes 12296 | tf_op jit(solution)/shard_map/ppermute | solution.py:587
  16.5 0.7 %copy-start.5 = (f32[2,8]{1,0:T(2,128)S(1)}, f32[2,8]{1,0:T(2,128)}, u32[]{:S(2)}) copy-start(f32[2,8]{1,0:T(2,128)} %coefs.7) | copy-start | bytes 196
  19.3 6.9 %collective-permute-start.6 = (f32[8,24,128]{2,1,0:T(8,128)S(1)}, f32[8,24,128]{2,1,0:T(8,128)S(1)}, u32[]{:S(2)}, u32[]{:S(2)}) collective-permute-start(f32[8,24,128]{2,1,0:T(8,128)S(1)} %get-tuple-element.22.rest_0_), channel_id=1, source_target_pairs={{0,3},{1,6},{2,1},{3,4},{4,7},{5,10},{6,5},{7,8},{8,11},{9,14},{10... | collective-permute-start | bytes 294920 | tf_op jit(solution)/shard_map/ppermute | solution.py:776
  20.1 7.1 %collective-permute-start.5 = (f32[8,24,128]{2,1,0:T(8,128)S(1)}, f32[8,24,128]{2,1,0:T(8,128)S(1)}, u32[]{:S(2)}, u32[]{:S(2)}) collective-permute-start(f32[8,24,128]{2,1,0:T(8,128)S(1)} %get-tuple-element.22.rest_0_), channel_id=1, source_target_pairs={{0,1},{1,4},{4,5},{5,8},{8,9},{9,12},{12,13},{13,0},{2,3},{3,6},{6... | collective-permute-start | bytes 294920 | tf_op jit(solution)/shard_map/ppermute | solution.py:587
  21.9 5.8 %collective-permute-start.4 = (f32[8,24,128]{2,1,0:T(8,128)S(1)}, f32[8,24,128]{2,1,0:T(8,128)S(1)}, u32[]{:S(2)}, u32[]{:S(2)}) collective-permute-start(f32[8,24,128]{2,1,0:T(8,128)S(1)} %get-tuple-element.22.rest_0_), channel_id=1, source_target_pairs={{0,2},{2,0},{1,3},{3,1},{4,6},{6,4},{5,7},{7,5},{8,10},{10,8},{9,1... | collective-permute-start | bytes 294920 | tf_op jit(solution)/shard_map/ppermute | solution.py:587

commit v4 on v3

--- a/solution.py
+++ b/solution.py
@@ -69,6 +69,60 @@
                 found = jnp.where((place >= 0) & (place < 4), tile(ref, level, at), found)
             turn = (16384 + first + STRIDE * level - base) & (LANES - 1)
             total = total + pltpu.roll(found, turn, 1)
+    return total
+
+
+def pack_pair(nest, source, parent, parent_source, out, fine_buf, coarse_buf, sems):
+    levels, rows, cols = nest.shape
+    parent_rows, parent_cols = parent.shape[1:]
+    right = lax.axis_index("gy") == 0
+    loads = []
+    for at, (ref, buf) in enumerate(
+        (
+            (parent, coarse_buf.at[0]),
+            (parent_source, coarse_buf.at[1]),
+            (nest, fine_buf.at[0]),
+            (source, fine_buf.at[1]),
+        )
+    ):
+        start = pl.multiple_of(jnp.where(right, ref.shape[2] - LANES, 0), LANES)
+        loads.append(pltpu.make_async_copy(ref.at[:, :, pl.ds(start, LANES)], buf, sems.at[at]))
+    for copy in loads:
+        copy.start()
+
+    def columns(value, count, to):
+        first = jnp.where(right, LANES - count, 0)
+        place = iota(value.shape, 1) - first
+        value = jnp.where((place >= 0) & (place < count), value, 0.0)
+        return pltpu.roll(value, (LANES + to - first) & (LANES - 1), 1)
+
+    part = jnp.zeros((parent_rows, LANES), jnp.float32)
+    loads[0].wait()
+    loads[1].wait()
+    for level in range(levels):
+        base = STRIDE * level
+        part = part + columns(coarse_buf[0, level], 1, base + PARENT_AT)
+        part = part + columns(coarse_buf[0, level], 2, base + STRIP_AT)
+        part = part + columns(coarse_buf[1, level], 2, base + STRIP_SOURCE_AT)
+    total = jnp.zeros((rows, LANES), jnp.float32)
+    loads[2].wait()
+    loads[3].wait()
+    for level in range(levels):
+        base = STRIDE * level
+        total = total + columns(fine_buf[0, level], 3, base)
+        total = total + columns(fine_buf[1, level], 3, base + SOURCE_AT)
+    out[...] = total
+    out[:parent_rows, :] += part
+
+
+def across_border(message, oy, parent_cols, me):
+    c = iota(message.shape, 1) & (STRIDE - 1)
+    place = jnp.where(me == 0, parent_cols + 1, 1) - oy
+    total = jnp.zeros(message.shape, jnp.float32)
+    for turn in (-1, 0, 2, 3):
+        at = jnp.where(c >= STRIP_SOURCE_AT, c - STRIP_SOURCE_AT, c - STRIP_AT) - turn
+        fits = (c >= STRIP_AT) & (at >= 0) & (at < 2) & (place == turn)
+        total = total + jnp.where(fits, turned(message, turn), 0.0)
     return total
 
 
@@ -177,11 +231,57 @@
     lax.fori_loop(0, levels // 2, two_levels, 0)
 
 
+def spread_coefs(parent_coefs, coefs, out):
+    levels = out.shape[2]
+    lane = iota((levels, LANES), 1)
+    row = iota((levels, LANES), 0)
+    for at, ref in enumerate((parent_coefs, coefs)):
+        for which in range(2):
+            packed = jnp.full(lane.shape, ref[which, 0], jnp.float32)
+            rows = packed
+            for level in range(1, levels):
+                packed = jnp.where(lane >= STRIDE * level, ref[which, level], packed)
+                rows = jnp.where(row == level, ref[which, level], rows)
+            out[0, 2 * at + which] = packed
+            out[1, 2 * at + which] = rows
+
+
 def inner_first(
-    band, oy_ref, coefs, nest, source, parent, parent_source, strip, first, packs
+    band,
+    ox_hbm,
+    oy_hbm,
+    parent_coefs,
+    coefs,
+    nest,
+    source,
+    parent,
+    parent_source,
+    strip,
+    first,
+    packs,
+    spread,
+    rows_out,
+    offsets_out,
+    ox_ref,
+    oy_ref,
+    sems,
 ):
     levels, rows, cols = nest.shape
-    strip[...] = edge_strip(lax.axis_index("gy"), band, oy_ref[0], parent, parent_source)
+    loads = [
+        pltpu.make_async_copy(ref, to, sems.at[at])
+        for at, (ref, to) in enumerate(((ox_hbm, ox_ref), (oy_hbm, oy_ref)))
+    ]
+    for copy in loads:
+        copy.start()
+    spread_coefs(parent_coefs, coefs, spread)
+    for copy in loads:
+        copy.wait()
+    ox, oy = ox_ref[0], oy_ref[0]
+    rows_out[0] = jnp.full(rows_out.shape[1:], ox, jnp.int32)
+    rows_out[1] = jnp.full(rows_out.shape[1:], oy, jnp.int32)
+    offsets_out[0] = ox
+    offsets_out[1] = oy
+    strip[...] = edge_strip(lax.axis_index("gy"), band, oy, parent, parent_source)
     lane = iota((rows, LANES), 1)
     for at, ref in enumerate((nest, source)):
         left = jnp.zeros(lane.shape, jnp.float32)
@@ -214,10 +314,10 @@
 
 
 def pack_rows(
-    parts, old_top, old_end, src_top, src_end, par_top, par_end, own_strip, *rest
+    parts, old_top, old_end, src_top, src_end, par_top, par_end, own_strip, offset_rows, *rest
 ):
     columns = rest[: parts - 1]
-    within, across, far, strip_out, both = rest[parts - 1 :]
+    across, within, far, strip_out, both = rest[parts - 1 :]
     core = lax.axis_index("gz")
     up, down = both.at[core], both.at[1 - core]
     levels, _, cols = old_top.shape
@@ -227,9 +327,13 @@
     strip_rows = own_strip.shape[0]
     lane = iota((strip_rows, LANES), 1)
     strips = own_strip[...]
-    for message in columns:
-        strips = strips + message[:strip_rows, :]
-    strips = jnp.where((lane & (STRIDE - 1)) >= STRIP_AT, strips, 0.0)
+    if parts == 2:
+        oy = jnp.concatenate([offset_rows[1]] * (strip_rows // 8), axis=0)
+        strips = strips + across_border(left[:strip_rows, :], oy, par_top.shape[2], me)
+    else:
+        for message in columns:
+            strips = strips + message[:strip_rows, :]
+        strips = jnp.where((lane & (STRIDE - 1)) >= STRIP_AT, strips, 0.0)
     strip_out[...] = strips
     far[...] = strips[:8]
     pieces = cols // LANES
@@ -268,16 +372,15 @@
 def edges(
     parts,
     parent_cols,
-    ox_ref,
-    parent_coefs,
-    coefs,
+    offset_rows,
+    spread,
     nest,
     source,
     third,
     packs,
     strips,
+    across,
     within,
-    across,
     beyond,
     y_left,
     y_right,
@@ -297,7 +400,6 @@
     both[0] = within[...]
     both[1] = across[...]
     before, after = both.at[1 - core], both.at[core]
-    ox = ox_ref[0]
     is_south = me == 0
     is_north = me == parts - 1
 
@@ -322,12 +424,8 @@
     )
     count = old.shape[0]
 
-    def per_level(ref, which, shape):
-        lane = iota(shape, 1)
-        total = jnp.full(shape, ref[which, 0], jnp.float32)
-        for level in range(1, levels):
-            total = jnp.where(lane >= STRIDE * level, ref[which, level], total)
-        return total
+    def packed_coef(which, height):
+        return jnp.concatenate([spread[0, which]] * (height // 8), axis=0)
 
     def stacked(value):
         lane = iota(value.shape, 1)
@@ -343,13 +441,13 @@
         )
 
     diff = (
-        per_level(parent_coefs, 0, old.shape) * (around(old) - 4.0 * old)
-        + per_level(parent_coefs, 1, old.shape) * (stacked(old) - 2.0 * old)
+        packed_coef(0, count) * (around(old) - 4.0 * old)
+        + packed_coef(1, count) * (stacked(old) - 2.0 * old)
         + turned(old, STRIP_AT - STRIP_SOURCE_AT)
     )
     index = iota((rows + 16, count), 0)
     nest_row = jnp.where(index < rows, index, jnp.where(index < rows + 8, index - rows - 3, index - 13))
-    parent_row = ((nest_row + 3) * 171 >> 9) - 1 + ox
+    parent_row = ((nest_row + 3) * 171 >> 9) - 1 + offset_rows[0, 0:1, :count]
     pick = (iota((rows + 16, count), 1) == parent_row).astype(jnp.float32)
     picked = jnp.dot(
         pick,
@@ -366,8 +464,8 @@
     at = lane - c + STRIP_AT + jnp.where(c >= rim_first + 3, 2, 1)
     rim_old = jnp.take_along_axis(picked_old[:rows], at, axis=1)
     rim_diff = jnp.take_along_axis(picked_diff[:rows], at, axis=1)
-    ch = per_level(coefs, 0, lane.shape)
-    cv = per_level(coefs, 1, lane.shape)
+    ch = packed_coef(2, rows)
+    cv = packed_coef(3, rows)
     centre = 1.0 - 4.0 * ch - 2.0 * cv
     left = jnp.where(c < 3, y_left[...], packs[0])
     left_src = jnp.where(c < 3, turned(y_left[...], -SOURCE_AT), packs[2])
@@ -433,8 +531,10 @@
         north = (lane >= LANES - RIM) & (lane < LANES - low) & is_north
         weight = substep / SUBSTEPS
         for level in range(levels):
-            c_h = coefs[0, level]
-            c_v = coefs[1, level]
+            c_h, c_v = (
+                jnp.concatenate([spread[1, which, level : level + 1, :]] * (width // LANES), axis=1)
+                for which in (2, 3)
+            )
             c_0 = 1.0 - 4.0 * c_h - 2.0 * c_v
             for window in range(2):
                 now = here[level, window]
@@ -503,7 +603,7 @@
 
 
 def parent_step(
-    parts, coefs, nest, parent, source, within, across, y_left, y_right, out, nest_out, tail, sem
+    parts, spread, nest, parent, source, within, across, y_left, y_right, out, nest_out, tail, sem
 ):
     store = pltpu.make_async_copy(nest, nest_out, sem)
     store.start()
@@ -541,16 +641,18 @@
         stacked = (parent[level - 1] if level > 0 else zero) + (
             parent[level + 1] if level < levels - 1 else zero
         )
-        ch = coefs[0, level]
-        cv = coefs[1, level]
+        ch, cv = (
+            jnp.concatenate([spread[1, which, level : level + 1, :]] * (cols // LANES), axis=1)
+            for which in (0, 1)
+        )
         out[level] = (
             (1.0 - 4.0 * ch - 2.0 * cv) * now + ch * around + (cv * stacked + source[level])
         )
     store.wait()
 
 
-def merge(parts, band, ox_ref, oy_ref, step, *rest):
-    own, previous, out, joined = (
+def merge(parts, band, offsets, step, *rest):
+    previous, own, out, joined = (
         rest[:parts],
         rest[parts : 2 * parts],
         rest[2 * parts],
@@ -559,8 +661,8 @@
     levels, rows, cols = step.shape
     foot = own[0].shape[2]
     me = lax.axis_index("gy")
-    ox = ox_ref[0]
-    oy = oy_ref[0]
+    ox = offsets[0]
+    oy = offsets[1]
     for k in range(parts):
         joined[k, :, :rows, :] = previous[k][...]
         joined[k, :, rows:, :] = own[k][...]
@@ -603,41 +705,76 @@
     anywhere = pl.BlockSpec(memory_space=pl.ANY)
     in_hbm = pl.BlockSpec(memory_space=pltpu.HBM)
     sides = 1 if parts == 2 else 2
-    packed = pl.pallas_call(
-        functools.partial(pack_columns, parts, band),
-        out_shape=[
-            shape((rows if k in (1, parts - 1) else parent_rows, LANES), f32)
-            for k in range(1, parts)
-        ],
-        in_specs=[in_hbm] * 5,
-        out_specs=[whole()] * (parts - 1),
-        scratch_shapes=[
-            VMEM((sides, levels, rows, LANES), f32),
-            VMEM((sides, levels, rows, LANES), f32),
-            VMEM(parent_old.shape, f32),
-            VMEM(parent_old.shape, f32),
-            pltpu.SMEM(offset_y.shape, jnp.int32),
-            pltpu.SemaphoreType.DMA((sides, 2)),
-            pltpu.SemaphoreType.DMA((3,)),
-        ],
-        compiler_params=params(MOST),
-        cost_estimate=cost(200000, 1000000),
-        name="pack_columns",
-    )(offset_y, nest_old, nest_source, parent_old, parent_source)
+    if parts == 2:
+        packed = [
+            pl.pallas_call(
+                pack_pair,
+                out_shape=shape((rows, LANES), f32),
+                in_specs=[in_hbm] * 4,
+                out_specs=whole(),
+                scratch_shapes=[
+                    VMEM((2, levels, rows, LANES), f32),
+                    VMEM((2, levels, parent_rows, LANES), f32),
+                    pltpu.SemaphoreType.DMA((4,)),
+                ],
+                compiler_params=params(MOST),
+                cost_estimate=cost(200000, 800000),
+                name="pack_pair",
+            )(nest_old, nest_source, parent_old, parent_source)
+        ]
+    else:
+        packed = pl.pallas_call(
+            functools.partial(pack_columns, parts, band),
+            out_shape=[
+                shape((rows if k in (1, parts - 1) else parent_rows, LANES), f32)
+                for k in range(1, parts)
+            ],
+            in_specs=[in_hbm] * 5,
+            out_specs=[whole()] * (parts - 1),
+            scratch_shapes=[
+                VMEM((sides, levels, rows, LANES), f32),
+                VMEM((sides, levels, rows, LANES), f32),
+                VMEM(parent_old.shape, f32),
+                VMEM(parent_old.shape, f32),
+                pltpu.SMEM(offset_y.shape, jnp.int32),
+                pltpu.SemaphoreType.DMA((sides, 2)),
+                pltpu.SemaphoreType.DMA((3,)),
+            ],
+            compiler_params=params(MOST),
+            cost_estimate=cost(200000, 1000000),
+            name="pack_columns",
+        )(offset_y, nest_old, nest_source, parent_old, parent_source)
     columns = [shifted(packed[k - 1], "gy", k) for k in range(1, parts)]
-    own_strip, first, packs = pl.pallas_call(
+    own_strip, first, packs, spread, offset_rows, offsets = pl.pallas_call(
         functools.partial(inner_first, band),
         out_shape=[
             shape((parent_rows, LANES), f32),
             shape(nest_old.shape, f32),
             shape((4, rows, LANES), f32),
+            shape((2, 4, levels, LANES), f32),
+            shape((2, 8, LANES), jnp.int32),
+            shape((2,), jnp.int32),
         ],
-        in_specs=[scalars()] * 2 + [whole()] * 4,
-        out_specs=[whole()] * 3,
+        in_specs=[in_hbm] * 2 + [scalars()] * 2 + [whole()] * 4,
+        out_specs=[whole()] * 5 + [scalars()],
+        scratch_shapes=[
+            pltpu.SMEM(offset_x.shape, jnp.int32),
+            pltpu.SMEM(offset_y.shape, jnp.int32),
+            pltpu.SemaphoreType.DMA((2,)),
+        ],
         compiler_params=params(),
         cost_estimate=cost(4000000, 3000000),
         name="inner_first",
-    )(offset_y, nest_coefs, nest_old, nest_source, parent_old, parent_source)
+    )(
+        offset_x,
+        offset_y,
+        parent_coefs,
+        nest_coefs,
+        nest_old,
+        nest_source,
+        parent_old,
+        parent_source,
+    )
 
     def block(ref, last):
         count = ref.shape[1] // 8 - 1 if last else 0
@@ -652,7 +789,7 @@
         shape((8, LANES), f32),
         shape((parent_rows, LANES), f32),
     ]
-    within, across, far, strips = pl.pallas_call(
+    across, within, far, strips = pl.pallas_call(
         functools.partial(pack_rows, parts),
         out_shape=outs,
         grid=(1,),
@@ -664,6 +801,7 @@
             block(parent_old, False),
             block(parent_old, True),
             full(own_strip.shape),
+            full(offset_rows.shape),
         ]
         + [full(message.shape) for message in columns],
         out_specs=[full(out.shape) for out in outs],
@@ -671,7 +809,7 @@
         compiler_params=params(),
         cost_estimate=cost(100000, 700000),
         name="pack_rows",
-    )(nest_old, nest_old, nest_source, nest_source, parent_old, parent_old, own_strip, *columns)
+    )(nest_old, nest_old, nest_source, nest_source, parent_old, parent_old, own_strip, offset_rows, *columns)
     across = swapped(across, 1)
     within = swapped(within, 0)
     beyond = shifted(far, along, -2)
@@ -691,7 +829,7 @@
             shape(nest_old.shape, f32),
             shape((levels, parent_rows, foot), f32),
         ],
-        in_specs=[scalars()] * 3 + [whole()] * 10,
+        in_specs=[whole()] * 12,
         out_specs=[whole(), whole()],
         scratch_shapes=[
             VMEM((2, height, width), f32),
@@ -704,35 +842,34 @@
         cost_estimate=cost(4000000, 3000000),
         name="edges",
     )(
-        offset_x,
-        parent_coefs,
-        nest_coefs,
+        offset_rows,
+        spread,
         nest_old,
         nest_source,
         third,
         packs,
         strips,
+        across,
         within,
-        across,
         beyond,
         columns[0],
         columns[-1],
     )
-    own = [coarse] + [shifted(coarse, "gy", k) for k in range(1, parts)]
     previous = [shifted(coarse, along, 1)] + [
         shifted_both(coarse, k) for k in range(1, parts)
     ]
+    own = [coarse] + [shifted(coarse, "gy", k) for k in range(1, parts)]
     step, nest_new = pl.pallas_call(
         functools.partial(parent_step, parts),
         out_shape=[shape(parent_old.shape, f32), shape(nest_old.shape, f32)],
-        in_specs=[scalars(), anywhere] + [whole()] * 6,
+        in_specs=[whole(), anywhere] + [whole()] * 6,
         out_specs=[whole(), in_hbm],
         scratch_shapes=[VMEM((2, levels, parent_cols), f32), pltpu.SemaphoreType.DMA],
         compiler_params=params(),
         cost_estimate=cost(800000, 2500000),
         name="parent_step",
     )(
-        parent_coefs,
+        spread,
         nest_done,
         parent_old,
         parent_source,
@@ -744,13 +881,13 @@
     parent_new = pl.pallas_call(
         functools.partial(merge, parts, band),
         out_shape=shape(parent_old.shape, f32),
-        in_specs=[scalars()] * 2 + [whole()] * (1 + 2 * parts),
+        in_specs=[scalars()] + [whole()] * (1 + 2 * parts),
         out_specs=whole(),
         scratch_shapes=[VMEM((parts, levels, 2 * parent_rows, foot), f32)],
         compiler_params=params(),
         cost_estimate=cost(200000, 800000),
         name="merge",
-    )(offset_x, offset_y, step, *own, *previous)
+    )(offsets, step, *previous, *own)
     return (parent_new, nest_new)
 
 

time: 28.7 us -> 28.3 us (0.986)
  starting transfers between devices: 11 us -> 9.24 us
  waiting for transfers between devices: 4.26 us -> 5.41 us
  Pallas kernels: 10.9 us -> 11.3 us
  local copies, waits for them, and re-layouts: 0.37 us -> 0.03 us
    ppermute x2, starting transfers between devices: 4.3 us -> 2.83 us  [swapped(): return lax.ppermute(value, along, pairs)]
    pallas_call x1, Pallas kernels: 1.81 us -> 2.88 us  [shards(): pl.pallas_call(functools.partial(inner_first, band), out_shape=[shape((pa...]
    ppermute x4, waiting for transfers between devices: 2.15 us -> 2.77 us  [shifted(): return lax.ppermute(value, axis, pairs)]
    pallas_call x1, Pallas kernels: 2.08 us -> 1.54 us  [shards(): pl.pallas_call(functools.partial(edges, parts, parent_cols), out_shape=[s...]
    pallas_call x1, Pallas kernels: 0.82 us -> 1.36 us  [shards(): pl.pallas_call(functools.partial(merge, parts, band), out_shape=shape(par...]
    ppermute x1, waiting for transfers between devices: 2.1 us -> 2.64 us  [shifted_both(): return lax.ppermute(value, ('gx', 'gy', 'gz'), pairs)]
    pallas_call x1, Pallas kernels: 1.58 us -> 1.07 us  [shards(): pl.pallas_call(functools.partial(parent_step, parts), out_shape=[shape(pa...]
    unnamed x12, local copies, waits for them, and re-layouts: 0.37 us -> 0.03 us
  transfers between devices with their start and end apart: 7 -> 7, of which waited for: 5 -> 4; matrix products, arithmetic and copies ran while one was open for 0% -> 0% of each run, Pallas kernels for 20% -> 22%
where the time goes in v4:
time: 28.3 us; the launch traced here: 28.1 us
  Pallas kernels  11.3 us (40%)
  starting transfers between devices  9.24 us (33%)
  waiting for transfers between devices  5.41 us (19%)
  between operations  2.09 us (7%)
    ppermute x4, starting transfers between devices, shifted(): return lax.ppermute(value, axis, pairs)  5.87 us
    pallas_call x1, Pallas kernels, shards(): pl.pallas_call(functools.partial(inner_first, band), out_shape=[shape((pa...  2.88 us
    ppermute x2, starting transfers between devices, swapped(): return lax.ppermute(value, along, pairs)  2.83 us
    ppermute x4, waiting for transfers between devices, shifted(): return lax.ppermute(value, axis, pairs)  2.77 us
    ppermute x1, waiting for transfers between devices, shifted_both(): return lax.ppermute(value, ('gx', 'gy', 'gz'), pairs)  2.64 us
    pallas_call x1, Pallas kernels, shards(): pl.pallas_call(pack_pair, out_shape=shape((rows, LANES), f32), in_specs=[...  2.18 us
    pallas_call x1, Pallas kernels, shards(): pl.pallas_call(inner_rest, out_shape=shape(nest_old.shape, f32), in_specs...  2.15 us
    pallas_call x1, Pallas kernels, shards(): pl.pallas_call(functools.partial(edges, parts, parent_cols), out_shape=[s...  1.54 us
  transfers between devices with their start and end apart: 7, of which 4 were waited for; matrix products, arithmetic and copies ran while one was open for 0% of the time, Pallas kernels for 22%

profile of v4, /device:TPU:0, one launch (start us, length us, event | category | flops | bytes accessed | tf_op | source)
XLA Modules:
  0.0 28.1 jit_solution(5145308347579005389)
XLA Ops:
  0.6 0.0 copy-start
  0.6 0.0 copy-start.1
  0.7 0.0 copy-start.2
  0.7 0.0 copy-start.3
  0.7 0.0 copy-start.5
  0.7 2.2 %pack_pair.1 = f32[72,128]{1,0:T(8,128)} custom-call(f32[8,72,384]{2,1,0:T(8,128)} %nest.5, f32[8,72,384]{2,1,0:T(8,128)} %source.8, f32[8,24,256]{2,1,0:T(8,128)} %parent.5, f32[8,24,256]{2,1,0:T(8,128)} %source.9), custom_call_target="tpu_custom_call" | custom-call | flops 200000 | bytes 800000 | tf_op jit(solution)/shard_map/pack_pair/pallas_call | solution.py:710
  2.9 3.0 %collective-permute-start = (f32[72,128]{1,0:T(8,128)}, f32[72,128]{1,0:T(8,128)S(1)}, u32[]{:S(2)}, u32[]{:S(2)}) collective-permute-start(f32[72,128]{1,0:T(8,128)} %pack_pair.1), channel_id=1, source_target_pairs={{0,2},{2,0},{1,3},{3,1},{4,6},{6,4},{5,7},{7,5},{8,10},{10,8},{9,1... | collective-permute-start | bytes 110600 | tf_op jit(solution)/shard_map/ppermute | solution.py:689
  6.5 0.0 copy-start.4
  7.2 0.0 copy-done
  7.2 0.0 copy-done.1
  7.2 0.0 copy-done.2
  7.2 0.0 copy-done.3
  7.2 0.0 copy-done.5
  7.2 0.0 copy-done.4
  7.2 2.9 %inner_first.1 = (f32[24,128]{1,0:T(8,128)S(1)}, f32[8,72,384]{2,1,0:T(8,128)S(1)}, f32[4,72,128]{2,1,0:T(8,128)S(1)}, f32[2,4,8,128]{3,2,1,0:T(8,128)S(1)}, s32[2,8,128]{2,1,0:T(8,128)S(1)}, /*index=5*/s32[2]{0:T(128)S(1)}) custom-call(s32[1]{0:T(128)S(6)} %copy.10.ox_hbm, s32[1]{0:T(128)S(6)} %copy.11.oy_hbm, f32[2,8]{1,0:T(2,128)S(1)} %copy-done.5, ...), custom_call_target="tpu_custom_call" | custom-call | flops 4000000 | bytes 3000000 | tf_op jit(solution)/shard_map/inner_first/pallas_call | solution.py:748
  10.1 0.0 collective-permute-done.rest_0_.y_left.y_right
  10.1 0.1 pack_rows.1
  10.3 2.8 %collective-permute-start.1 = (f32[56,384]{1,0:T(8,128)S(1)}, f32[56,384]{1,0:T(8,128)S(1)}, u32[]{:S(2)}, u32[]{:S(2)}) collective-permute-start(f32[56,384]{1,0:T(8,128)S(1)} %get-tuple-element.23), channel_id=1, source_target_pairs={{1,4},{4,1},{5,8},{8,5},{9,12},{12,9},{13,0},{0,13},{3,6},{6,3},{7... | collective-permute-start | bytes 258056 | tf_op jit(solution)/shard_map/ppermute | solution.py:900
  13.1 0.0 collective-permute-start.2
  13.1 1.2 %collective-permute-start.3 = (f32[8,128]{1,0:T(8,128)S(1)}, f32[8,128]{1,0:T(8,128)S(1)}, u32[]{:S(2)}, u32[]{:S(2)}) collective-permute-start(f32[8,128]{1,0:T(8,128)S(1)} %get-tuple-element.25), channel_id=1, source_target_pairs={{0,12},{1,13},{4,0},{5,1},{8,4},{9,5},{12,8},{13,9},{2,14},{3,15},... | collective-permute-start | bytes 12296 | tf_op jit(solution)/shard_map/ppermute | solution.py:689
  14.3 2.1 %inner_rest.1.third = f32[8,72,384]{2,1,0:T(8,128)S(1)} custom-call(f32[2,8]{1,0:T(2,128)S(1)} %copy-done.4, f32[8,72,384]{2,1,0:T(8,128)S(1)} %get-tuple-element.19.first, f32[8,72,384]{2,1,0:T(8,128)S(1)} %copy-done, f32[24,128]{1,0:T(8,128)S(1)} %get-tuple-element.21.after_pack.strips), custom_call_target="tpu_custom_call" | custom-call | flops 8000000 | bytes 6000000 | tf_op jit(solution)/shard_map/inner_rest/pallas_call | solution.py:816
  16.5 0.3 %collective-permute-done.3.beyond = f32[8,128]{1,0:T(8,128)S(1)} collective-permute-done((f32[8,128]{1,0:T(8,128)S(1)}, f32[8,128]{1,0:T(8,128)S(1)}, u32[]{:S(2)}, u32[]{:S(2)}) %collective-permute-start.3) | collective-permute-done | bytes 4128 | tf_op jit(solution)/shard_map/ppermute | solution.py:689
  16.8 0.0 collective-permute-done.1.across
  16.8 0.0 collective-permute-done.2.within
  16.8 1.5 %edges.1 = (f32[8,72,384]{2,1,0:T(8,128)S(1)}, f32[8,24,128]{2,1,0:T(8,128)S(1)}) custom-call(s32[2,8,128]{2,1,0:T(8,128)S(1)} %get-tuple-element.18.offset_rows, f32[2,4,8,128]{3,2,1,0:T(8,128)S(1)} %get-tuple-element.17.spread, f32[8,72,384]{2,1,0:T(8,128)S(1)} %copy-done.1, f32[8,72,384]{2,1,0:T(8,128)S(1)} %copy-done, ...), custom_call_target="tpu_custom_call" | custom-call | flops 4000000 | bytes 3000000 | tf_op jit(solution)/shard_map/edges/pallas_call | solution.py:826
  18.3 0.6 %collective-permute-start.6 = (f32[8,24,128]{2,1,0:T(8,128)S(1)}, f32[8,24,128]{2,1,0:T(8,128)S(1)}, u32[]{:S(2)}, u32[]{:S(2)}) collective-permute-start(f32[8,24,128]{2,1,0:T(8,128)S(1)} %get-tuple-element.28.rest_2_), channel_id=1, source_target_pairs={{0,2},{2,0},{1,3},{3,1},{4,6},{6,4},{5,7},{7,5},{8,10},{10,8},{9,1... | collective-permute-start | bytes 294920 | tf_op jit(solution)/shard_map/ppermute | solution.py:689
  18.9 0.5 %collective-permute-start.5 = (f32[8,24,128]{2,1,0:T(8,128)S(1)}, f32[8,24,128]{2,1,0:T(8,128)S(1)}, u32[]{:S(2)}, u32[]{:S(2)}) collective-permute-start(f32[8,24,128]{2,1,0:T(8,128)S(1)} %get-tuple-element.28.rest_2_), channel_id=1, source_target_pairs={{0,3},{1,6},{2,1},{3,4},{4,7},{5,10},{6,5},{7,8},{8,11},{9,14},{10... | collective-permute-start | bytes 294920 | tf_op jit(solution)/shard_map/ppermute | solution.py:913
  19.4 1.1 %collective-permute-start.4 = (f32[8,24,128]{2,1,0:T(8,128)S(1)}, f32[8,24,128]{2,1,0:T(8,128)S(1)}, u32[]{:S(2)}, u32[]{:S(2)}) collective-permute-start(f32[8,24,128]{2,1,0:T(8,128)S(1)} %get-tuple-element.28.rest_2_), channel_id=1, source_target_pairs={{0,1},{1,4},{4,5},{5,8},{8,9},{9,12},{12,13},{13,0},{2,3},{3,6},{6... | collective-permute-start | bytes 294920 | tf_op jit(solution)/shard_map/ppermute | solution.py:689
  20.5 1.1 %parent_step.1 = (f32[8,24,256]{2,1,0:T(8,128)S(1)}, f32[8,72,384]{2,1,0:T(8,128)}) custom-call(f32[2,4,8,128]{3,2,1,0:T(8,128)S(1)} %get-tuple-element.17.spread, f32[8,72,384]{2,1,0:T(8,128)S(1)} %get-tuple-element.26.nest, f32[8,24,256]{2,1,0:T(8,128)S(1)} %copy-done.2, f32[8,24,256]{2,1,0:T(8,128)S(1)} %copy-done.3, ...), custom_call_target="tpu_custom_call" | custom-call | flops 800000 | bytes 2500000 | tf_op jit(solution)/shard_map/parent_step/pallas_call | solution.py:862
  21.6 1.4 %collective-permute-done.6.rest_3_ = f32[8,24,128]{2,1,0:T(8,128)S(1)} collective-permute-done((f32[8,24,128]{2,1,0:T(8,128)S(1)}, f32[8,24,128]{2,1,0:T(8,128)S(1)}, u32[]{:S(2)}, u32[]{:S(2)}) %collective-permute-start.6) | collective-permute-done | bytes 98336 | tf_op jit(solution)/shard_map/ppermute | solution.py:689
  23.0 2.6 %collective-permute-done.5.rest_1_ = f32[8,24,128]{2,1,0:T(8,128)S(1)} collective-permute-done((f32[8,24,128]{2,1,0:T(8,128)S(1)}, f32[8,24,128]{2,1,0:T(8,128)S(1)}, u32[]{:S(2)}, u32[]{:S(2)}) %collective-permute-start.5) | collective-permute-done | bytes 98336 | tf_op jit(solution)/shard_map/ppermute | solution.py:913
  25.6 1.1 %collective-permute-done.4.rest_0_ = f32[8,24,128]{2,1,0:T(8,128)S(1)} collective-permute-done((f32[8,24,128]{2,1,0:T(8,128)S(1)}, f32[8,24,128]{2,1,0:T(8,128)S(1)}, u32[]{:S(2)}, u32[]{:S(2)}) %collective-permute-start.4) | collective-permute-done | bytes 98336 | tf_op jit(solution)/shard_map/ppermute | solution.py:689
  26.7 1.4 %merge.1 = f32[8,24,256]{2,1,0:T(8,128)} custom-call(s32[2]{0:T(128)S(1)} %get-tuple-element.16.offsets, f32[8,24,256]{2,1,0:T(8,128)S(1)} %get-tuple-element.27.step, f32[8,24,128]{2,1,0:T(8,128)S(1)} %collective-permute-done.4.rest_0_, f32[8,24,128]{2,1,0:T(8,128)S(1)} %collective-permute-done.5.rest_1_, f32[8,24,128]{2,1,0:T(8,128)S(1)} %get-tuple-element.28.rest_2_, ...), custom_call_target="tpu_custom_call" | custom-call | flops 200000 | bytes 800000 | tf_op jit(solution)/shard_map/merge/pallas_call | solution.py:881
Async XLA Ops:
  0.6 6.6 %copy-start = (f32[8,72,384]{2,1,0:T(8,128)S(1)}, f32[8,72,384]{2,1,0:T(8,128)}, u32[]{:S(2)}) copy-start(f32[8,72,384]{2,1,0:T(8,128)} %source.8) | copy-start | bytes 2654212
  0.6 6.6 %copy-start.1 = (f32[8,72,384]{2,1,0:T(8,128)S(1)}, f32[8,72,384]{2,1,0:T(8,128)}, u32[]{:S(2)}) copy-start(f32[8,72,384]{2,1,0:T(8,128)} %nest.5) | copy-start | bytes 2654212
  0.7 6.6 %copy-start.2 = (f32[8,24,256]{2,1,0:T(8,128)S(1)}, f32[8,24,256]{2,1,0:T(8,128)}, u32[]{:S(2)}) copy-start(f32[8,24,256]{2,1,0:T(8,128)} %parent.5) | copy-start | bytes 589828
  0.7 6.6 %copy-start.3 = (f32[8,24,256]{2,1,0:T(8,128)S(1)}, f32[8,24,256]{2,1,0:T(8,128)}, u32[]{:S(2)}) copy-start(f32[8,24,256]{2,1,0:T(8,128)} %source.9) | copy-start | bytes 589828
  0.7 6.6 %copy-start.5 = (f32[2,8]{1,0:T(2,128)S(1)}, f32[2,8]{1,0:T(2,128)}, u32[]{:S(2)}) copy-start(f32[2,8]{1,0:T(2,128)} %parent_coefs.1) | copy-start | bytes 196
  2.9 7.3 %collective-permute-start = (f32[72,128]{1,0:T(8,128)}, f32[72,128]{1,0:T(8,128)S(1)}, u32[]{:S(2)}, u32[]{:S(2)}) collective-permute-start(f32[72,128]{1,0:T(8,128)} %pack_pair.1), channel_id=1, source_target_pairs={{0,2},{2,0},{1,3},{3,1},{4,6},{6,4},{5,7},{7,5},{8,10},{10,8},{9,1... | collective-permute-start | bytes 110600 | tf_op jit(solution)/shard_map/ppermute | solution.py:689
  6.5 0.7 %copy-start.4 = (f32[2,8]{1,0:T(2,128)S(1)}, f32[2,8]{1,0:T(2,128)}, u32[]{:S(2)}) copy-start(f32[2,8]{1,0:T(2,128)} %coefs.3) | copy-start | bytes 196
  10.3 6.5 %collective-permute-start.1 = (f32[56,384]{1,0:T(8,128)S(1)}, f32[56,384]{1,0:T(8,128)S(1)}, u32[]{:S(2)}, u32[]{:S(2)}) collective-permute-start(f32[56,384]{1,0:T(8,128)S(1)} %get-tuple-element.23), channel_id=1, source_target_pairs={{1,4},{4,1},{5,8},{8,5},{9,12},{12,9},{13,0},{0,13},{3,6},{6,3},{7... | collective-permute-start | bytes 258056 | tf_op jit(solution)/shard_map/ppermute | solution.py:900
  13.1 3.6 %collective-permute-start.2 = (f32[56,384]{1,0:T(8,128)S(1)}, f32[56,384]{1,0:T(8,128)S(1)}, u32[]{:S(2)}, u32[]{:S(2)}) collective-permute-start(f32[56,384]{1,0:T(8,128)S(1)} %get-tuple-element.24), channel_id=1, source_target_pairs={{0,1},{1,0},{4,5},{5,4},{8,9},{9,8},{12,13},{13,12},{2,3},{3,2},{6... | collective-permute-start | bytes 258056 | tf_op jit(solution)/shard_map/ppermute | solution.py:900
  13.1 3.6 %collective-permute-start.3 = (f32[8,128]{1,0:T(8,128)S(1)}, f32[8,128]{1,0:T(8,128)S(1)}, u32[]{:S(2)}, u32[]{:S(2)}) collective-permute-start(f32[8,128]{1,0:T(8,128)S(1)} %get-tuple-element.25), channel_id=1, source_target_pairs={{0,12},{1,13},{4,0},{5,1},{8,4},{9,5},{12,8},{13,9},{2,14},{3,15},... | collective-permute-start | bytes 12296 | tf_op jit(solution)/shard_map/ppermute | solution.py:689
  18.3 4.7 %collective-permute-start.6 = (f32[8,24,128]{2,1,0:T(8,128)S(1)}, f32[8,24,128]{2,1,0:T(8,128)S(1)}, u32[]{:S(2)}, u32[]{:S(2)}) collective-permute-start(f32[8,24,128]{2,1,0:T(8,128)S(1)} %get-tuple-element.28.rest_2_), channel_id=1, source_target_pairs={{0,2},{2,0},{1,3},{3,1},{4,6},{6,4},{5,7},{7,5},{8,10},{10,8},{9,1... | collective-permute-start | bytes 294920 | tf_op jit(solution)/shard_map/ppermute | solution.py:689
  18.9 6.7 %collective-permute-start.5 = (f32[8,24,128]{2,1,0:T(8,128)S(1)}, f32[8,24,128]{2,1,0:T(8,128)S(1)}, u32[]{:S(2)}, u32[]{:S(2)}) collective-permute-start(f32[8,24,128]{2,1,0:T(8,128)S(1)} %get-tuple-element.28.rest_2_), channel_id=1, source_target_pairs={{0,3},{1,6},{2,1},{3,4},{4,7},{5,10},{6,5},{7,8},{8,11},{9,14},{10... | collective-permute-start | bytes 294920 | tf_op jit(solution)/shard_map/ppermute | solution.py:913
  19.4 7.3 %collective-permute-start.4 = (f32[8,24,128]{2,1,0:T(8,128)S(1)}, f32[8,24,128]{2,1,0:T(8,128)S(1)}, u32[]{:S(2)}, u32[]{:S(2)}) collective-permute-start(f32[8,24,128]{2,1,0:T(8,128)S(1)} %get-tuple-element.28.rest_2_), channel_id=1, source_target_pairs={{0,1},{1,4},{4,5},{5,8},{8,9},{9,12},{12,13},{13,0},{2,3},{3,6},{6... | collective-permute-start | bytes 294920 | tf_op jit(solution)/shard_map/ppermute | solution.py:689

commit v5 on v4

--- a/solution.py
+++ b/solution.py
@@ -248,8 +248,7 @@
 
 def inner_first(
     band,
-    ox_hbm,
-    oy_hbm,
+    oy_ref,
     parent_coefs,
     coefs,
     nest,
@@ -260,27 +259,12 @@
     first,
     packs,
     spread,
-    rows_out,
-    offsets_out,
-    ox_ref,
-    oy_ref,
-    sems,
+    oy_rows,
 ):
     levels, rows, cols = nest.shape
-    loads = [
-        pltpu.make_async_copy(ref, to, sems.at[at])
-        for at, (ref, to) in enumerate(((ox_hbm, ox_ref), (oy_hbm, oy_ref)))
-    ]
-    for copy in loads:
-        copy.start()
+    oy = oy_ref[0]
+    oy_rows[...] = jnp.full(oy_rows.shape, oy, jnp.int32)
     spread_coefs(parent_coefs, coefs, spread)
-    for copy in loads:
-        copy.wait()
-    ox, oy = ox_ref[0], oy_ref[0]
-    rows_out[0] = jnp.full(rows_out.shape[1:], ox, jnp.int32)
-    rows_out[1] = jnp.full(rows_out.shape[1:], oy, jnp.int32)
-    offsets_out[0] = ox
-    offsets_out[1] = oy
     strip[...] = edge_strip(lax.axis_index("gy"), band, oy, parent, parent_source)
     lane = iota((rows, LANES), 1)
     for at, ref in enumerate((nest, source)):
@@ -314,7 +298,7 @@
 
 
 def pack_rows(
-    parts, old_top, old_end, src_top, src_end, par_top, par_end, own_strip, offset_rows, *rest
+    parts, old_top, old_end, src_top, src_end, par_top, par_end, own_strip, oy_rows, *rest
 ):
     columns = rest[: parts - 1]
     across, within, far, strip_out, both = rest[parts - 1 :]
@@ -328,12 +312,15 @@
     lane = iota((strip_rows, LANES), 1)
     strips = own_strip[...]
     if parts == 2:
-        oy = jnp.concatenate([offset_rows[1]] * (strip_rows // 8), axis=0)
+        oy = jnp.concatenate([oy_rows[...]] * (strip_rows // 8), axis=0)
         strips = strips + across_border(left[:strip_rows, :], oy, par_top.shape[2], me)
     else:
         for message in columns:
             strips = strips + message[:strip_rows, :]
-        strips = jnp.where((lane & (STRIDE - 1)) >= STRIP_AT, strips, 0.0)
+    c = lane & (STRIDE - 1)
+    strips = jnp.where(c >= STRIP_AT, strips, 0.0)
+    strips = jnp.where(c == PARENT_AT, left[:strip_rows, :], strips)
+    strips = jnp.where(c == PARENT_AT + 1, turned(right[:strip_rows, :], 1), strips)
     strip_out[...] = strips
     far[...] = strips[:8]
     pieces = cols // LANES
@@ -372,7 +359,7 @@
 def edges(
     parts,
     parent_cols,
-    offset_rows,
+    ox_ref,
     spread,
     nest,
     source,
@@ -381,11 +368,12 @@
     strips,
     across,
     within,
-    beyond,
+    far,
     y_left,
     y_right,
     result,
     coarse_out,
+    far_out,
     both,
     ping,
     pong,
@@ -403,6 +391,7 @@
     is_south = me == 0
     is_north = me == parts - 1
 
+    far_out[...] = far[...]
     sub = iota((8, LANES), 0)
     old = jnp.concatenate(
         [
@@ -411,13 +400,9 @@
             after[TAIL_ROW + 8 : TAIL_ROW + 16, :LANES],
             after[TAIL_ROW + 8 : TAIL_ROW + 16, LANES : 2 * LANES],
             jnp.where(
-                sub == 0,
-                beyond[...],
-                jnp.where(
-                    sub == 7,
-                    before[TAIL_ROW : TAIL_ROW + 8, parent_cols : parent_cols + LANES],
-                    0.0,
-                ),
+                sub == 7,
+                before[TAIL_ROW : TAIL_ROW + 8, parent_cols : parent_cols + LANES],
+                0.0,
             ),
         ],
         axis=0,
@@ -447,7 +432,7 @@
     )
     index = iota((rows + 16, count), 0)
     nest_row = jnp.where(index < rows, index, jnp.where(index < rows + 8, index - rows - 3, index - 13))
-    parent_row = ((nest_row + 3) * 171 >> 9) - 1 + offset_rows[0, 0:1, :count]
+    parent_row = ((nest_row + 3) * 171 >> 9) - 1 + ox_ref[0]
     pick = (iota((rows + 16, count), 1) == parent_row).astype(jnp.float32)
     picked = jnp.dot(
         pick,
@@ -603,15 +588,37 @@
 
 
 def parent_step(
-    parts, spread, nest, parent, source, within, across, y_left, y_right, out, nest_out, tail, sem
+    parts,
+    band,
+    ox_ref,
+    oy_ref,
+    spread,
+    nest,
+    parent,
+    source,
+    within,
+    across,
+    beyond,
+    y_left,
+    y_right,
+    out,
+    nest_out,
+    late,
+    tail,
+    corner,
+    sem,
 ):
     store = pltpu.make_async_copy(nest, nest_out, sem)
     store.start()
     core = lax.axis_index("gz")
     levels, rows, cols = parent.shape
-    tail[0] = within[TAIL_ROW : TAIL_ROW + levels, :cols]
-    tail[1] = across[TAIL_ROW : TAIL_ROW + levels, :cols]
+    tail[0] = within[TAIL_ROW : TAIL_ROW + levels, : cols + LANES]
+    tail[1] = across[TAIL_ROW : TAIL_ROW + levels, : cols + LANES]
     me = lax.axis_index("gy")
+    is_last = ox_ref[0] == rows - 1
+    wide = iota((1, cols), 1)
+    south = (wide == oy_ref[0] + 2 - me * cols) & is_last
+    north = (wide == oy_ref[0] + band - 3 - me * cols) & is_last
     row = iota((rows, cols), 0)
     lane = iota((rows, cols), 1)
     has_left = me > 0
@@ -624,8 +631,8 @@
         at = STRIDE * level + PARENT_AT
         from_left = left[:, at : at + 1]
         from_right = right[:, at : at + 1]
-        top = tail[1 - core, level : level + 1, :]
-        end = tail[core, level : level + 1, :]
+        top = tail[1 - core, level : level + 1, :cols]
+        end = tail[core, level : level + 1, :cols]
         around = (
             jnp.where(row == 0, top, pltpu.roll(now, 1, 0))
             + jnp.where(row == rows - 1, end, pltpu.roll(now, rows - 1, 0))
@@ -648,10 +655,44 @@
         out[level] = (
             (1.0 - 4.0 * ch - 2.0 * cv) * now + ch * around + (cv * stacked + source[level])
         )
+        at = cols + STRIDE * level + PARENT_AT
+        before_end = jnp.where(
+            wide == 0, tail[core, 0:1, at : at + 1], pltpu.roll(end, 1, 1)
+        )
+        after_end = jnp.where(
+            wide == cols - 1, tail[core, 0:1, at + 1 : at + 2], pltpu.roll(end, cols - 1, 1)
+        )
+        nest_ch = spread[1, 2, level : level + 1, :]
+        nest_ch = jnp.concatenate([nest_ch] * (cols // LANES), axis=1)
+        share = nest_ch * nest_ch * ch * (1.0 / SUBSTEPS)
+        late[level : level + 1, :] = (share * (1.0 / (RATIO * RATIO))) * (
+            jnp.where(south, before_end, 0.0) + jnp.where(north, after_end, 0.0)
+        )
     store.wait()
 
-
-def merge(parts, band, offsets, step, *rest):
+    @pl.when(is_last & ((me == 0) | (me == parts - 1)))
+    def _():
+        nest_rows, nest_cols = nest.shape[1:]
+        first = pl.multiple_of(jnp.where(me == 0, 0, nest_cols - LANES), LANES)
+        place = (slice(None), pl.ds(nest_rows - 8, 8), pl.ds(first, LANES))
+        load = pltpu.make_async_copy(nest.at[place], corner, sem)
+        load.start()
+        load.wait()
+        sub = iota((8, LANES), 0)
+        lane = iota((8, LANES), 1)
+        cell = (sub == 7) & (lane == jnp.where(me == 0, RIM, LANES - RIM - 1))
+        for level in range(levels):
+            at = STRIDE * level + STRIP_AT
+            value = jnp.where(me == 0, beyond[0:1, at + 2 : at + 3], beyond[0:1, at + 1 : at + 2])
+            nest_ch = spread[1, 2, level : level + 1, :]
+            share = nest_ch * nest_ch * spread[1, 0, level : level + 1, :] * (1.0 / SUBSTEPS)
+            corner[level] += jnp.where(cell, share * value, 0.0)
+        again = pltpu.make_async_copy(corner, nest_out.at[place], sem)
+        again.start()
+        again.wait()
+
+
+def merge(parts, band, ox_ref, oy_ref, late, step, *rest):
     previous, own, out, joined = (
         rest[:parts],
         rest[parts : 2 * parts],
@@ -661,12 +702,13 @@
     levels, rows, cols = step.shape
     foot = own[0].shape[2]
     me = lax.axis_index("gy")
-    ox = offsets[0]
-    oy = offsets[1]
+    ox = ox_ref[0]
+    oy = oy_ref[0]
     for k in range(parts):
         joined[k, :, :rows, :] = previous[k][...]
         joined[k, :, rows:, :] = own[k][...]
     lane = iota((rows, LANES), 1)
+    row = iota((rows, LANES), 0)
     for level in range(levels):
         values = [tile(step, level, piece) for piece in range(cols // LANES)]
         for k in range(parts):
@@ -680,6 +722,8 @@
                 at = lane + (piece * LANES + me * cols - oy)
                 values[piece] = jnp.where((at >= low) & (at < high), block, values[piece])
         for piece, value in enumerate(values):
+            term = late[level : level + 1, piece * LANES : (piece + 1) * LANES]
+            value = value + jnp.where(row == rows - 2, term, 0.0)
             out[level, :, piece * LANES : (piece + 1) * LANES] = value
 
 
@@ -745,28 +789,21 @@
             name="pack_columns",
         )(offset_y, nest_old, nest_source, parent_old, parent_source)
     columns = [shifted(packed[k - 1], "gy", k) for k in range(1, parts)]
-    own_strip, first, packs, spread, offset_rows, offsets = pl.pallas_call(
+    own_strip, first, packs, spread, oy_rows = pl.pallas_call(
         functools.partial(inner_first, band),
         out_shape=[
             shape((parent_rows, LANES), f32),
             shape(nest_old.shape, f32),
             shape((4, rows, LANES), f32),
             shape((2, 4, levels, LANES), f32),
-            shape((2, 8, LANES), jnp.int32),
-            shape((2,), jnp.int32),
+            shape((8, LANES), jnp.int32),
         ],
-        in_specs=[in_hbm] * 2 + [scalars()] * 2 + [whole()] * 4,
-        out_specs=[whole()] * 5 + [scalars()],
-        scratch_shapes=[
-            pltpu.SMEM(offset_x.shape, jnp.int32),
-            pltpu.SMEM(offset_y.shape, jnp.int32),
-            pltpu.SemaphoreType.DMA((2,)),
-        ],
+        in_specs=[scalars()] * 3 + [whole()] * 4,
+        out_specs=[whole()] * 5,
         compiler_params=params(),
         cost_estimate=cost(4000000, 3000000),
         name="inner_first",
     )(
-        offset_x,
         offset_y,
         parent_coefs,
         nest_coefs,
@@ -801,7 +838,7 @@
             block(parent_old, False),
             block(parent_old, True),
             full(own_strip.shape),
-            full(offset_rows.shape),
+            full(oy_rows.shape),
         ]
         + [full(message.shape) for message in columns],
         out_specs=[full(out.shape) for out in outs],
@@ -809,10 +846,9 @@
         compiler_params=params(),
         cost_estimate=cost(100000, 700000),
         name="pack_rows",
-    )(nest_old, nest_old, nest_source, nest_source, parent_old, parent_old, own_strip, offset_rows, *columns)
+    )(nest_old, nest_old, nest_source, nest_source, parent_old, parent_old, own_strip, oy_rows, *columns)
     across = swapped(across, 1)
     within = swapped(within, 0)
-    beyond = shifted(far, along, -2)
     third = pl.pallas_call(
         inner_rest,
         out_shape=shape(nest_old.shape, f32),
@@ -823,14 +859,15 @@
         cost_estimate=cost(8000000, 6000000),
         name="inner_rest",
     )(nest_coefs, first, nest_source, strips)
-    nest_done, coarse = pl.pallas_call(
+    nest_done, coarse, far = pl.pallas_call(
         functools.partial(edges, parts, parent_cols),
         out_shape=[
             shape(nest_old.shape, f32),
             shape((levels, parent_rows, foot), f32),
+            shape((8, LANES), f32),
         ],
-        in_specs=[whole()] * 12,
-        out_specs=[whole(), whole()],
+        in_specs=[scalars()] + [whole()] * 11,
+        out_specs=[whole()] * 3,
         scratch_shapes=[
             VMEM((2, height, width), f32),
             VMEM((levels, 2, 8, width), f32),
@@ -842,7 +879,7 @@
         cost_estimate=cost(4000000, 3000000),
         name="edges",
     )(
-        offset_rows,
+        offset_x,
         spread,
         nest_old,
         nest_source,
@@ -851,7 +888,7 @@
         strips,
         across,
         within,
-        beyond,
+        far,
         columns[0],
         columns[-1],
     )
@@ -859,35 +896,47 @@
         shifted_both(coarse, k) for k in range(1, parts)
     ]
     own = [coarse] + [shifted(coarse, "gy", k) for k in range(1, parts)]
-    step, nest_new = pl.pallas_call(
-        functools.partial(parent_step, parts),
-        out_shape=[shape(parent_old.shape, f32), shape(nest_old.shape, f32)],
-        in_specs=[whole(), anywhere] + [whole()] * 6,
-        out_specs=[whole(), in_hbm],
-        scratch_shapes=[VMEM((2, levels, parent_cols), f32), pltpu.SemaphoreType.DMA],
+    beyond = shifted(far, along, -2)
+    step, nest_new, late = pl.pallas_call(
+        functools.partial(parent_step, parts, band),
+        out_shape=[
+            shape(parent_old.shape, f32),
+            shape(nest_old.shape, f32),
+            shape((levels, parent_cols), f32),
+        ],
+        in_specs=[scalars()] * 2 + [whole(), anywhere] + [whole()] * 7,
+        out_specs=[whole(), in_hbm, whole()],
+        scratch_shapes=[
+            VMEM((2, levels, parent_cols + LANES), f32),
+            VMEM((levels, 8, LANES), f32),
+            pltpu.SemaphoreType.DMA,
+        ],
         compiler_params=params(),
         cost_estimate=cost(800000, 2500000),
         name="parent_step",
     )(
+        offset_x,
+        offset_y,
         spread,
         nest_done,
         parent_old,
         parent_source,
         within,
         across,
+        beyond,
         columns[0],
         columns[-1],
     )
     parent_new = pl.pallas_call(
         functools.partial(merge, parts, band),
         out_shape=shape(parent_old.shape, f32),
-        in_specs=[scalars()] + [whole()] * (1 + 2 * parts),
+        in_specs=[scalars()] * 2 + [whole()] * (2 + 2 * parts),
         out_specs=whole(),
         scratch_shapes=[VMEM((parts, levels, 2 * parent_rows, foot), f32)],
         compiler_params=params(),
         cost_estimate=cost(200000, 800000),
         name="merge",
-    )(offsets, step, *previous, *own)
+    )(offset_x, offset_y, late, step, *previous, *own)
     return (parent_new, nest_new)
 
 

time: 28.3 us -> 26 us (0.919)
  waiting for transfers between devices: 5.41 us -> 2.76 us
  starting transfers between devices: 9.24 us -> 11.3 us
  Pallas kernels: 11.3 us -> 9.63 us
    ppermute x4, starting transfers between devices: 5.87 us -> 8.47 us  [shifted(): return lax.ppermute(value, axis, pairs)]
    ppermute x1, waiting for transfers between devices: 2.64 us -> 0.78 us  [shifted_both(): return lax.ppermute(value, ('gx', 'gy', 'gz'), pairs)]
    ppermute x4, waiting for transfers between devices: 2.77 us -> 1.34 us  [shifted(): return lax.ppermute(value, axis, pairs)]
    pallas_call x1, Pallas kernels: 2.88 us -> 1.82 us  [shards(): pl.pallas_call(functools.partial(inner_first, band), out_shape=[shape((pa...]
    ppermute x2, waiting for transfers between devices: 0.01 us -> 0.65 us  [swapped(): return lax.ppermute(value, along, pairs)]
    pallas_call x1, Pallas kernels: 1.36 us -> 0.83 us  [shards(): pl.pallas_call(functools.partial(merge, parts, band), out_shape=shape(par...]
    ppermute x1, starting transfers between devices: 0.54 us -> 0.01 us  [shifted_both(): return lax.ppermute(value, ('gx', 'gy', 'gz'), pairs)]
  transfers between devices with their start and end apart: 7 -> 7, of which waited for: 4 -> 3; matrix products, arithmetic and copies ran while one was open for 0% -> 0% of each run, Pallas kernels for 22% -> 19%
where the time goes in v5:
time: 26 us; the launch traced here: 25.8 us
  starting transfers between devices  11.3 us (43%)
  Pallas kernels  9.63 us (37%)
  waiting for transfers between devices  2.76 us (11%)
  between operations  2.09 us (8%)
    ppermute x4, starting transfers between devices, shifted(): return lax.ppermute(value, axis, pairs)  8.47 us
    ppermute x2, starting transfers between devices, swapped(): return lax.ppermute(value, along, pairs)  2.83 us
    pallas_call x1, Pallas kernels, shards(): pl.pallas_call(pack_pair, out_shape=shape((rows, LANES), f32), in_specs=[...  2.18 us
    pallas_call x1, Pallas kernels, shards(): pl.pallas_call(inner_rest, out_shape=shape(nest_old.shape, f32), in_specs...  2.15 us
    pallas_call x1, Pallas kernels, shards(): pl.pallas_call(functools.partial(inner_first, band), out_shape=[shape((pa...  1.82 us
    pallas_call x1, Pallas kernels, shards(): pl.pallas_call(functools.partial(edges, parts, parent_cols), out_shape=[s...  1.5 us
    ppermute x4, waiting for transfers between devices, shifted(): return lax.ppermute(value, axis, pairs)  1.34 us
    pallas_call x1, Pallas kernels, shards(): pl.pallas_call(functools.partial(parent_step, parts, band), out_shape=[sh...  1.02 us
  transfers between devices with their start and end apart: 7, of which 3 were waited for; matrix products, arithmetic and copies ran while one was open for 0% of the time, Pallas kernels for 19%

profile of v5, /device:TPU:0, one launch (start us, length us, event | category | flops | bytes accessed | tf_op | source)
XLA Modules:
  0.0 25.8 jit_solution(15794959838086353848)
XLA Ops:
  0.6 0.0 copy-start
  0.6 0.0 copy-start.1
  0.7 0.0 copy-start.2
  0.7 0.0 copy-start.3
  0.7 0.0 copy-start.5
  0.7 2.2 %pack_pair.1 = f32[72,128]{1,0:T(8,128)} custom-call(f32[8,72,384]{2,1,0:T(8,128)} %nest.5, f32[8,72,384]{2,1,0:T(8,128)} %source.8, f32[8,24,256]{2,1,0:T(8,128)} %parent.5, f32[8,24,256]{2,1,0:T(8,128)} %source.9), custom_call_target="tpu_custom_call" | custom-call | flops 200000 | bytes 800000 | tf_op jit(solution)/shard_map/pack_pair/pallas_call | solution.py:754
  2.9 0.0 copy-start.4
  2.9 3.0 %collective-permute-start = (f32[72,128]{1,0:T(8,128)}, f32[72,128]{1,0:T(8,128)S(1)}, u32[]{:S(2)}, u32[]{:S(2)}) collective-permute-start(f32[72,128]{1,0:T(8,128)} %pack_pair.1), channel_id=1, source_target_pairs={{0,2},{2,0},{1,3},{3,1},{4,6},{6,4},{5,7},{7,5},{8,10},{10,8},{9,1... | collective-permute-start | bytes 110600 | tf_op jit(solution)/shard_map/ppermute | solution.py:733
  6.5 0.0 copy-done
  6.5 0.0 copy-done.1
  6.6 0.0 copy-done.2
  6.6 0.0 copy-done.3
  6.6 0.0 copy-done.5
  6.6 0.0 copy-done.4
  6.6 1.8 %inner_first.1 = (f32[24,128]{1,0:T(8,128)S(1)}, f32[8,72,384]{2,1,0:T(8,128)S(1)}, f32[4,72,128]{2,1,0:T(8,128)S(1)}, f32[2,4,8,128]{3,2,1,0:T(8,128)S(1)}, s32[8,128]{1,0:T(8,128)S(1)}) custom-call(s32[1]{0:T(128)S(6)} %copy.11.oy_ref, f32[2,8]{1,0:T(2,128)S(1)} %copy-done.5, f32[2,8]{1,0:T(2,128)S(1)} %copy-done.4, f32[8,72,384]{2,1,0:T(8,128)S(1)} %copy-done.1, ...), custom_call_target="tpu_custom_call" | custom-call | flops 4000000 | bytes 3000000 | tf_op jit(solution)/shard_map/inner_first/pallas_call | solution.py:792
  8.4 0.0 collective-permute-done.rest_0_.y_left.y_right
  8.4 0.1 pack_rows.1
  8.6 2.8 %collective-permute-start.1 = (f32[56,384]{1,0:T(8,128)S(1)}, f32[56,384]{1,0:T(8,128)S(1)}, u32[]{:S(2)}, u32[]{:S(2)}) collective-permute-start(f32[56,384]{1,0:T(8,128)S(1)} %get-tuple-element.23), channel_id=1, source_target_pairs={{1,4},{4,1},{5,8},{8,5},{9,12},{12,9},{13,0},{0,13},{3,6},{6,3},{7... | collective-permute-start | bytes 258056 | tf_op jit(solution)/shard_map/ppermute | solution.py:949
  11.4 0.0 collective-permute-start.2
  12.1 2.1 %inner_rest.1.third = f32[8,72,384]{2,1,0:T(8,128)S(1)} custom-call(f32[2,8]{1,0:T(2,128)S(1)} %copy-done.4, f32[8,72,384]{2,1,0:T(8,128)S(1)} %get-tuple-element.18.first, f32[8,72,384]{2,1,0:T(8,128)S(1)} %copy-done, f32[24,128]{1,0:T(8,128)S(1)} %get-tuple-element.21.after_pack.strips), custom_call_target="tpu_custom_call" | custom-call | flops 8000000 | bytes 6000000 | tf_op jit(solution)/shard_map/inner_rest/pallas_call | solution.py:852
  14.2 0.6 %collective-permute-done.1.across = f32[56,384]{1,0:T(8,128)S(1)} collective-permute-done((f32[56,384]{1,0:T(8,128)S(1)}, f32[56,384]{1,0:T(8,128)S(1)}, u32[]{:S(2)}, u32[]{:S(2)}) %collective-permute-start.1) | collective-permute-done | bytes 86048 | tf_op jit(solution)/shard_map/ppermute | solution.py:949
  14.9 0.0 collective-permute-done.2.within
  14.9 1.5 %edges.1 = (f32[8,72,384]{2,1,0:T(8,128)S(1)}, f32[8,24,128]{2,1,0:T(8,128)S(1)}, f32[8,128]{1,0:T(8,128)S(1)}) custom-call(s32[1]{0:T(128)S(6)} %copy.10.ox_ref, f32[2,4,8,128]{3,2,1,0:T(8,128)S(1)} %get-tuple-element.17.spread, f32[8,72,384]{2,1,0:T(8,128)S(1)} %copy-done.1, f32[8,72,384]{2,1,0:T(8,128)S(1)} %copy-done, ...), custom_call_target="tpu_custom_call" | custom-call | flops 4000000 | bytes 3000000 | tf_op jit(solution)/shard_map/edges/pallas_call | solution.py:862
  16.4 1.8 %collective-permute-start.6 = (f32[8,24,128]{2,1,0:T(8,128)S(1)}, f32[8,24,128]{2,1,0:T(8,128)S(1)}, u32[]{:S(2)}, u32[]{:S(2)}) collective-permute-start(f32[8,24,128]{2,1,0:T(8,128)S(1)} %get-tuple-element.30.rest_2_), channel_id=1, source_target_pairs={{0,2},{2,0},{1,3},{3,1},{4,6},{6,4},{5,7},{7,5},{8,10},{10,8},{9,1... | collective-permute-start | bytes 294920 | tf_op jit(solution)/shard_map/ppermute | solution.py:733
  18.2 0.0 collective-permute-start.5
  18.2 0.0 collective-permute-start.4
  18.2 3.6 %collective-permute-start.3 = (f32[8,128]{1,0:T(8,128)S(1)}, f32[8,128]{1,0:T(8,128)S(1)}, u32[]{:S(2)}, u32[]{:S(2)}) collective-permute-start(f32[8,128]{1,0:T(8,128)S(1)} %get-tuple-element.27), channel_id=1, source_target_pairs={{0,12},{1,13},{4,0},{5,1},{8,4},{9,5},{12,8},{13,9},{2,14},{3,15},... | collective-permute-start | bytes 12296 | tf_op jit(solution)/shard_map/ppermute | solution.py:733
  21.8 1.3 %collective-permute-done.3.beyond = f32[8,128]{1,0:T(8,128)S(1)} collective-permute-done((f32[8,128]{1,0:T(8,128)S(1)}, f32[8,128]{1,0:T(8,128)S(1)}, u32[]{:S(2)}, u32[]{:S(2)}) %collective-permute-start.3) | collective-permute-done | bytes 4128 | tf_op jit(solution)/shard_map/ppermute | solution.py:733
  23.2 1.0 %parent_step.1 = (f32[8,24,256]{2,1,0:T(8,128)S(1)}, f32[8,72,384]{2,1,0:T(8,128)}, f32[8,256]{1,0:T(8,128)S(1)}) custom-call(s32[1]{0:T(128)S(6)} %copy.10.ox_ref, s32[1]{0:T(128)S(6)} %copy.11.oy_ref, f32[2,4,8,128]{3,2,1,0:T(8,128)S(1)} %get-tuple-element.17.spread, f32[8,72,384]{2,1,0:T(8,128)S(1)} %get-tuple-element.26.nest, ...), custom_call_target="tpu_custom_call" | custom-call | flops 800000 | bytes 2500000 | tf_op jit(solution)/shard_map/parent_step/pallas_call | solution.py:900
  24.2 0.0 collective-permute-done.6.rest_3_
  24.2 0.8 %collective-permute-done.5.rest_1_ = f32[8,24,128]{2,1,0:T(8,128)S(1)} collective-permute-done((f32[8,24,128]{2,1,0:T(8,128)S(1)}, f32[8,24,128]{2,1,0:T(8,128)S(1)}, u32[]{:S(2)}, u32[]{:S(2)}) %collective-permute-start.5) | collective-permute-done | bytes 98336 | tf_op jit(solution)/shard_map/ppermute | solution.py:962
  25.0 0.0 collective-permute-done.4.rest_0_
  25.0 0.8 %merge.1 = f32[8,24,256]{2,1,0:T(8,128)} custom-call(s32[1]{0:T(128)S(6)} %copy.10.ox_ref, s32[1]{0:T(128)S(6)} %copy.11.oy_ref, f32[8,256]{1,0:T(8,128)S(1)} %get-tuple-element.28.late, f32[8,24,256]{2,1,0:T(8,128)S(1)} %get-tuple-element.29.step, f32[8,24,128]{2,1,0:T(8,128)S(1)} %collective-permute-done.4.rest_0_, ...), custom_call_target="tpu_custom_call" | custom-call | flops 200000 | bytes 800000 | tf_op jit(solution)/shard_map/merge/pallas_call | solution.py:930
Async XLA Ops:
  0.6 5.9 %copy-start = (f32[8,72,384]{2,1,0:T(8,128)S(1)}, f32[8,72,384]{2,1,0:T(8,128)}, u32[]{:S(2)}) copy-start(f32[8,72,384]{2,1,0:T(8,128)} %source.8) | copy-start | bytes 2654212
  0.6 5.9 %copy-start.1 = (f32[8,72,384]{2,1,0:T(8,128)S(1)}, f32[8,72,384]{2,1,0:T(8,128)}, u32[]{:S(2)}) copy-start(f32[8,72,384]{2,1,0:T(8,128)} %nest.5) | copy-start | bytes 2654212
  0.7 5.9 %copy-start.2 = (f32[8,24,256]{2,1,0:T(8,128)S(1)}, f32[8,24,256]{2,1,0:T(8,128)}, u32[]{:S(2)}) copy-start(f32[8,24,256]{2,1,0:T(8,128)} %parent.5) | copy-start | bytes 589828
  0.7 5.9 %copy-start.3 = (f32[8,24,256]{2,1,0:T(8,128)S(1)}, f32[8,24,256]{2,1,0:T(8,128)}, u32[]{:S(2)}) copy-start(f32[8,24,256]{2,1,0:T(8,128)} %source.9) | copy-start | bytes 589828
  0.7 5.9 %copy-start.5 = (f32[2,8]{1,0:T(2,128)S(1)}, f32[2,8]{1,0:T(2,128)}, u32[]{:S(2)}) copy-start(f32[2,8]{1,0:T(2,128)} %parent_coefs.1) | copy-start | bytes 196
  2.9 3.7 %copy-start.4 = (f32[2,8]{1,0:T(2,128)S(1)}, f32[2,8]{1,0:T(2,128)}, u32[]{:S(2)}) copy-start(f32[2,8]{1,0:T(2,128)} %coefs.3) | copy-start | bytes 196
  2.9 5.5 %collective-permute-start = (f32[72,128]{1,0:T(8,128)}, f32[72,128]{1,0:T(8,128)S(1)}, u32[]{:S(2)}, u32[]{:S(2)}) collective-permute-start(f32[72,128]{1,0:T(8,128)} %pack_pair.1), channel_id=1, source_target_pairs={{0,2},{2,0},{1,3},{3,1},{4,6},{6,4},{5,7},{7,5},{8,10},{10,8},{9,1... | collective-permute-start | bytes 110600 | tf_op jit(solution)/shard_map/ppermute | solution.py:733
  8.6 6.3 %collective-permute-start.1 = (f32[56,384]{1,0:T(8,128)S(1)}, f32[56,384]{1,0:T(8,128)S(1)}, u32[]{:S(2)}, u32[]{:S(2)}) collective-permute-start(f32[56,384]{1,0:T(8,128)S(1)} %get-tuple-element.23), channel_id=1, source_target_pairs={{1,4},{4,1},{5,8},{8,5},{9,12},{12,9},{13,0},{0,13},{3,6},{6,3},{7... | collective-permute-start | bytes 258056 | tf_op jit(solution)/shard_map/ppermute | solution.py:949
  11.4 3.5 %collective-permute-start.2 = (f32[56,384]{1,0:T(8,128)S(1)}, f32[56,384]{1,0:T(8,128)S(1)}, u32[]{:S(2)}, u32[]{:S(2)}) collective-permute-start(f32[56,384]{1,0:T(8,128)S(1)} %get-tuple-element.24), channel_id=1, source_target_pairs={{0,1},{1,0},{4,5},{5,4},{8,9},{9,8},{12,13},{13,12},{2,3},{3,2},{6... | collective-permute-start | bytes 258056 | tf_op jit(solution)/shard_map/ppermute | solution.py:949
  16.4 7.8 %collective-permute-start.6 = (f32[8,24,128]{2,1,0:T(8,128)S(1)}, f32[8,24,128]{2,1,0:T(8,128)S(1)}, u32[]{:S(2)}, u32[]{:S(2)}) collective-permute-start(f32[8,24,128]{2,1,0:T(8,128)S(1)} %get-tuple-element.30.rest_2_), channel_id=1, source_target_pairs={{0,2},{2,0},{1,3},{3,1},{4,6},{6,4},{5,7},{7,5},{8,10},{10,8},{9,1... | collective-permute-start | bytes 294920 | tf_op jit(solution)/shard_map/ppermute | solution.py:733
  18.2 6.8 %collective-permute-start.5 = (f32[8,24,128]{2,1,0:T(8,128)S(1)}, f32[8,24,128]{2,1,0:T(8,128)S(1)}, u32[]{:S(2)}, u32[]{:S(2)}) collective-permute-start(f32[8,24,128]{2,1,0:T(8,128)S(1)} %get-tuple-element.30.rest_2_), channel_id=1, source_target_pairs={{0,3},{1,6},{2,1},{3,4},{4,7},{5,10},{6,5},{7,8},{8,11},{9,14},{10... | collective-permute-start | bytes 294920 | tf_op jit(solution)/shard_map/ppermute | solution.py:962
  18.2 6.8 %collective-permute-start.4 = (f32[8,24,128]{2,1,0:T(8,128)S(1)}, f32[8,24,128]{2,1,0:T(8,128)S(1)}, u32[]{:S(2)}, u32[]{:S(2)}) collective-permute-start(f32[8,24,128]{2,1,0:T(8,128)S(1)} %get-tuple-element.30.rest_2_), channel_id=1, source_target_pairs={{0,1},{1,4},{4,5},{5,8},{8,9},{9,12},{12,13},{13,0},{2,3},{3,6},{6... | collective-permute-start | bytes 294920 | tf_op jit(solution)/shard_map/ppermute | solution.py:733
  18.2 5.0 %collective-permute-start.3 = (f32[8,128]{1,0:T(8,128)S(1)}, f32[8,128]{1,0:T(8,128)S(1)}, u32[]{:S(2)}, u32[]{:S(2)}) collective-permute-start(f32[8,128]{1,0:T(8,128)S(1)} %get-tuple-element.27), channel_id=1, source_target_pairs={{0,12},{1,13},{4,0},{5,1},{8,4},{9,5},{12,8},{13,9},{2,14},{3,15},... | collective-permute-start | bytes 12296 | tf_op jit(solution)/shard_map/ppermute | solution.py:733
